TPU v7x, 32 devices: a whole 2x2x4 slice. The times are simulated.
32 devices in a mesh: section: 4 (over x, core), dp: 4 (over z), chan: 2 (over y).
Axes of the slice: x: 2, y: 2, z: 4, core: 2. Of those that a mesh axis runs over, the one named last changes fastest.
Arguments:
- feats: bfloat16 [8, 32, 128, 2048], P('dp', None, None, 'chan'), may hold values from -6 to 6
- offsets: int32 [8], P('dp'), may hold values from 0 to 127
- widths: int32 [8], P('dp'), may hold values from 32 to 64
- labels: int32 [8, 32, 128], P('dp'), may hold values from 0 to 19
- dw_kernel: bfloat16 [4, 9, 2048], P('section', None, 'chan'), may hold values from -2 to 2
- pw_weight: bfloat16 [4, 2048, 256], P('section', 'chan'), may hold values from -0.125 to 0.125
- pw_bias: float32 [4, 256], P('section', 'chan'), may hold values from -3 to 3
- proj: bfloat16 [4, 256, 256], P('section', 'chan'), may hold values from -0.1875 to 0.1875
- proj_bias: float32 [256], P('chan'), may hold values from -3 to 3
- upstream: bfloat16 [256, 8, 32, 128], P('chan', 'dp'), may hold values from -6 to 6
Outputs:
- aspp_out: bfloat16 [256, 8, 32, 128], P('chan', 'dp')
- input_grad: bfloat16 [8, 32, 128, 2048], P('dp', 'section', None, 'chan')
- grad_dw: float32 [4, 9, 2048], P('section', None, 'chan')
- grad_pw: float32 [4, 2048, 256], P('section', 'chan')
- grad_pw_bias: float32 [4, 256], P('section', 'chan')
- grad_proj: float32 [4, 256, 256], P('section', 'chan')
- grad_proj_bias: float32 [256], P('chan')
All inputs are finite; a program needn't handle non-finite values.
Results may differ from a plain program's by a relative error of at most 0.008.
Values may be sent and summed in bfloat16 or wider, within the bound.
A program may use at most 192 MiB of HBM per device.

v0:
```python
import math

import jax
import jax.numpy as jnp
from jax import lax
from jax.sharding import PartitionSpec as P

RATE = 6


void_class = 19


def prefix(shard, axis, combine, identity):
    devices, place = (lax.axis_size(axis), lax.axis_index(axis))
    everything = lax.all_gather(shard, axis)
    start = jnp.broadcast_to(jnp.asarray(identity, shard.dtype), shard.shape)

    def step(k, before):
        reached = k < place
        new = combine(before, everything[k])
        return jnp.where(reached, new, before)

    return lax.fori_loop(0, devices, step, start)


def spread(value, axis, source):
    kept = jnp.where(lax.axis_index(axis) == source, value, 0).astype(value.dtype)
    return lax.psum(kept, axis)


def column_band(offsets, widths, col_count):
    columns = jnp.arange(col_count, dtype=jnp.int32)
    return jnp.mod(columns[None, :] - offsets[:, None], col_count) < widths[:, None]


def swish_slope(value):
    sig = jax.nn.sigmoid(value)
    return sig * (1.0 + value * (1.0 - sig))


def add_terms(earlier, latter):
    return earlier + latter


def local(feats, offsets, widths, labels, dw_kernel, pw_weight, pw_bias, proj, proj_bias, upstream):
    frame_count, row_count, col_count, chan_count = feats.shape
    segments = lax.axis_size("section")
    dilation = RATE * lax.axis_index("section")
    margin = RATE * (segments - 1)
    keep = column_band(offsets, widths, col_count)
    masked = feats * keep[:, None, :, None].astype(jnp.bfloat16)
    padded = jnp.pad(masked, ((0, 0), (margin, margin), (margin, margin), (0, 0)))
    kernel = dw_kernel[0].astype(jnp.float32)
    pixel_count = frame_count * row_count * col_count
    scaling = 1.0 / math.sqrt(pixel_count * lax.axis_size("dp"))

    def tap_slice(source, tap_index, direction):
        row_step = tap_index // 3 - 1
        col_step = tap_index % 3 - 1
        anchor = (
            0,
            margin + direction * dilation * row_step,
            margin + direction * dilation * col_step,
            0,
        )
        return lax.dynamic_slice(source, anchor, (frame_count, row_count, col_count, chan_count))

    accum = jnp.zeros((frame_count, row_count, col_count, chan_count), jnp.float32)
    for tap_index in range(9):
        accum = accum + tap_slice(padded, tap_index, 1).astype(jnp.float32) * kernel[tap_index]
    depth_out = accum.astype(jnp.bfloat16)
    depth_rows = depth_out.reshape(pixel_count, chan_count)
    weight = pw_weight[0]
    branch_share = pw_bias.shape[1]
    columns = weight
    preact = (
        lax.psum_scatter(
            lax.dot_general(
                columns, depth_rows, (((0,), (1,)), ((), ())), preferred_element_type=jnp.float32
            ),
            "chan",
            scatter_dimension=0,
            tiled=True,
        )
        + pw_bias[0][:, None]
    )
    branch_act = jax.nn.silu(preact).astype(jnp.bfloat16)
    proj_local = proj[0]
    columns = proj_local
    zpart = lax.psum_scatter(
        lax.dot_general(
            columns, branch_act, (((0,), (0,)), ((), ())), preferred_element_type=jnp.float32
        ),
        "chan",
        scatter_dimension=0,
        tiled=True,
    )
    up_rows = upstream.reshape(branch_share, pixel_count).astype(jnp.float32)
    labeled = (labels != void_class).reshape(pixel_count).astype(jnp.float32)
    before = prefix(zpart, "section", add_terms, jnp.zeros_like(zpart))
    zvalue = before + zpart + proj_bias[:, None]
    result = jax.nn.silu(zvalue).astype(jnp.bfloat16)
    gradient = (up_rows * swish_slope(zvalue) * labeled[None, :]).astype(jnp.bfloat16)
    result, out_grad = (result, gradient)
    result, out_grad = (
        spread(result, "section", segments - 1),
        spread(out_grad, "section", segments - 1),
    )
    proj_bias_grad = jnp.sum(out_grad.astype(jnp.float32), axis=1) * scaling
    shard_rows = lax.all_gather(out_grad, "chan", axis=0, tiled=True)
    act_grad = jnp.dot(proj_local, shard_rows, preferred_element_type=jnp.float32)
    piece_grad = lax.dot_general(
        branch_act, shard_rows, (((1,), (1,)), ((), ())), preferred_element_type=jnp.float32
    )
    proj_grad = piece_grad
    act_grad, proj_grad = (act_grad, proj_grad)
    pre_grad = (act_grad * swish_slope(preact)).astype(jnp.bfloat16)
    pw_bias_grad = jnp.sum(pre_grad.astype(jnp.float32), axis=1) * scaling
    shard_rows = lax.all_gather(pre_grad, "chan", axis=0, tiled=True)
    columns = weight
    depth_acc = lax.dot_general(
        shard_rows, columns, (((0,), (1,)), ((), ())), preferred_element_type=jnp.float32
    )
    piece_grad = lax.dot_general(
        depth_rows, shard_rows, (((0,), (1,)), ((), ())), preferred_element_type=jnp.float32
    )
    weight_grad = piece_grad
    depth_acc, weight_grad = (depth_acc, weight_grad)
    depth_grad = depth_acc.astype(jnp.bfloat16).reshape(
        frame_count, row_count, col_count, chan_count
    )
    padded_grad = jnp.pad(depth_grad, ((0, 0), (margin, margin), (margin, margin), (0, 0)))
    depth_f = depth_grad.astype(jnp.float32)
    input_term = jnp.zeros((frame_count, row_count, col_count, chan_count), jnp.float32)
    tap_grads = []
    for tap_index in range(9):
        source = tap_slice(padded, tap_index, 1).astype(jnp.float32)
        tap_grads.append(jnp.sum(source * depth_f, axis=(0, 1, 2)) * scaling)
        input_term = (
            input_term
            + tap_slice(padded_grad, tap_index, -1).astype(jnp.float32) * kernel[tap_index]
        )
    kernel_grad = jnp.stack(tap_grads)
    input_rows = lax.psum_scatter(input_term, "section", scatter_dimension=1, tiled=True)
    input_grad = (input_rows * keep[:, None, :, None].astype(jnp.float32)).astype(jnp.bfloat16)
    kernel_grad, weight_grad, pw_bias_grad, proj_grad, proj_bias_grad = lax.psum(
        (kernel_grad, weight_grad * scaling, pw_bias_grad, proj_grad * scaling, proj_bias_grad),
        "dp",
    )
    aspp_out = result.reshape(branch_share, frame_count, row_count, col_count)
    return (
        aspp_out,
        input_grad,
        kernel_grad[None],
        weight_grad[None],
        pw_bias_grad[None],
        proj_grad[None],
        proj_bias_grad,
    )


def solution(mesh):
    in_specs = (
        P("dp", None, None, "chan"),
        P("dp"),
        P("dp"),
        P("dp", None, None),
        P("section", None, "chan"),
        P("section", "chan", None),
        P("section", "chan"),
        P("section", "chan", None),
        P("chan"),
        P("chan", "dp", None, None),
    )
    out_specs = (
        P("chan", "dp", None, None),
        P("dp", "section", None, "chan"),
        P("section", None, "chan"),
        P("section", "chan", None),
        P("section", "chan"),
        P("section", "chan", None),
        P("chan"),
    )
    return jax.shard_map(local, mesh=mesh, in_specs=in_specs, out_specs=out_specs, check_vma=False)
```

profile of v0, /device:TPU:0, one launch (start us, length us, event | category | flops | bytes accessed | tf_op | source)
XLA Modules:
  0.0 1201.1 jit_solution(8399671618688531222)
XLA Ops:
  7.2 0.0 reduce-scatter.7.cloned.1.call-start
  7.2 1.0 fusion.39
  8.4 1.3 fusion.37
  9.7 14.0 %broadcast_multiply_fusion = bf16[2,32,128,1024]{3,2,1,0:T(8,128)(2,1)} fusion(bf16[2,32,128,1024]{3,2,1,0:T(8,128)(2,1)} %param.12, bf16[2,128]{1,0:T(2,128)(2,1)S(1)} %get-tuple-element.146), kind=kLoop, calls=%fused_computation.67 | loop fusion | flops 8388608 | bytes 33554944 | tf_op jit(solution)/shard_map/mul | solution.py:52
  23.8 71.7 %fusion.8 = bf16[2,32,128,1024]{3,2,1,0:T(8,128)(2,1)} fusion(bf16[2,32,128,1024]{3,2,1,0:T(8,128)(2,1)} %broadcast_multiply_fusion, f32[1024]{0:T(1024)S(1)} %bitcast.118, f32[1024]{0:T(1024)S(1)} %bitcast.116, f32[1024]{0:T(1024)S(1)} %bitcast.114, f32[1024]{0:T(1024)S(1)} %bitcast.112, f32[1024]{0:T(1024)S(1)} %bitcast.110, f32[1024]{0:T(1024)S(1)} %bitcast.108, ...), kind=kLoop, calls=%fused_computation.44 | loop fusion | flops 226492416 | bytes 33591312 | tf_op jit(solution)/shard_map/convert_element_type | solution.py:72
  95.5 13.6 %convolution_bitcast_fusion.1 = f32[256,8192]{0,1:T(8,128)} fusion(bf16[8192,1024]{1,0:T(8,128)(2,1)} %bitcast.97, bf16[1,1024,256]{2,1,0:T(8,128)(2,1)S(1)} %copy-done), kind=kOutput, calls=%fused_computation.61 | convolution fusion | flops 4294967296 | bytes 25690112 | tf_op jit(solution)/shard_map/dot_general | solution.py:79
  109.1 0.0 reduce-scatter.9.cloned.1.call-start
  109.2 101.1 %reduce-scatter.7.cloned.1.call-done = f32[128,8192]{0,1:T(8,128)} async-done(((f32[256,8192]{0,1:T(8,128)}), f32[128,8192]{0,1:T(8,128)}) %reduce-scatter.7.cloned.1.call-update) | async-done | bytes 4194320 | tf_op jit(solution)/shard_map/reduce_scatter | solution.py:78
  210.3 6.8 convolution_bitcast_fusion
  217.2 0.0 all-gather.9.cloned.1.call-start
  217.2 99.3 %reduce-scatter.9.cloned.1.call-done = f32[128,8192]{0,1:T(8,128)} async-done(((f32[256,8192]{0,1:T(8,128)}), f32[128,8192]{0,1:T(8,128)}) %reduce-scatter.9.cloned.1.call-update) | async-done | bytes 4194320 | tf_op jit(solution)/shard_map/reduce_scatter | solution.py:91
  316.6 0.0 all-reduce.10.cloned.1.call-start
  316.7 3.4 copy.24
  320.1 106.2 %all-gather.9.cloned.1.call-done = f32[512,8192]{0,1:T(8,128)} async-done(((f32[128,8192]{0,1:T(8,128)}), f32[512,8192]{0,1:T(8,128)}) %all-gather.9.cloned.1.call-update) | async-done | bytes 16777232 | tf_op jit(solution)/shard_map/all_gather | solution.py:16
  426.3 17.5 %copy.25 = f32[512,8192]{1,0:T(8,128)} copy(f32[512,8192]{0,1:T(8,128)} %all-gather.9.cloned.1.call-done) | data formatting | bytes 33554432
  443.8 22.8 %while.14 = (s32[]{:T(128)}, f32[128,8192]{1,0:T(8,128)}, s32[]{:T(128)}, f32[4,128,8192]{2,1,0:T(8,128)}, s32[]{:T(128)}, /*index=5*/s32[]{:T(128)}) while((s32[]{:T(128)}, f32[128,8192]{1,0:T(8,128)}, s32[]{:T(128)}, f32[4,128,8192]{2,1,0:T(8,128)}, s32[]{:T(128)}, /*index=5*/s32[]{:T(128)}) %tuple.84), condition=%wide.region_3.4_spmd.clone, body=%wide.region_2.3_spmd.clone.sunk | while | flops 3145732 | bytes 12583005 | solution.py:24
  443.8 4.8 add_select_fusion.2
  448.5 6.0 add_select_fusion.2
  454.6 6.0 add_select_fusion.2
  460.6 6.0 add_select_fusion.2
  466.6 5.6 copy.22
  472.2 8.1 broadcast_select_fusion
  480.3 2.9 copy.23
  483.2 0.0 all-gather.5.cloned.1.call-start
  483.2 85.8 %all-reduce.10.cloned.1.call-done = (bf16[128,2,32,128]{3,2,1,0:T(8,128)(2,1)}, bf16[128,8192]{0,1:T(8,128)(2,1)}) async-done(((bf16[128,2,32,128]{3,2,1,0:T(8,128)(2,1)}, bf16[128,8192]{0,1:T(8,128)(2,1)}), (bf16[128,2,32,128]{3,2,1,0:T(8,128)(2,1)}, bf16[128,8192]{0,1:T(8,128)(2,1)})) %all-reduce.10.cloned.1.call-update) | async-done | bytes 4194320 | tf_op jit(solution)/shard_map/psum | solution.py:29
  569.1 0.0 all-gather.7.cloned.1.call-start
  569.1 58.3 %all-gather.5.cloned.1.call-done = bf16[256,8192]{0,1:T(8,128)(2,1)} async-done(((bf16[128,8192]{0,1:T(8,128)(2,1)}), bf16[256,8192]{0,1:T(8,128)(2,1)}) %all-gather.5.cloned.1.call-update) | async-done | bytes 4194320 | tf_op jit(solution)/shard_map/all_gather | solution.py:111
  627.4 7.3 convert_reduce_fusion.1
  634.7 0.0 reduce-scatter.11.cloned.1.call-start
  634.8 56.7 %all-gather.7.cloned.1.call-done = bf16[256,8192]{0,1:T(8,128)(2,1)} async-done(((bf16[128,8192]{0,1:T(8,128)(2,1)}), bf16[256,8192]{0,1:T(8,128)(2,1)}) %all-gather.7.cloned.1.call-update) | async-done | bytes 4194320 | tf_op jit(solution)/shard_map/all_gather | solution.py:120
  691.5 74.8 %fusion.22 = (f32[1024]{0:T(1024)S(1)}, f32[1024]{0:T(1024)S(1)}, f32[1024]{0:T(1024)S(1)}, f32[1024]{0:T(1024)S(1)}, f32[1024]{0:T(1024)S(1)}, /*index=5*/f32[1...) fusion(s32[]{:T(128)S(6)} %select_n.96, s32[]{:T(128)S(6)} %select_n.95, ...), kind=kOutput, calls=%fused_computation.58 | convolution fusion | flops 4538227712 | bytes 38309904 | tf_op jit(solution)/shard_map/dot_general | solution.py:122
  766.5 76.8 %fusion.13 = f32[2,32,128,1024]{3,2,1,0:T(8,128)} fusion(bf16[2,32,128,1024]{3,2,1,0:T(8,128)(2,1)} %bitcast.96, s32[]{:T(128)S(6)} %select_n.96, s32[]{:T(128)S(6)} %select_n.95, s32[]{:T(128)S(6)} %select_n.94, s32[]{:T(128)S(6)} %select_n.93, f32[1024]{0:T(1024)S(1)} %bitcast.119, f32[1024]{0:T(1024)S(1)} %bitcast.117, f32[1024]{0:T(1024)S(1)} %bitcast.115, ...), kind=kLoop, calls=%fused_computation.49 | loop fusion | flops 218103808 | bytes 50368528 | tf_op jit(solution)/shard_map/add | solution.py:141
  843.3 12.1 %copy.26 = f32[2,32,128,1024]{3,2,0,1:T(8,128)S(1)} copy(f32[2,32,128,1024]{3,2,1,0:T(8,128)} %fusion.13) | data formatting | bytes 67108864
  855.4 39.9 %copy.28 = f32[4,8,256,1024]{3,1,2,0:T(8,128)} copy(f32[4,8,256,1024]{3,2,1,0:T(8,128)S(1)} %bitcast.93) | data formatting | bytes 67108864
  895.3 0.0 all-reduce.8.cloned.1.call-start
  895.3 1.5 copy-done.2
  896.9 1.1 convert_reduce_fusion
  898.0 6.3 fusion.30
  904.3 13.0 %fusion.29 = f32[1,1024,256]{2,1,0:T(8,128)} fusion(bf16[8192,1024]{1,0:T(8,128)(2,1)} %bitcast.98, bf16[256,8192]{0,1:T(8,128)(2,1)S(1)} %copy-done.26), kind=kOutput, calls=%fused_computation.81 | convolution fusion | flops 4295229440 | bytes 22020096 | tf_op jit(solution)/shard_map/dot_general | solution.py:125
  917.4 0.1 stack.2
  917.5 20.6 %all-reduce.2 = (f32[1,9,1024]{2,0,1:T(1,128)}, f32[1,128]{1,0:T(1,128)}, f32[128]{0:T(128)}) all-reduce(f32[1,9,1024]{2,0,1:T(1,128)S(1)} %broadcast_in_dim.29, f32[1,128]{1,0:T(1,128)S(1)} %multiply_bitcast_fusion, f32[128]{0:T(128)S(1)} %broadcast_multiply_fusion.10), channel_id=1, replica_groups=mesh['section'=4,'dp'=4,'chan'=2] {'dp'}, use_global_device_ids=true, to_apply=%region_16.17 | all-reduce | flops 9472 | bytes 75776 | tf_op jit(solution)/shard_map/psum | solution.py:147
  938.1 191.3 %reduce-scatter.11.cloned.1.call-done = f32[8,262144]{1,0:T(8,128)} async-done(((f32[32,262144]{1,0:T(8,128)}), f32[8,262144]{1,0:T(8,128)}) %reduce-scatter.11.cloned.1.call-update) | async-done | bytes 8388624
  1129.4 8.3 copy.29
  1137.7 3.4 fusion.25
  1141.1 47.7 %all-reduce.8.cloned.1.call-done = (f32[1,1024,256]{2,1,0:T(8,128)}, f32[1,128,256]{2,1,0:T(8,128)}) async-done(((f32[1,1024,256]{2,1,0:T(8,128)}, f32[1,128,256]{2,1,0:T(8,128)}), (f32[1,1024,256]{2,1,0:T(8,128)}, f32[1,128,256]{2,1,0:T(8,128)})) %all-reduce.8.cloned.1.call-update) | async-done | bytes 1179664 | tf_op jit(solution)/shard_map/psum | solution.py:147
  1188.9 1.3 copy.43
  1190.2 2.3 copy.44
  1192.4 1.6 copy.45
  (79 shorter events, 0.3 us)
Async XLA Ops:
  7.2 88.3 %copy-start = (bf16[1,1024,256]{2,1,0:T(8,128)(2,1)S(1)}, bf16[1,1024,256]{2,1,0:T(8,128)(2,1)}, u32[]{:S(2)}) copy-start(bf16[1,1024,256]{2,1,0:T(8,128)(2,1)} %param.17) | copy-start | bytes 1572868
  7.2 203.1 %reduce-scatter.7.cloned.1.call-start = ((), (), s32[]{:S(2)}) async-start(), calls=%async_computation.3 | async-start | bytes 12582912 | tf_op jit(solution)/shard_map/reduce_scatter | solution.py:78
  8.3 15.4 %copy-start.5 = (f32[1,1,1024]{2,1,0:T(1,128)}, f32[1,1,1024]{2,1,0:T(1,128)S(1)}, u32[]{:S(2)}) copy-start(f32[1,1,1024]{2,1,0:T(1,128)S(1)} %get-tuple-element.136) | copy-start | bytes 12292
  8.3 15.4 %copy-start.7 = (f32[1,1,1024]{2,1,0:T(1,128)}, f32[1,1,1024]{2,1,0:T(1,128)S(1)}, u32[]{:S(2)}) copy-start(f32[1,1,1024]{2,1,0:T(1,128)S(1)} %get-tuple-element.137) | copy-start | bytes 12292
  8.3 15.4 %copy-start.9 = (f32[1,1,1024]{2,1,0:T(1,128)}, f32[1,1,1024]{2,1,0:T(1,128)S(1)}, u32[]{:S(2)}) copy-start(f32[1,1,1024]{2,1,0:T(1,128)S(1)} %get-tuple-element.138) | copy-start | bytes 12292
  8.3 15.4 %copy-start.11 = (f32[1,1,1024]{2,1,0:T(1,128)}, f32[1,1,1024]{2,1,0:T(1,128)S(1)}, u32[]{:S(2)}) copy-start(f32[1,1,1024]{2,1,0:T(1,128)S(1)} %get-tuple-element.139) | copy-start | bytes 12292
  8.3 15.4 %copy-start.13 = (f32[1,1,1024]{2,1,0:T(1,128)}, f32[1,1,1024]{2,1,0:T(1,128)S(1)}, u32[]{:S(2)}) copy-start(f32[1,1,1024]{2,1,0:T(1,128)S(1)} %get-tuple-element.140) | copy-start | bytes 12292
  8.3 15.4 %copy-start.15 = (f32[1,1,1024]{2,1,0:T(1,128)}, f32[1,1,1024]{2,1,0:T(1,128)S(1)}, u32[]{:S(2)}) copy-start(f32[1,1,1024]{2,1,0:T(1,128)S(1)} %get-tuple-element.141) | copy-start | bytes 12292
  8.3 15.4 %copy-start.17 = (f32[1,1,1024]{2,1,0:T(1,128)}, f32[1,1,1024]{2,1,0:T(1,128)S(1)}, u32[]{:S(2)}) copy-start(f32[1,1,1024]{2,1,0:T(1,128)S(1)} %get-tuple-element.142) | copy-start | bytes 12292
  8.4 15.4 %copy-start.19 = (f32[1,1,1024]{2,1,0:T(1,128)}, f32[1,1,1024]{2,1,0:T(1,128)S(1)}, u32[]{:S(2)}) copy-start(f32[1,1,1024]{2,1,0:T(1,128)S(1)} %get-tuple-element.143) | copy-start | bytes 12292
  8.4 15.4 %copy-start.21 = (f32[1,1,1024]{2,1,0:T(1,128)}, f32[1,1,1024]{2,1,0:T(1,128)S(1)}, u32[]{:S(2)}) copy-start(f32[1,1,1024]{2,1,0:T(1,128)S(1)} %get-tuple-element.144) | copy-start | bytes 12292
  95.5 114.8 %copy-start.27 = (bf16[1,128,256]{2,1,0:T(8,128)(2,1)S(1)}, bf16[1,128,256]{2,1,0:T(8,128)(2,1)}, u32[]{:S(2)}) copy-start(bf16[1,128,256]{2,1,0:T(8,128)(2,1)} %param.19) | copy-start | bytes 196612
  95.5 114.8 %copy-start.28 = (f32[1,128]{1,0:T(1,128)S(1)}, f32[1,128]{1,0:T(1,128)}, u32[]{:S(2)}) copy-start(f32[1,128]{1,0:T(1,128)} %param.18) | copy-start | bytes 1540
  109.1 207.4 %reduce-scatter.9.cloned.1.call-start = ((), (), s32[]{:S(2)}) async-start(), calls=%async_computation.4 | async-start | bytes 12582912 | tf_op jit(solution)/shard_map/reduce_scatter | solution.py:91
  210.3 106.3 %copy-start.3 = (bf16[128,2,32,128]{3,2,1,0:T(8,128)(2,1)S(1)}, bf16[128,2,32,128]{3,2,1,0:T(8,128)(2,1)}, u32[]{:S(2)}) copy-start(bf16[128,2,32,128]{3,2,1,0:T(8,128)(2,1)} %param.21) | copy-start | bytes 6291460
  217.1 102.9 %copy-start.23 = (s32[2,32,128]{2,1,0:T(8,128)S(1)}, s32[2,32,128]{2,1,0:T(8,128)}, u32[]{:S(2)}) copy-start(s32[2,32,128]{2,1,0:T(8,128)} %param.15) | copy-start | bytes 98308
  217.2 209.2 %all-gather.9.cloned.1.call-start = ((), (), s32[]{:S(2)}) async-start(), calls=%async_computation.7 | async-start | bytes 20971520 | tf_op jit(solution)/shard_map/all_gather | solution.py:16
  316.6 252.4 %all-reduce.10.cloned.1.call-start = ((), (), s32[]{:S(2)}) async-start(), calls=%async_computation.10 | async-start | bytes 8388608 | tf_op jit(solution)/shard_map/psum | solution.py:29
  443.8 28.4 %copy-start.25 = (f32[128]{0:T(128)S(1)}, f32[128]{0:T(128)}, u32[]{:S(2)}) copy-start(f32[128]{0:T(128)} %param.20) | copy-start | bytes 1540
  483.2 144.2 %all-gather.5.cloned.1.call-start = ((), (), s32[]{:S(2)}) async-start(), calls=%async_computation.5 | async-start | bytes 6291456 | tf_op jit(solution)/shard_map/all_gather | solution.py:111
  569.1 122.5 %all-gather.7.cloned.1.call-start = ((), (), s32[]{:S(2)}) async-start(), calls=%async_computation.6 | async-start | bytes 6291456 | tf_op jit(solution)/shard_map/all_gather | solution.py:120
  634.7 131.7 %copy-start.6 = (f32[1,1,1024]{2,1,0:T(1,128)S(1)}, f32[1,1,1024]{2,1,0:T(1,128)}, u32[]{:S(2)}) copy-start(f32[1,1,1024]{2,1,0:T(1,128)} %copy-done.5) | copy-start | bytes 12292
  634.7 131.7 %copy-start.8 = (f32[1,1,1024]{2,1,0:T(1,128)S(1)}, f32[1,1,1024]{2,1,0:T(1,128)}, u32[]{:S(2)}) copy-start(f32[1,1,1024]{2,1,0:T(1,128)} %copy-done.7) | copy-start | bytes 12292
  634.7 131.7 %copy-start.10 = (f32[1,1,1024]{2,1,0:T(1,128)S(1)}, f32[1,1,1024]{2,1,0:T(1,128)}, u32[]{:S(2)}) copy-start(f32[1,1,1024]{2,1,0:T(1,128)} %copy-done.9) | copy-start | bytes 12292
  634.7 131.7 %copy-start.12 = (f32[1,1,1024]{2,1,0:T(1,128)S(1)}, f32[1,1,1024]{2,1,0:T(1,128)}, u32[]{:S(2)}) copy-start(f32[1,1,1024]{2,1,0:T(1,128)} %copy-done.11) | copy-start | bytes 12292
  634.7 131.7 %copy-start.14 = (f32[1,1,1024]{2,1,0:T(1,128)S(1)}, f32[1,1,1024]{2,1,0:T(1,128)}, u32[]{:S(2)}) copy-start(f32[1,1,1024]{2,1,0:T(1,128)} %copy-done.13) | copy-start | bytes 12292
  634.7 131.7 %copy-start.16 = (f32[1,1,1024]{2,1,0:T(1,128)S(1)}, f32[1,1,1024]{2,1,0:T(1,128)}, u32[]{:S(2)}) copy-start(f32[1,1,1024]{2,1,0:T(1,128)} %copy-done.15) | copy-start | bytes 12292
  634.7 131.7 %copy-start.18 = (f32[1,1,1024]{2,1,0:T(1,128)S(1)}, f32[1,1,1024]{2,1,0:T(1,128)}, u32[]{:S(2)}) copy-start(f32[1,1,1024]{2,1,0:T(1,128)} %copy-done.17) | copy-start | bytes 12292
  634.7 131.7 %copy-start.20 = (f32[1,1,1024]{2,1,0:T(1,128)S(1)}, f32[1,1,1024]{2,1,0:T(1,128)}, u32[]{:S(2)}) copy-start(f32[1,1,1024]{2,1,0:T(1,128)} %copy-done.19) | copy-start | bytes 12292
  634.7 131.7 %copy-start.22 = (f32[1,1,1024]{2,1,0:T(1,128)S(1)}, f32[1,1,1024]{2,1,0:T(1,128)}, u32[]{:S(2)}) copy-start(f32[1,1,1024]{2,1,0:T(1,128)} %copy-done.21) | copy-start | bytes 12292
  634.7 494.6 %reduce-scatter.11.cloned.1.call-start = ((), (), s32[]{:S(2)}) async-start(), calls=%async_computation.8 | async-start | bytes 41943040
  895.3 1.6 copy-start.2
  895.3 2.7 copy-start.30
  895.3 2.7 copy-start.29
  895.3 293.6 %all-reduce.8.cloned.1.call-start = ((), (), s32[]{:S(2)}) async-start(), calls=%async_computation.9 | async-start | bytes 2359296 | tf_op jit(solution)/shard_map/psum | solution.py:147
  896.8 7.4 copy-start.26
  904.3 233.4 %copy-start.24 = (f32[2,128]{1,0:T(2,128)S(1)}, f32[2,128]{1,0:T(2,128)}, u32[]{:S(2)}) copy-start(f32[2,128]{1,0:T(2,128)} %get-tuple-element.145) | copy-start | bytes 3076
  917.3 271.5 %copy-start.4 = (bf16[128,2,32,128]{3,2,1,0:T(8,128)(2,1)S(1)}, bf16[128,2,32,128]{3,2,1,0:T(8,128)(2,1)}, u32[]{:S(2)}) copy-start(bf16[128,2,32,128]{3,2,1,0:T(8,128)(2,1)} %get-tuple-element.201) | copy-start | bytes 6291460
  1129.4 64.6 %copy-start.1 = (bf16[1,1024,256]{2,1,0:T(8,128)(2,1)S(1)}, bf16[1,1024,256]{2,1,0:T(8,128)(2,1)}, u32[]{:S(2)}) copy-start(bf16[1,1024,256]{2,1,0:T(8,128)(2,1)} %param.17) | copy-start | bytes 1572868
Sparse Core Ops, SparseCore 0:
  109.3 100.9 reduce-scatter.6
  217.3 99.2 reduce-scatter.8
  318.1 108.1 all-gather.8
  483.3 85.6 all-reduce.9
  570.5 56.8 all-gather.4
  634.8 56.7 all-gather.6
  895.4 233.9 reduce-scatter.10
  1132.5 56.2 all-reduce.7
where the time goes:
time: 1210 us; the launch traced here: 1200 us
  waiting for transfers between devices  747 us (62%)
  other arithmetic  199 us (16%)
  matrix products  122 us (10%)
  local copies, waits for them, and re-layouts  97.6 us (8%)
  blocking collectives  20.6 us (2%)
  between operations  14.8 us (1%)
    unnamed x9, waiting for transfers between devices  191 us
    all_gather x1, waiting for transfers between devices, prefix(): everything = lax.all_gather(shard, axis)  106 us
    reduce_scatter x1, waiting for transfers between devices, local(): lax.psum_scatter(lax.dot_general(columns, depth_rows, (((0,), (1,)), ((),...  101 us
    reduce_scatter x1, waiting for transfers between devices, local(): lax.psum_scatter(lax.dot_general(columns, branch_act, (((0,), (0,)), ((),...  99.3 us
    psum x1, waiting for transfers between devices, spread(): return lax.psum(kept, axis)  85.8 us
    unnamed x69, local copies, waits for them, and re-layouts  84.5 us
    add x1, other arithmetic, local(): input_term + tap_slice(padded_grad, tap_index, -1).astype(jnp.float32) *...  76.8 us
    dot_general x1, matrix products, local(): lax.dot_general(shard_rows, columns, (((0,), (1,)), ((), ())), preferred_...  74.8 us
  transfers between devices with their start and end apart: 8, of which 8 were waited for; matrix products, arithmetic and copies ran while one was open for 3% of the time, Pallas kernels for 0%

commit v1 on v0

v1 whole, which is shorter than its diff:
```python
import math

import jax
import jax.numpy as jnp
from jax import lax
from jax.experimental import pallas as pl
from jax.experimental.pallas import tpu as pltpu
from jax.sharding import PartitionSpec as P

RATE = 6
BAND = 64
VOID = 19
LANES = 128
VMEM_LIMIT = 56 * 1024 * 1024


def swish_slope(value):
    sig = jax.nn.sigmoid(value)
    return sig * (1.0 + value * (1.0 - sig))


def column_masks(first, step, count, cols):
    place = lax.broadcasted_iota(jnp.int32, (count, LANES), 0) + first
    place = jnp.where(place >= cols, place - cols, place)
    place = jnp.where(place < 0, place + cols, place)
    lower = (place - step >= 0).astype(jnp.float32)
    upper = (place + step < cols).astype(jnp.float32)
    return lower, upper


def forward_kernel(scal, feats, taps, weight, depth, band, pre, masked, doubled, left, right, *, margin, wing):
    rows, cols, chans = feats.shape[1:]
    ext = depth.shape[1]
    off, width, rate = scal[0], scal[1], scal[2]
    groups = [pl.ds(g * LANES, LANES) for g in range(chans // LANES)]

    @pl.when(pl.program_id(0) == 0)
    def _():
        masked[...] = jnp.zeros_like(masked)
        left[...] = jnp.zeros_like(left)
        right[...] = jnp.zeros_like(right)
        pre[...] = jnp.zeros_like(pre)

    inside = (lax.broadcasted_iota(jnp.int32, (BAND, LANES), 0) < width).astype(jnp.float32)

    def fill(h, carry):
        for g, lanes in enumerate(groups):
            row = feats[0, h, :, lanes].astype(jnp.float32)
            doubled[g, 0:cols] = row
            doubled[g, cols:cols + BAND] = row[0:BAND]
            part = doubled[g, pl.ds(off, BAND)] * inside
            masked[margin + h, :, lanes] = part
            band[h, :, lanes] = part.astype(jnp.bfloat16)
        return carry

    lax.fori_loop(0, rows, fill, 0)

    lower, upper = column_masks(off - wing, rate, ext, cols)
    kernel = taps[...].astype(jnp.float32)
    batch = 4 if rows % 4 == 0 else 1

    def row_group(i, carry):
        for k in range(batch):
            h = i * batch + k
            for g in range(chans // LANES):
                lanes = groups[g]
                sources = [masked[h + margin + (t - 1) * rate, :, lanes] for t in range(3)]
                sums = []
                for j in range(3):
                    total = sources[0] * kernel[j:j + 1, g * LANES:(g + 1) * LANES]
                    for t in (1, 2):
                        total = total + sources[t] * kernel[3 * t + j:3 * t + j + 1, g * LANES:(g + 1) * LANES]
                    sums.append(total)
                left[k, g, 2 * wing:2 * wing + BAND] = sums[0]
                right[k, g, wing:wing + BAND] = sums[2]
                from_left = left[k, g, pl.ds(wing - rate, ext)] * lower
                from_right = right[k, g, pl.ds(rate, ext)] * upper
                wings = jnp.zeros((wing, LANES), jnp.float32)
                middle = jnp.concatenate([wings, sums[1], wings], axis=0)
                depth[h, :, lanes] = (from_left + from_right + middle).astype(jnp.bfloat16)
        some = depth[pl.ds(i * batch, batch)].reshape(batch * ext, chans)
        here = pl.ds(pl.multiple_of(i * batch * ext, 16), batch * ext)
        pre[here, :] += jnp.dot(some, weight[...], preferred_element_type=jnp.float32)
        return carry

    lax.fori_loop(0, rows // batch, row_group, 0)


def forward_call(scal, feats, taps, weight, frame, margin, wing):
    rows, cols, chans = feats.shape[1:]
    ext = BAND + 2 * wing
    block = min(256, chans)
    outs = weight.shape[1]
    buffer = 3 * wing + BAND
    return pl.pallas_call(
        lambda *refs: forward_kernel(*refs, margin=margin, wing=wing),
        grid_spec=pltpu.PrefetchScalarGridSpec(
            num_scalar_prefetch=1,
            grid=(chans // block,),
            in_specs=[
                pl.BlockSpec((1, rows, cols, block), lambda c, s: (frame, 0, 0, c)),
                pl.BlockSpec((9, block), lambda c, s: (0, c)),
                pl.BlockSpec((block, outs), lambda c, s: (c, 0)),
            ],
            out_specs=[
                pl.BlockSpec((rows, ext, block), lambda c, s: (0, 0, c)),
                pl.BlockSpec((rows, BAND, block), lambda c, s: (0, 0, c)),
                pl.BlockSpec((rows * ext, outs), lambda c, s: (0, 0)),
            ],
            scratch_shapes=[
                pltpu.VMEM((rows + 2 * margin, BAND, block), jnp.float32),
                pltpu.VMEM((block // LANES, cols + BAND, LANES), jnp.float32),
                pltpu.VMEM((4, block // LANES, buffer, LANES), jnp.float32),
                pltpu.VMEM((4, block // LANES, buffer, LANES), jnp.float32),
            ],
        ),
        out_shape=[
            jax.ShapeDtypeStruct((rows, ext, chans), jnp.bfloat16),
            jax.ShapeDtypeStruct((rows, BAND, chans), jnp.bfloat16),
            jax.ShapeDtypeStruct((rows * ext, outs), jnp.float32),
        ],
        compiler_params=pltpu.CompilerParams(vmem_limit_bytes=VMEM_LIMIT),
        cost_estimate=pl.CostEstimate(
            flops=2 * rows * ext * chans * outs, bytes_accessed=2 * rows * chans * (cols + ext + BAND), transcendentals=0
        ),
        name="depth_pointwise",
    )(scal, feats, taps, weight)


def backward_kernel(scal, grad, weight, taps, band, term, dw, spread, *, margin, wing):
    rows, ext, outs = grad.shape
    chans = weight.shape[0]
    cols = scal[3]
    off, width, rate = scal[0], scal[1], scal[2]
    batch = 4 if rows % 4 == 0 else 1

    @pl.when(pl.program_id(0) == 0)
    def _():
        spread[...] = jnp.zeros_like(spread)

    def product(i, carry):
        some = grad[pl.ds(i * batch, batch)].reshape(batch * ext, outs)
        out = lax.dot_general(some, weight[...], (((1,), (1,)), ((), ())), preferred_element_type=jnp.float32)
        out = out.astype(jnp.bfloat16).astype(jnp.float32).reshape(batch, ext, chans)
        for g in range(chans // LANES):
            spread[g, pl.ds(margin + i * batch, batch)] = out[:, :, g * LANES:(g + 1) * LANES]
        return carry

    lax.fori_loop(0, rows // batch, product, 0)

    lower, upper = column_masks(off, rate, BAND, cols)
    inside = (lax.broadcasted_iota(jnp.int32, (BAND, LANES), 0) < width).astype(jnp.float32)
    kernel = taps[...].astype(jnp.float32)
    valid = (upper * inside, inside, lower * inside)

    for g in range(chans // LANES):
        lanes = pl.ds(g * LANES, LANES)

        def one_row(h, sums):
            here = band[h, :, lanes].astype(jnp.float32)
            total = None
            new = []
            for j in range(3):
                source = here * valid[j] if j != 1 else here
                part = None
                for t in range(3):
                    value = spread[g, h + margin - (t - 1) * rate, pl.ds(wing - (j - 1) * rate, BAND)]
                    new.append(sums[3 * j + t] + (source * value).reshape(BAND // 8, 8, LANES).sum(axis=0))
                    scaled = value * kernel[3 * t + j:3 * t + j + 1, g * LANES:(g + 1) * LANES]
                    part = scaled if part is None else part + scaled
                part = part * valid[j]
                total = part if total is None else total + part
            term[h, :, lanes] = total.astype(jnp.bfloat16)
            return tuple(new)

        start = tuple(jnp.zeros((8, LANES), jnp.float32) for _ in range(9))
        sums = lax.fori_loop(0, rows, one_row, start)
        for t in range(3):
            for j in range(3):
                dw[3 * t + j:3 * t + j + 1, lanes] = jnp.sum(sums[3 * j + t], axis=0, keepdims=True)


def backward_call(scal, grad, weight, taps, band, margin, wing):
    rows, ext, outs = grad.shape
    chans = weight.shape[0]
    block = min(256, chans)
    return pl.pallas_call(
        lambda *refs: backward_kernel(*refs, margin=margin, wing=wing),
        grid_spec=pltpu.PrefetchScalarGridSpec(
            num_scalar_prefetch=1,
            grid=(chans // block,),
            in_specs=[
                pl.BlockSpec((rows, ext, outs), lambda c, s: (0, 0, 0)),
                pl.BlockSpec((block, outs), lambda c, s: (c, 0)),
                pl.BlockSpec((9, block), lambda c, s: (0, c)),
                pl.BlockSpec((rows, BAND, block), lambda c, s: (0, 0, c)),
            ],
            out_specs=[
                pl.BlockSpec((rows, BAND, block), lambda c, s: (0, 0, c)),
                pl.BlockSpec((9, block), lambda c, s: (0, c)),
            ],
            scratch_shapes=[pltpu.VMEM((block // LANES, rows + 2 * margin, ext, LANES), jnp.float32)],
        ),
        out_shape=[
            jax.ShapeDtypeStruct((rows, BAND, chans), jnp.bfloat16),
            jax.ShapeDtypeStruct((9, chans), jnp.float32),
        ],
        compiler_params=pltpu.CompilerParams(vmem_limit_bytes=VMEM_LIMIT),
        cost_estimate=pl.CostEstimate(
            flops=2 * rows * ext * chans * outs, bytes_accessed=8 * rows * chans * BAND, transcendentals=0
        ),
        name="depth_gradients",
    )(scal, grad, weight, taps, band)


def pick(array, index, axis=0):
    return lax.dynamic_index_in_dim(array, index, axis, keepdims=False)


def owner_sum(blocks, axis):
    size, me = lax.axis_size(axis), lax.axis_index(axis)
    total = pick(blocks, me).astype(jnp.float32)
    for k in range(1, size):
        sent = pick(blocks, lax.rem(me + k, size)).astype(jnp.bfloat16)
        total = total + lax.ppermute(sent, axis, [(i, (i + k) % size) for i in range(size)]).astype(jnp.float32)
    return total


def trade(blocks, axis):
    size, me = lax.axis_size(axis), lax.axis_index(axis)
    result = blocks
    for k in range(1, size):
        sent = pick(blocks, lax.rem(me + k, size))
        got = lax.ppermute(sent, axis, [(i, (i + k) % size) for i in range(size)])
        result = lax.dynamic_update_index_in_dim(result, got, lax.rem(me + size - k, size), 0)
    return result


def gather(block, axis):
    size, me = lax.axis_size(axis), lax.axis_index(axis)
    if size == 2:
        got = lax.ppermute(block, axis, [(0, 1), (1, 0)])
        return jnp.where(me == 0, jnp.stack([block, got]), jnp.stack([got, block]))
    return lax.all_gather(block, axis)


def halving_sum(blocks, axis):
    size, me = lax.axis_size(axis), lax.axis_index(axis)
    shape = blocks.shape[1:]
    bit = 1
    while bit < size:
        blocks = blocks.reshape((blocks.shape[0] // 2, 2) + shape)
        mine = lax.rem(me // bit, 2)
        sent = pick(blocks, 1 - mine, 1).astype(jnp.bfloat16)
        got = lax.ppermute(sent, axis, [(i, i ^ bit) for i in range(size)])
        blocks = pick(blocks, mine, 1).astype(jnp.float32) + got.astype(jnp.float32)
        bit *= 2
    return blocks[0]


def doubling_gather(block, axis):
    size, me = lax.axis_size(axis), lax.axis_index(axis)
    shape = block.shape
    block = block[None]
    bit = size // 2
    while bit:
        got = lax.ppermute(block, axis, [(i, i ^ bit) for i in range(size)])
        mine = lax.rem(me // bit, 2)
        both = jnp.where(mine == 0, jnp.stack([block, got], 1), jnp.stack([got, block], 1))
        block = both.reshape((2 * block.shape[0],) + shape)
        bit //= 2
    return block


def rolled(array, start, axis):
    length = array.shape[axis]
    return lax.dynamic_slice_in_dim(jnp.concatenate([array, array], axis), start, length, axis)


def local(feats, offsets, widths, labels, dw_kernel, pw_weight, pw_bias, proj, proj_bias, upstream):
    frames, rows, cols, chans = feats.shape
    sections, parts = lax.axis_size("section"), lax.axis_size("chan")
    section, part = lax.axis_index("section"), lax.axis_index("chan")
    rate = (RATE * section).astype(jnp.int32)
    margin = RATE * (sections - 1)
    wing = -(-margin // 8) * 8
    ext = BAND + 2 * wing
    share = pw_bias.shape[1]
    branch = share * parts
    scaling = 1.0 / math.sqrt(frames * rows * cols * lax.axis_size("dp"))
    rows_own = rows // parts
    pixels = rows_own * cols
    piece = pixels // sections
    taps, weight = dw_kernel[0], pw_weight[0]

    proj_all = lax.all_gather(proj[0], "chan", axis=0, tiled=True)
    biases = lax.all_gather(jnp.stack([pw_bias[0], proj_bias]), "chan", axis=1, tiled=True)
    pw_bias_all, proj_bias_all = biases[0], biases[1]

    starts = [lax.rem(offsets[f] + (cols - wing), cols) for f in range(frames)]
    scals = [jnp.stack([offsets[f], widths[f], rate, jnp.int32(cols)]) for f in range(frames)]

    ups, labeled = [], []
    for f in range(frames):
        up = rolled(upstream[:, f], starts[f], 2).reshape(share, parts, sections, piece)
        up = pick(up, section, 2).transpose(1, 0, 2)
        ups.append(trade(up, "chan").reshape(branch, piece).T)
        marks = rolled(labels[f], starts[f], 1).reshape(parts, sections, piece)
        labeled.append((pick(pick(marks, part), section) != VOID).astype(jnp.float32))

    firsts = [forward_call(scals[f], feats, taps, weight, f, margin, wing) for f in range(frames)]

    results, terms = [], []
    dw_sum = pw_sum = proj_sum = pw_bias_sum = proj_bias_sum = 0.0
    for f in range(frames):
        depth, band, pre = firsts[f]
        own = owner_sum(pre.reshape(parts, rows_own * ext, branch), "chan") + pw_bias_all
        rest = jnp.broadcast_to(pw_bias_all, (rows_own, cols - ext, branch))
        preact = jnp.concatenate([own.reshape(rows_own, ext, branch), rest], axis=1).reshape(pixels, branch)
        act = jax.nn.silu(preact).astype(jnp.bfloat16)
        zpart = jnp.dot(act, proj_all, preferred_element_type=jnp.float32)
        zvalue = halving_sum(zpart.reshape(sections, piece, branch), "section") + proj_bias_all
        result = jax.nn.silu(zvalue).astype(jnp.bfloat16)
        out_grad = ups[f].astype(jnp.float32) * swish_slope(zvalue) * labeled[f][:, None]
        out_grad = doubling_gather(out_grad.astype(jnp.bfloat16), "section").reshape(pixels, branch)

        act_grad = lax.dot_general(out_grad, proj_all, (((1,), (1,)), ((), ())), preferred_element_type=jnp.float32)
        pre_grad = (act_grad * swish_slope(preact)).astype(jnp.bfloat16)
        sent = pre_grad.reshape(rows_own, cols, branch)[:, :ext]
        grad_rows = gather(sent, "chan").reshape(rows, ext, branch)
        term, dw = backward_call(scals[f], grad_rows, weight, taps, band, margin, wing)
        own_rows = halving_sum(term.reshape(sections, rows // sections, BAND, chans), "section")
        own_rows = jnp.pad(own_rows.astype(jnp.bfloat16), ((0, 0), (0, cols - BAND), (0, 0)))
        terms.append(rolled(own_rows, lax.rem(cols - offsets[f], cols), 1))

        swapped = trade(result.reshape(piece, parts, share).transpose(1, 2, 0), "chan")
        whole = doubling_gather(swapped, "section").transpose(2, 1, 0, 3).reshape(share, rows, cols)
        results.append(rolled(whole, lax.rem(cols - starts[f], cols), 2))

        dw_sum = dw_sum + dw
        pw_sum = pw_sum + lax.dot_general(
            depth.reshape(rows * ext, chans), grad_rows.reshape(rows * ext, branch),
            (((0,), (0,)), ((), ())), preferred_element_type=jnp.float32,
        )
        proj_sum = proj_sum + lax.dot_general(
            act, out_grad, (((0,), (0,)), ((), ())), preferred_element_type=jnp.float32
        )
        pw_bias_sum = pw_bias_sum + jnp.sum(pre_grad.astype(jnp.float32), axis=0)
        proj_bias_sum = proj_bias_sum + jnp.sum(out_grad.astype(jnp.float32), axis=0)

    shared = jnp.concatenate([proj_sum, pw_bias_sum[None], proj_bias_sum[None]], axis=0) * scaling
    shared = lax.psum(shared, ("chan", "dp"))
    kernel_grad, weight_grad = lax.psum((dw_sum * scaling, pw_sum * scaling), "dp")
    mine = part * share
    return (
        jnp.stack(results, 1),
        jnp.stack(terms, 0),
        kernel_grad[None],
        weight_grad[None],
        lax.dynamic_slice_in_dim(shared[branch], mine, share)[None],
        lax.dynamic_slice_in_dim(shared, mine, share, 0)[None],
        lax.dynamic_slice_in_dim(shared[branch + 1], mine, share),
    )


def solution(mesh):
    in_specs = (
        P("dp", None, None, "chan"),
        P("dp"),
        P("dp"),
        P("dp", None, None),
        P("section", None, "chan"),
        P("section", "chan", None),
        P("section", "chan"),
        P("section", "chan", None),
        P("chan"),
        P("chan", "dp", None, None),
    )
    out_specs = (
        P("chan", "dp", None, None),
        P("dp", "section", None, "chan"),
        P("section", None, "chan"),
        P("section", "chan", None),
        P("section", "chan"),
        P("section", "chan", None),
        P("chan"),
    )
    return jax.shard_map(local, mesh=mesh, in_specs=in_specs, out_specs=out_specs, check_vma=False)
```

time: 1210 us -> 363 us (0.30)
  waiting for transfers between devices: 747 us -> 60.8 us
  other arithmetic: 199 us -> 49.2 us
  matrix products: 122 us -> 12 us
  Pallas kernels: 0 us -> 101 us
  local copies, waits for them, and re-layouts: 97.6 us -> 50.2 us
  blocking collectives: 20.6 us -> 46.2 us
  starting transfers between devices: 0.32 us -> 19.3 us
    all_gather x3 -> x0, waiting for transfers between devices: 221 us -> none  [the longest x1 106 us: prefix(): everything = lax.all_gather(shard, axis)]
    reduce_scatter x2 -> x0, waiting for transfers between devices: 200 us -> none  [the longest x1 101 us: local(): lax.psum_scatter(lax.dot_general(columns, depth_rows, (((0,), (1,)), ((),...]
    unnamed x9 -> x2, waiting for transfers between devices: 191 us -> 0.03 us
    psum x2, waiting for transfers between devices: 134 us -> 12.2 us  [the longest x1 12.2 us: local(): lax.psum((dw_sum * scaling, pw_sum * scaling), 'dp')]
    dot_general x6 -> x8, matrix products: 122 us -> 12 us  [the longest x2 8.42 us: local(): lax.dot_general(depth.reshape(rows * ext, chans), grad_rows.reshape(rows...]
    pallas_call x0 -> x4, Pallas kernels: none -> 101 us  [the longest x2 54.1 us: backward_call(): pl.pallas_call(lambda *refs: backward_kernel(*refs, margin=margin, wing=w...]
    unnamed x69 -> x55, local copies, waits for them, and re-layouts: 84.5 us -> 11.3 us
    convert_element_type x4 -> x8, other arithmetic: 76.5 us -> 8.67 us  [the longest x2 2.5 us: local(): own_rows.astype(jnp.bfloat16)]
  transfers between devices with their start and end apart: 8 -> 26, of which waited for: 8 -> 11; matrix products, arithmetic and copies ran while one was open for 3% -> 23% of each run, Pallas kernels for 0% -> 22%
where the time goes in v1:
time: 363 us; the launch traced here: 358 us
  Pallas kernels  101 us (28%)
  waiting for transfers between devices  60.8 us (17%)
  local copies, waits for them, and re-layouts  50.2 us (14%)
  other arithmetic  49.2 us (14%)
  blocking collectives  46.2 us (13%)
  starting transfers between devices  19.3 us (5%)
  between operations  19.2 us (5%)
  matrix products  12 us (3%)
    pallas_call x2, Pallas kernels, backward_call(): pl.pallas_call(lambda *refs: backward_kernel(*refs, margin=margin, wing=w...  54.1 us
    pallas_call x2, Pallas kernels, forward_call(): pl.pallas_call(lambda *refs: forward_kernel(*refs, margin=margin, wing=wi...  46.5 us
    psum x1, blocking collectives, local(): lax.psum((dw_sum * scaling, pw_sum * scaling), 'dp')  22.9 us
    ppermute x8, waiting for transfers between devices, halving_sum(): got = lax.ppermute(sent, axis, [(i, i ^ bit) for i in range(size)])  19.3 us
    all_gather x1, blocking collectives, local(): lax.all_gather(jnp.stack([pw_bias[0], proj_bias]), 'chan', axis=1, tiled=...  17.7 us
    ppermute x8, waiting for transfers between devices, doubling_gather(): got = lax.ppermute(block, axis, [(i, i ^ bit) for i in range(size)])  14.5 us
    ppermute x2, waiting for transfers between devices, gather(): got = lax.ppermute(block, axis, [(0, 1), (1, 0)])  13 us
    psum x1, waiting for transfers between devices, local(): lax.psum((dw_sum * scaling, pw_sum * scaling), 'dp')  12.2 us
  transfers between devices with their start and end apart: 26, of which 11 were waited for; matrix products, arithmetic and copies ran while one was open for 23% of the time, Pallas kernels for 22%

profile of v1, /device:TPU:0, one launch (start us, length us, event | category | flops | bytes accessed | tf_op | source)
XLA Modules:
  0.0 357.6 jit_solution(14522032993608563277)
XLA Ops:
  10.7 3.3 pad_add_fusion
  13.9 23.4 %depth_pointwise.2 = (bf16[32,112,1024]{2,1,0:T(8,128)(2,1)}, bf16[32,64,1024]{2,1,0:T(8,128)(2,1)}, f32[3584,256]{1,0:T(8,128)}) custom-call(s32[4]{0:T(128)} %get-tuple-element.96.refs_0_, bf16[2,32,128,1024]{3,2,1,0:T(8,128)(2,1)} %refs_1_.3, bf16[9,1024]{1,0:T(8,128)(2,1)} %bitcast.320, bf16[1024,256]{1,0:T(8,128)(2,1)} %bitcast.298), custom_call_target="tpu_custom_call" | custom-call | flops 1879048192 | bytes 19922944 | tf_op jit(solution)/shard_map/depth_pointwise/pallas_call | solution.py:95
  37.3 2.5 fusion.28
  39.8 3.0 collective-permute-start
  42.8 23.2 %depth_pointwise.3 = (bf16[32,112,1024]{2,1,0:T(8,128)(2,1)}, bf16[32,64,1024]{2,1,0:T(8,128)(2,1)}, f32[3584,256]{1,0:T(8,128)}) custom-call(s32[4]{0:T(128)} %get-tuple-element.95.refs_0_, bf16[2,32,128,1024]{3,2,1,0:T(8,128)(2,1)} %refs_1_.3, bf16[9,1024]{1,0:T(8,128)(2,1)} %bitcast.321, bf16[1024,256]{1,0:T(8,128)(2,1)} %bitcast.299), custom_call_target="tpu_custom_call" | custom-call | flops 1879048192 | bytes 19922944 | tf_op jit(solution)/shard_map/depth_pointwise/pallas_call | solution.py:95
  66.0 2.5 fusion.29
  69.8 1.9 fusion.47
  75.5 2.1 collective-permute-start.18
  79.8 17.7 %all_gather.6 = f32[2,256]{1,0:T(2,128)S(1)} all-gather(f32[2,128]{1,0:T(2,128)S(1)} %pad_maximum_fusion.4), channel_id=1, replica_groups=mesh['section'=4,'dp'=4,'chan'=2] {'chan'}, dimensions={1}, use_global_device_ids=true | all-gather | bytes 3072 | tf_op jit(solution)/shard_map/all_gather | solution.py:297
  98.0 5.7 %all-gather = bf16[1,256,256]{2,1,0:T(8,128)(2,1)S(1)} all-gather(bf16[1,128,256]{2,1,0:T(8,128)(2,1)} %param.17), channel_id=2, replica_groups=mesh['section'=4,'dp'=4,'chan'=2] {'chan'}, dimensions={1}, use_global_device_ids=true | all-gather | bytes 196608 | tf_op jit(solution)/shard_map/all_gather | solution.py:296
  105.8 3.0 fusion.17
  108.8 2.2 multiply_convert_fusion
  117.0 2.0 copy.97
  119.0 1.6 bitcast_add_fusion.2
  124.1 2.0 fusion.15
  126.1 3.8 %collective-permute-done.8 = bf16[1,512,256]{2,1,0:T(8,128)(2,1)S(1)} collective-permute-done((bf16[1,512,256]{2,1,0:T(8,128)(2,1)S(1)}, bf16[1,512,256]{2,1,0:T(8,128)(2,1)S(1)}, u32[]{:S(2)}, u32[]{:S(2)}) %collective-permute-start.8) | collective-permute-done | bytes 262176 | tf_op jit(solution)/shard_map/ppermute | solution.py:255
  129.9 5.2 %collective-permute-done.2 = bf16[1,512,256]{2,1,0:T(8,128)(2,1)S(1)} collective-permute-done((bf16[1,512,256]{2,1,0:T(8,128)(2,1)S(1)}, bf16[1,512,256]{2,1,0:T(8,128)(2,1)S(1)}, u32[]{:S(2)}, u32[]{:S(2)}) %collective-permute-start.2) | collective-permute-done | bytes 262176 | tf_op jit(solution)/shard_map/ppermute | solution.py:255
  136.6 2.0 copy.95
  138.6 2.1 copy.96
  140.7 1.5 multiply_convert_fusion.7
  143.2 1.7 collective-permute-start.13
  145.3 2.0 collective-permute-start.9
  150.3 1.8 collective-permute-start.10
  152.6 5.5 %collective-permute-done.19 = bf16[1,512,256]{2,1,0:T(8,128)(2,1)S(1)} collective-permute-done((bf16[1,512,256]{2,1,0:T(8,128)(2,1)S(1)}, bf16[1,512,256]{2,1,0:T(8,128)(2,1)S(1)}, u32[]{:S(2)}, u32[]{:S(2)}) %collective-permute-start.19) | collective-permute-done | bytes 262176 | tf_op jit(solution)/shard_map/ppermute | solution.py:267
  158.4 5.3 %collective-permute-done.4 = bf16[1,2,128,512]{3,2,1,0:T(8,128)(2,1)S(1)} collective-permute-done((bf16[1,2,128,512]{3,2,1,0:T(8,128)(2,1)S(1)}, bf16[1,2,128,512]{3,2,1,0:T(8,128)(2,1)S(1)}, u32[]{:S(2)}, u32[]{:S(2)}) %collective-permute-start.4) | collective-permute-done | bytes 262176 | tf_op jit(solution)/shard_map/ppermute | solution.py:267
  164.6 3.5 collective-permute-done.10
  173.6 1.6 collective-permute-start.15
  185.1 13.0 %collective-permute-done.15 = bf16[16,112,256]{2,1,0:T(8,128)(2,1)} collective-permute-done((bf16[16,112,256]{2,1,0:T(8,128)(2,1)}, bf16[16,112,256]{2,1,0:T(8,128)(2,1)}, u32[]{:S(2)}, u32[]{:S(2)}) %collective-permute-start.15) | collective-permute-done | bytes 917536 | tf_op jit(solution)/shard_map/ppermute | solution.py:242
  198.1 3.6 %maximum_select_fusion = bf16[2,16,112,256]{3,2,1,0:T(8,128)(2,1)} fusion(bf16[1,16,112,256]{3,2,1,0:T(8,128)(2,1)} %bitcast.75, bf16[1,16,112,256]{3,2,1,0:T(8,128)(2,1)} %get-tuple-element.69, pred[]{:T(512)S(6)} %eq.8), kind=kLoop, calls=%fused_computation.54 | loop fusion | flops 2752512 | bytes 3670017 | tf_op jit(solution)/shard_map/jit(_where)/select_n | solution.py:243
  201.7 27.1 %depth_gradients.2 = (bf16[32,64,1024]{2,1,0:T(8,128)(2,1)}, f32[9,1024]{1,0:T(8,128)}) custom-call(s32[4]{0:T(128)} %get-tuple-element.96.refs_0_, bf16[32,112,256]{2,1,0:T(8,128)(2,1)} %bitcast.266, bf16[1024,256]{1,0:T(8,128)(2,1)} %bitcast.300, bf16[9,1024]{1,0:T(8,128)(2,1)} %bitcast.322, bf16[32,64,1024]{2,1,0:T(8,128)(2,1)} %get-tuple-element.19.refs_4_), custom_call_target="tpu_custom_call" | custom-call | flops 1879048192 | bytes 16777216 | tf_op jit(solution)/shard_map/depth_gradients/pallas_call | solution.py:187
  228.8 3.2 dynamic-slice_bitcast_fusion.1
  232.0 3.0 maximum_select_fusion.1
  235.0 27.0 %depth_gradients.3 = (bf16[32,64,1024]{2,1,0:T(8,128)(2,1)}, f32[9,1024]{1,0:T(8,128)}) custom-call(s32[4]{0:T(128)} %get-tuple-element.95.refs_0_, bf16[32,112,256]{2,1,0:T(8,128)(2,1)} %bitcast.261, bf16[1024,256]{1,0:T(8,128)(2,1)} %bitcast.301, bf16[9,1024]{1,0:T(8,128)(2,1)} %bitcast.323, bf16[32,64,1024]{2,1,0:T(8,128)(2,1)} %get-tuple-element.21.refs_4_), custom_call_target="tpu_custom_call" | custom-call | flops 1879048192 | bytes 16777216 | tf_op jit(solution)/shard_map/depth_gradients/pallas_call | solution.py:187
  262.1 3.1 dynamic-slice_bitcast_fusion
  267.9 2.1 copy.92
  271.8 1.6 dynamic-slice_bitcast_fusion.2
  273.4 5.3 %fusion.52 = f32[1024,256]{1,0:T(8,128)S(1)} fusion(bf16[3584,1024]{1,0:T(8,128)(2,1)} %bitcast.260, bf16[3584,256]{1,0:T(8,128)(2,1)S(1)} %bitcast.262), kind=kOutput, calls=%fused_computation.158 | convolution fusion | flops 1879048192 | bytes 10223616 | tf_op jit(solution)/shard_map/dot_general | solution.py:341
  278.7 2.7 convert_add_fusion.1
  282.5 4.0 %convert_add_fusion = f32[2,8,64,1024]{3,2,1,0:T(8,128)S(1)} fusion(bf16[2,8,64,1024]{3,2,1,0:T(8,128)(2,1)} %collective-permute-done.22, bf16[2,2,8,64,1024]{4,3,2,1,0:T(8,128)(2,1)S(1)} %bitcast.279, s32[]{:T(128)S(6)} %select_n.288), kind=kLoop, calls=%fused_computation.5 | loop fusion | flops 3145728 | bytes 8388612 | tf_op jit(solution)/shard_map/add | solution.py:256
  289.9 3.1 fusion.19
  293.0 22.9 %psum.21 = f32[1,9,1024]{2,1,0:T(8,128)S(1)} all-reduce(f32[1,9,1024]{2,1,0:T(8,128)S(1)} %multiply_bitcast_fusion), channel_id=1, replica_groups=mesh['section'=4,'dp'=4,'chan'=2] {'dp'}, use_global_device_ids=true, to_apply=%region_0.1 | all-reduce | flops 9216 | bytes 73728 | tf_op jit(solution)/shard_map/psum | solution.py:353
  316.6 2.1 fusion.20
  318.9 10.3 %collective-permute-done.23 = bf16[1,8,64,1024]{3,2,1,0:T(8,128)(2,1)S(1)} collective-permute-done((bf16[1,8,64,1024]{3,2,1,0:T(8,128)(2,1)}, bf16[1,8,64,1024]{3,2,1,0:T(8,128)(2,1)S(1)}, u32[]{:S(2)}, u32[]{:S(2)}) %collective-permute-start.23) | collective-permute-done | bytes 1048608 | tf_op jit(solution)/shard_map/ppermute | solution.py:255
  329.9 1.6 fusion.5
  331.5 1.6 fusion.3
  333.1 2.4 pad_maximum_fusion
  335.4 12.2 %all-reduce.5.cloned.1.call-done = f32[1,1024,256]{2,1,0:T(8,128)} async-done(((f32[1,1024,256]{2,1,0:T(8,128)}), f32[1,1024,256]{2,1,0:T(8,128)}) %all-reduce.5.cloned.1.call-update) | async-done | bytes 1048592 | tf_op jit(solution)/shard_map/psum | solution.py:353
  347.6 2.3 copy.108
  (172 shorter events, 52.4 us)
Async XLA Ops:
  8.0 262.0 %all-reduce.7.cloned.1.call-start = ((), (), s32[]{:S(2)}) async-start(), calls=%async_computation.1 | async-start | bytes 540672 | tf_op jit(solution)/shard_map/psum | solution.py:352
  39.8 65.9 %collective-permute-start = (bf16[1792,256]{1,0:T(8,128)(2,1)}, bf16[1792,256]{1,0:T(8,128)(2,1)}, u32[]{:S(2)}, u32[]{:S(2)}) collective-permute-start(bf16[1792,256]{1,0:T(8,128)(2,1)} %fusion.28), channel_id=1, source_target_pairs={{0,1},{1,0},{2,3},{3,2},{4,5},{5,4},{6,7},{7,6},{8,9},{9,8},{10,11... | collective-permute-start | bytes 2752520 | tf_op jit(solution)/shard_map/ppermute | solution.py:225
  68.5 37.3 %collective-permute-start.6 = (bf16[1792,256]{1,0:T(8,128)(2,1)}, bf16[1792,256]{1,0:T(8,128)(2,1)}, u32[]{:S(2)}, u32[]{:S(2)}) collective-permute-start(bf16[1792,256]{1,0:T(8,128)(2,1)} %fusion.29), channel_id=1, source_target_pairs={{0,1},{1,0},{2,3},{3,2},{4,5},{5,4},{6,7},{7,6},{8,9},{9,8},{10,11... | collective-permute-start | bytes 2752520 | tf_op jit(solution)/shard_map/ppermute | solution.py:225
  74.5 5.2 %copy-start.21 = (f32[128]{0:T(128)S(1)}, f32[128]{0:T(128)}, u32[]{:S(2)}) copy-start(f32[128]{0:T(128)} %param.18) | copy-start | bytes 1540
  74.5 5.2 %copy-start.22 = (f32[1,128]{1,0:T(1,128)S(1)}, f32[1,128]{1,0:T(1,128)}, u32[]{:S(2)}) copy-start(f32[1,128]{1,0:T(1,128)} %param.16) | copy-start | bytes 1540
  75.3 22.4 %copy-start.20 = (s32[2,32,128]{2,1,0:T(8,128)S(1)}, s32[2,32,128]{2,1,0:T(8,128)}, u32[]{:S(2)}) copy-start(s32[2,32,128]{2,1,0:T(8,128)} %param.13) | copy-start | bytes 98308
  75.5 28.2 %collective-permute-start.18 = (bf16[128,512]{1,0:T(8,128)(2,1)S(1)}, bf16[128,512]{1,0:T(8,128)(2,1)S(1)}, u32[]{:S(2)}, u32[]{:S(2)}) collective-permute-start(bf16[128,512]{1,0:T(8,128)(2,1)S(1)} %bitcast.324), channel_id=1, source_target_pairs={{0,1},{1,0},{2,3},{3,2},{4,5},{5,4},{6,7},{7,6},{8,9},{9,8},{10,11... | collective-permute-start | bytes 393224 | tf_op jit(solution)/shard_map/ppermute | solution.py:234
  78.4 26.5 %collective-permute-start.12 = (bf16[128,512]{1,0:T(8,128)(2,1)}, bf16[128,512]{1,0:T(8,128)(2,1)}, u32[]{:S(2)}, u32[]{:S(2)}) collective-permute-start(bf16[128,512]{1,0:T(8,128)(2,1)} %bitcast.59), channel_id=1, source_target_pairs={{0,1},{1,0},{2,3},{3,2},{4,5},{5,4},{6,7},{7,6},{8,9},{9,8},{10,11... | collective-permute-start | bytes 393224 | tf_op jit(solution)/shard_map/ppermute | solution.py:234
  111.0 2.2 copy-start.3
  111.7 1.5 copy-start.17
  112.7 6.4 %collective-permute-start.7 = (bf16[2,512,256]{2,1,0:T(8,128)(2,1)}, bf16[2,512,256]{2,1,0:T(8,128)(2,1)}, u32[]{:S(2)}, u32[]{:S(2)}) collective-permute-start(bf16[2,512,256]{2,1,0:T(8,128)(2,1)} %fusion.31), channel_id=1, source_target_pairs={{0,8},{8,0},{16,24},{24,16},{1,9},{9,1},{17,25},{25,17},{2,10},{10... | collective-permute-start | bytes 1572872 | tf_op jit(solution)/shard_map/ppermute | solution.py:255
  116.1 6.0 %collective-permute-start.1 = (bf16[2,512,256]{2,1,0:T(8,128)(2,1)}, bf16[2,512,256]{2,1,0:T(8,128)(2,1)}, u32[]{:S(2)}, u32[]{:S(2)}) collective-permute-start(bf16[2,512,256]{2,1,0:T(8,128)(2,1)} %fusion.30), channel_id=1, source_target_pairs={{0,8},{8,0},{16,24},{24,16},{1,9},{9,1},{17,25},{25,17},{2,10},{10... | collective-permute-start | bytes 1572872 | tf_op jit(solution)/shard_map/ppermute | solution.py:255
  119.0 3.1 copy-start.16
  120.7 3.4 copy-start.4
  120.7 9.2 %collective-permute-start.8 = (bf16[1,512,256]{2,1,0:T(8,128)(2,1)S(1)}, bf16[1,512,256]{2,1,0:T(8,128)(2,1)S(1)}, u32[]{:S(2)}, u32[]{:S(2)}) collective-permute-start(bf16[1,512,256]{2,1,0:T(8,128)(2,1)S(1)} %dynamic-slice_convert_fusion.5), channel_id=1, source_target_pairs={{0,16},{8,24},{16,0},{24,8},{1,17},{9,25},{17,1},{25,9},{2,18},{10... | collective-permute-start | bytes 786440 | tf_op jit(solution)/shard_map/ppermute | solution.py:255
  123.3 11.8 %copy-start.13 = (f32[256,512]{0,1:T(8,128)S(1)}, f32[256,512]{0,1:T(8,128)}, u32[]{:S(2)}) copy-start(f32[256,512]{0,1:T(8,128)} %copy.98) | copy-start | bytes 1572868
  123.3 11.8 %copy-start.14 = (f32[256,512]{0,1:T(8,128)S(1)}, f32[256,512]{0,1:T(8,128)}, u32[]{:S(2)}) copy-start(f32[256,512]{0,1:T(8,128)} %copy.97) | copy-start | bytes 1572868
  123.3 11.8 %collective-permute-start.2 = (bf16[1,512,256]{2,1,0:T(8,128)(2,1)S(1)}, bf16[1,512,256]{2,1,0:T(8,128)(2,1)S(1)}, u32[]{:S(2)}, u32[]{:S(2)}) collective-permute-start(bf16[1,512,256]{2,1,0:T(8,128)(2,1)S(1)} %dynamic-slice_convert_fusion.6), channel_id=1, source_target_pairs={{0,16},{8,24},{16,0},{24,8},{1,17},{9,25},{17,1},{25,9},{2,18},{10... | collective-permute-start | bytes 786440 | tf_op jit(solution)/shard_map/ppermute | solution.py:255
  142.3 5.6 %collective-permute-start.3 = (bf16[128,512]{1,0:T(8,128)(2,1)S(1)}, bf16[128,512]{1,0:T(8,128)(2,1)S(1)}, u32[]{:S(2)}, u32[]{:S(2)}) collective-permute-start(bf16[128,512]{1,0:T(8,128)(2,1)S(1)} %dynamic-slice_bitcast_fusion.4), channel_id=1, source_target_pairs={{0,1},{1,0},{2,3},{3,2},{4,5},{5,4},{6,7},{7,6},{8,9},{9,8},{10,11... | collective-permute-start | bytes 393224 | tf_op jit(solution)/shard_map/ppermute | solution.py:234
  143.2 9.2 %collective-permute-start.13 = (bf16[1,512,256]{2,1,0:T(8,128)(2,1)S(1)}, bf16[1,512,256]{2,1,0:T(8,128)(2,1)S(1)}, u32[]{:S(2)}, u32[]{:S(2)}) collective-permute-start(bf16[1,512,256]{2,1,0:T(8,128)(2,1)S(1)} %bitcast.295), channel_id=1, source_target_pairs={{0,16},{8,24},{16,0},{24,8},{1,17},{9,25},{17,1},{25,9},{2,18},{10... | collective-permute-start | bytes 786440 | tf_op jit(solution)/shard_map/ppermute | solution.py:267
  145.0 13.1 %collective-permute-start.19 = (bf16[1,512,256]{2,1,0:T(8,128)(2,1)S(1)}, bf16[1,512,256]{2,1,0:T(8,128)(2,1)S(1)}, u32[]{:S(2)}, u32[]{:S(2)}) collective-permute-start(bf16[1,512,256]{2,1,0:T(8,128)(2,1)S(1)} %bitcast.292), channel_id=1, source_target_pairs={{0,16},{8,24},{16,0},{24,8},{1,17},{9,25},{17,1},{25,9},{2,18},{10... | collective-permute-start | bytes 786440 | tf_op jit(solution)/shard_map/ppermute | solution.py:267
  145.3 5.0 %collective-permute-start.9 = (bf16[128,512]{1,0:T(8,128)(2,1)S(1)}, bf16[128,512]{1,0:T(8,128)(2,1)S(1)}, u32[]{:S(2)}, u32[]{:S(2)}) collective-permute-start(bf16[128,512]{1,0:T(8,128)(2,1)S(1)} %dynamic-slice_bitcast_fusion.3), channel_id=1, source_target_pairs={{0,1},{1,0},{2,3},{3,2},{4,5},{5,4},{6,7},{7,6},{8,9},{9,8},{10,11... | collective-permute-start | bytes 393224 | tf_op jit(solution)/shard_map/ppermute | solution.py:234
  147.9 15.8 %collective-permute-start.4 = (bf16[1,2,128,512]{3,2,1,0:T(8,128)(2,1)S(1)}, bf16[1,2,128,512]{3,2,1,0:T(8,128)(2,1)S(1)}, u32[]{:S(2)}, u32[]{:S(2)}) collective-permute-start(bf16[1,2,128,512]{3,2,1,0:T(8,128)(2,1)S(1)} %bitcast.289), channel_id=1, source_target_pairs={{0,16},{8,24},{16,0},{24,8},{1,17},{9,25},{17,1},{25,9},{2,18},{10... | collective-permute-start | bytes 786440 | tf_op jit(solution)/shard_map/ppermute | solution.py:267
  150.3 17.7 %collective-permute-start.10 = (bf16[1,2,128,512]{3,2,1,0:T(8,128)(2,1)S(1)}, bf16[1,2,128,512]{3,2,1,0:T(8,128)(2,1)S(1)}, u32[]{:S(2)}, u32[]{:S(2)}) collective-permute-start(bf16[1,2,128,512]{3,2,1,0:T(8,128)(2,1)S(1)} %bitcast.285), channel_id=1, source_target_pairs={{0,16},{8,24},{16,0},{24,8},{1,17},{9,25},{17,1},{25,9},{2,18},{10... | collective-permute-start | bytes 786440 | tf_op jit(solution)/shard_map/ppermute | solution.py:267
  152.5 16.5 %collective-permute-start.14 = (bf16[2,512,256]{2,1,0:T(8,128)(2,1)S(1)}, bf16[2,512,256]{2,1,0:T(8,128)(2,1)S(1)}, u32[]{:S(2)}, u32[]{:S(2)}) collective-permute-start(bf16[2,512,256]{2,1,0:T(8,128)(2,1)S(1)} %maximum_select_fusion.10), channel_id=1, source_target_pairs={{0,8},{8,0},{16,24},{24,16},{1,9},{9,1},{17,25},{25,17},{2,10},{10... | collective-permute-start | bytes 1572872 | tf_op jit(solution)/shard_map/ppermute | solution.py:267
  158.1 11.4 %collective-permute-start.20 = (bf16[2,512,256]{2,1,0:T(8,128)(2,1)S(1)}, bf16[2,512,256]{2,1,0:T(8,128)(2,1)S(1)}, u32[]{:S(2)}, u32[]{:S(2)}) collective-permute-start(bf16[2,512,256]{2,1,0:T(8,128)(2,1)S(1)} %maximum_select_fusion.11), channel_id=1, source_target_pairs={{0,8},{8,0},{16,24},{24,16},{1,9},{9,1},{17,25},{25,17},{2,10},{10... | collective-permute-start | bytes 1572872 | tf_op jit(solution)/shard_map/ppermute | solution.py:267
  164.6 14.5 %collective-permute-start.5 = (bf16[2,2,128,512]{3,2,1,0:T(8,128)(2,1)}, bf16[2,2,128,512]{3,2,1,0:T(8,128)(2,1)}, u32[]{:S(2)}, u32[]{:S(2)}) collective-permute-start(bf16[2,2,128,512]{3,2,1,0:T(8,128)(2,1)} %maximum_select_fusion.7), channel_id=1, source_target_pairs={{0,8},{8,0},{16,24},{24,16},{1,9},{9,1},{17,25},{25,17},{2,10},{10... | collective-permute-start | bytes 1572872 | tf_op jit(solution)/shard_map/ppermute | solution.py:267
  168.9 14.1 %collective-permute-start.11 = (bf16[2,2,128,512]{3,2,1,0:T(8,128)(2,1)}, bf16[2,2,128,512]{3,2,1,0:T(8,128)(2,1)}, u32[]{:S(2)}, u32[]{:S(2)}) collective-permute-start(bf16[2,2,128,512]{3,2,1,0:T(8,128)(2,1)} %maximum_select_fusion.8), channel_id=1, source_target_pairs={{0,8},{8,0},{16,24},{24,16},{1,9},{9,1},{17,25},{25,17},{2,10},{10... | collective-permute-start | bytes 1572872 | tf_op jit(solution)/shard_map/ppermute | solution.py:267
  170.0 1.7 copy-start.5
  173.6 24.5 %collective-permute-start.15 = (bf16[16,112,256]{2,1,0:T(8,128)(2,1)}, bf16[16,112,256]{2,1,0:T(8,128)(2,1)}, u32[]{:S(2)}, u32[]{:S(2)}) collective-permute-start(bf16[16,112,256]{2,1,0:T(8,128)(2,1)} %get-tuple-element.70), channel_id=1, source_target_pairs={{0,1},{1,0},{2,3},{3,2},{4,5},{5,4},{6,7},{7,6},{8,9},{9,8},{10,11... | collective-permute-start | bytes 2752520 | tf_op jit(solution)/shard_map/ppermute | solution.py:242
  177.1 170.4 %all-reduce.5.cloned.1.call-start = ((), (), s32[]{:S(2)}) async-start(), calls=%async_computation | async-start | bytes 2097152 | tf_op jit(solution)/shard_map/psum | solution.py:353
  178.7 53.3 %collective-permute-start.21 = (bf16[16,112,256]{2,1,0:T(8,128)(2,1)}, bf16[16,112,256]{2,1,0:T(8,128)(2,1)}, u32[]{:S(2)}, u32[]{:S(2)}) collective-permute-start(bf16[16,112,256]{2,1,0:T(8,128)(2,1)} %get-tuple-element.72), channel_id=1, source_target_pairs={{0,1},{1,0},{2,3},{3,2},{4,5},{5,4},{6,7},{7,6},{8,9},{9,8},{10,11... | collective-permute-start | bytes 2752520 | tf_op jit(solution)/shard_map/ppermute | solution.py:242
  228.8 3.2 copy-start.11
  232.0 46.7 %collective-permute-start.16 = (bf16[2,8,64,1024]{3,2,1,0:T(8,128)(2,1)}, bf16[2,8,64,1024]{3,2,1,0:T(8,128)(2,1)}, u32[]{:S(2)}, u32[]{:S(2)}) collective-permute-start(bf16[2,8,64,1024]{3,2,1,0:T(8,128)(2,1)} %dynamic-slice_bitcast_fusion.1), channel_id=1, source_target_pairs={{0,8},{8,0},{16,24},{24,16},{1,9},{9,1},{17,25},{25,17},{2,10},{10... | collective-permute-start | bytes 6291464 | tf_op jit(solution)/shard_map/ppermute | solution.py:255
  265.2 17.3 %collective-permute-start.22 = (bf16[2,8,64,1024]{3,2,1,0:T(8,128)(2,1)}, bf16[2,8,64,1024]{3,2,1,0:T(8,128)(2,1)}, u32[]{:S(2)}, u32[]{:S(2)}) collective-permute-start(bf16[2,8,64,1024]{3,2,1,0:T(8,128)(2,1)} %dynamic-slice_bitcast_fusion), channel_id=1, source_target_pairs={{0,8},{8,0},{16,24},{24,16},{1,9},{9,1},{17,25},{25,17},{2,10},{10... | collective-permute-start | bytes 6291464 | tf_op jit(solution)/shard_map/ppermute | solution.py:255
  267.9 5.4 %copy-start.6 = (bf16[2,16,112,256]{3,2,1,0:T(8,128)(2,1)S(1)}, bf16[2,16,112,256]{3,2,1,0:T(8,128)(2,1)}, u32[]{:S(2)}) copy-start(bf16[2,16,112,256]{3,2,1,0:T(8,128)(2,1)} %maximum_select_fusion.1) | copy-start | bytes 5505028
  273.4 5.3 %copy-start.9 = (bf16[32,64,1024]{2,1,0:T(8,128)(2,1)S(1)}, bf16[32,64,1024]{2,1,0:T(8,128)(2,1)}, u32[]{:S(2)}) copy-start(bf16[32,64,1024]{2,1,0:T(8,128)(2,1)} %get-tuple-element.20) | copy-start | bytes 12582916
  278.7 3.8 %copy-start.10 = (bf16[32,64,1024]{2,1,0:T(8,128)(2,1)S(1)}, bf16[32,64,1024]{2,1,0:T(8,128)(2,1)}, u32[]{:S(2)}) copy-start(bf16[32,64,1024]{2,1,0:T(8,128)(2,1)} %get-tuple-element.22) | copy-start | bytes 12582916
  278.7 11.1 %slice-start = ((s8[7340032]{0:T(1024)(128)(4,1)}), s8[4194304]{0:T(1024)(128)(4,1)S(1)}, s32[]{:S(2)}) async-start(s8[7340032]{0:T(1024)(128)(4,1)} %bitcast.263), calls=%async_computation.2 | async-start | bytes 8388608
  281.4 5.1 %copy-start = (f32[2,8,64,1024]{3,2,1,0:T(8,128)}, f32[2,8,64,1024]{3,2,1,0:T(8,128)S(1)}, u32[]{:S(2)}) copy-start(f32[2,8,64,1024]{3,2,1,0:T(8,128)S(1)} %convert_add_fusion.1) | copy-start | bytes 12582916
  281.6 8.2 %slice-start.1 = ((s8[7340032]{0:T(1024)(128)(4,1)}), s8[3145728]{0:T(1024)(128)(4,1)S(1)}, s32[]{:S(2)}) async-start(s8[7340032]{0:T(1024)(128)(4,1)} %bitcast.263), calls=%async_computation.3 | async-start | bytes 6291456
  281.6 35.0 %collective-permute-start.17 = (bf16[1,8,64,1024]{3,2,1,0:T(8,128)(2,1)S(1)}, bf16[1,8,64,1024]{3,2,1,0:T(8,128)(2,1)S(1)}, u32[]{:S(2)}, u32[]{:S(2)}) collective-permute-start(bf16[1,8,64,1024]{3,2,1,0:T(8,128)(2,1)S(1)} %dynamic-slice_convert_fusion.1), channel_id=1, source_target_pairs={{0,16},{8,24},{16,0},{24,8},{1,17},{9,25},{17,1},{25,9},{2,18},{10... | collective-permute-start | bytes 3145736 | tf_op jit(solution)/shard_map/ppermute | solution.py:255
  286.5 2.4 copy-start.1
  286.5 3.3 copy-start.7
  288.9 40.3 %collective-permute-start.23 = (bf16[1,8,64,1024]{3,2,1,0:T(8,128)(2,1)}, bf16[1,8,64,1024]{3,2,1,0:T(8,128)(2,1)S(1)}, u32[]{:S(2)}, u32[]{:S(2)}) collective-permute-start(bf16[1,8,64,1024]{3,2,1,0:T(8,128)(2,1)} %dynamic-slice_convert_fusion), channel_id=1, source_target_pairs={{0,16},{8,24},{16,0},{24,8},{1,17},{9,25},{17,1},{25,9},{2,18},{10... | collective-permute-start | bytes 3145736 | tf_op jit(solution)/shard_map/ppermute | solution.py:255
  289.8 3.1 copy-start.18
  289.9 3.1 copy-start.19
  316.6 12.6 %copy-start.2 = (f32[2,8,64,1024]{3,2,1,0:T(8,128)S(1)}, f32[2,8,64,1024]{3,2,1,0:T(8,128)}, u32[]{:S(2)}) copy-start(f32[2,8,64,1024]{3,2,1,0:T(8,128)} %copy-done.1) | copy-start | bytes 12582916
  (3 other events, 3.5 us)
Sparse Core Ops, SparseCore 0:
  177.3 71.7 all-reduce.6
Sparse Core Ops, SparseCore 1:
  293.1 54.4 all-reduce.4

commit v2 on v1

--- a/solution.py
+++ b/solution.py
@@ -28,7 +28,12 @@
     return lower, upper
 
 
-def forward_kernel(scal, feats, taps, weight, depth, band, pre, masked, doubled, left, right, *, margin, wing):
+def tap_rows(taps, g):
+    kernel = taps[:, g * LANES:(g + 1) * LANES].astype(jnp.float32)
+    return [jnp.broadcast_to(kernel[t:t + 1], (8, LANES))[None] for t in range(9)]
+
+
+def forward_kernel(scal, feats, taps, weight, depth, band, pre, masked, doubled, left, middle, right, edges, *, margin, wing, batch):
     rows, cols, chans = feats.shape[1:]
     ext = depth.shape[1]
     off, width, rate = scal[0], scal[1], scal[2]
@@ -38,46 +43,56 @@
     def _():
         masked[...] = jnp.zeros_like(masked)
         left[...] = jnp.zeros_like(left)
+        middle[...] = jnp.zeros_like(middle)
         right[...] = jnp.zeros_like(right)
         pre[...] = jnp.zeros_like(pre)
-
-    inside = (lax.broadcasted_iota(jnp.int32, (BAND, LANES), 0) < width).astype(jnp.float32)
-
-    def fill(h, carry):
-        for g, lanes in enumerate(groups):
-            row = feats[0, h, :, lanes].astype(jnp.float32)
-            doubled[g, 0:cols] = row
-            doubled[g, cols:cols + BAND] = row[0:BAND]
-            part = doubled[g, pl.ds(off, BAND)] * inside
-            masked[margin + h, :, lanes] = part
-            band[h, :, lanes] = part.astype(jnp.bfloat16)
+        lower, upper = column_masks(off - wing, rate, ext, cols)
+        edges[0] = lower
+        edges[1] = upper
+
+    def fill(i, carry):
+        for k in range(batch):
+            for g, lanes in enumerate(groups):
+                row = feats[0, i * batch + k, :, lanes].astype(jnp.float32)
+                doubled[k, g, 0:cols] = row
+                doubled[k, g, cols:cols + BAND] = row[0:BAND]
+        inside = (lax.broadcasted_iota(jnp.int32, (BAND, LANES), 0) < width).astype(jnp.float32)
+        for k in range(batch):
+            h = i * batch + k
+            for g, lanes in enumerate(groups):
+                part = doubled[k, g, pl.ds(off, BAND)] * inside
+                masked[g, margin + h] = part
+                band[h, :, lanes] = part.astype(jnp.bfloat16)
         return carry
 
-    lax.fori_loop(0, rows, fill, 0)
-
-    lower, upper = column_masks(off - wing, rate, ext, cols)
-    kernel = taps[...].astype(jnp.float32)
-    batch = 4 if rows % 4 == 0 else 1
+    lax.fori_loop(0, rows // batch, fill, 0)
+    kernels = [tap_rows(taps, g) for g in range(len(groups))]
 
     def row_group(i, carry):
         for k in range(batch):
             h = i * batch + k
-            for g in range(chans // LANES):
-                lanes = groups[g]
-                sources = [masked[h + margin + (t - 1) * rate, :, lanes] for t in range(3)]
-                sums = []
-                for j in range(3):
-                    total = sources[0] * kernel[j:j + 1, g * LANES:(g + 1) * LANES]
-                    for t in (1, 2):
-                        total = total + sources[t] * kernel[3 * t + j:3 * t + j + 1, g * LANES:(g + 1) * LANES]
-                    sums.append(total)
-                left[k, g, 2 * wing:2 * wing + BAND] = sums[0]
-                right[k, g, wing:wing + BAND] = sums[2]
-                from_left = left[k, g, pl.ds(wing - rate, ext)] * lower
-                from_right = right[k, g, pl.ds(rate, ext)] * upper
-                wings = jnp.zeros((wing, LANES), jnp.float32)
-                middle = jnp.concatenate([wings, sums[1], wings], axis=0)
-                depth[h, :, lanes] = (from_left + from_right + middle).astype(jnp.bfloat16)
+            for g in range(len(groups)):
+                for u in range(0, BAND, 16):
+                    sources = [
+                        masked[g, h + margin + (t - 1) * rate, u:u + 16].reshape(2, 8, LANES) for t in range(3)
+                    ]
+                    sums = []
+                    for j in range(3):
+                        total = sources[0] * kernels[g][j]
+                        for t in (1, 2):
+                            total = total + sources[t] * kernels[g][3 * t + j]
+                        sums.append(total.reshape(16, LANES))
+                    left[k, g, 2 * wing + u:2 * wing + u + 16] = sums[0]
+                    middle[k, g, wing + u:wing + u + 16] = sums[1]
+                    right[k, g, wing + u:wing + u + 16] = sums[2]
+        for k in range(batch):
+            h = i * batch + k
+            for g, lanes in enumerate(groups):
+                for e in range(0, ext, 16):
+                    from_left = left[k, g, pl.ds(wing - rate + e, 16)] * edges[0, e:e + 16]
+                    from_right = right[k, g, pl.ds(rate + e, 16)] * edges[1, e:e + 16]
+                    out = from_left + from_right + middle[k, g, e:e + 16]
+                    depth[h, e:e + 16, lanes] = out.astype(jnp.bfloat16)
         some = depth[pl.ds(i * batch, batch)].reshape(batch * ext, chans)
         here = pl.ds(pl.multiple_of(i * batch * ext, 16), batch * ext)
         pre[here, :] += jnp.dot(some, weight[...], preferred_element_type=jnp.float32)
@@ -92,8 +107,10 @@
     block = min(256, chans)
     outs = weight.shape[1]
     buffer = 3 * wing + BAND
+    batch = 4 if rows % 4 == 0 else 1
+    lanes = block // LANES
     return pl.pallas_call(
-        lambda *refs: forward_kernel(*refs, margin=margin, wing=wing),
+        lambda *refs: forward_kernel(*refs, margin=margin, wing=wing, batch=batch),
         grid_spec=pltpu.PrefetchScalarGridSpec(
             num_scalar_prefetch=1,
             grid=(chans // block,),
@@ -108,10 +125,12 @@
                 pl.BlockSpec((rows * ext, outs), lambda c, s: (0, 0)),
             ],
             scratch_shapes=[
-                pltpu.VMEM((rows + 2 * margin, BAND, block), jnp.float32),
-                pltpu.VMEM((block // LANES, cols + BAND, LANES), jnp.float32),
-                pltpu.VMEM((4, block // LANES, buffer, LANES), jnp.float32),
-                pltpu.VMEM((4, block // LANES, buffer, LANES), jnp.float32),
+                pltpu.VMEM((lanes, rows + 2 * margin, BAND, LANES), jnp.float32),
+                pltpu.VMEM((batch, lanes, cols + BAND, LANES), jnp.float32),
+                pltpu.VMEM((batch, lanes, buffer, LANES), jnp.float32),
+                pltpu.VMEM((batch, lanes, ext, LANES), jnp.float32),
+                pltpu.VMEM((batch, lanes, buffer, LANES), jnp.float32),
+                pltpu.VMEM((2, ext, LANES), jnp.float32),
             ],
         ),
         out_shape=[
@@ -127,7 +146,7 @@
     )(scal, feats, taps, weight)
 
 
-def backward_kernel(scal, grad, weight, taps, band, term, dw, spread, *, margin, wing):
+def backward_kernel(scal, grad, weight, taps, band, term, dw, spread, valid, *, margin, wing):
     rows, ext, outs = grad.shape
     chans = weight.shape[0]
     cols = scal[3]
@@ -137,6 +156,11 @@
     @pl.when(pl.program_id(0) == 0)
     def _():
         spread[...] = jnp.zeros_like(spread)
+        lower, upper = column_masks(off, rate, BAND, cols)
+        inside = (lax.broadcasted_iota(jnp.int32, (BAND, LANES), 0) < width).astype(jnp.float32)
+        valid[0] = upper * inside
+        valid[1] = inside
+        valid[2] = lower * inside
 
     def product(i, carry):
         some = grad[pl.ds(i * batch, batch)].reshape(batch * ext, outs)
@@ -148,42 +172,41 @@
 
     lax.fori_loop(0, rows // batch, product, 0)
 
-    lower, upper = column_masks(off, rate, BAND, cols)
-    inside = (lax.broadcasted_iota(jnp.int32, (BAND, LANES), 0) < width).astype(jnp.float32)
-    kernel = taps[...].astype(jnp.float32)
-    valid = (upper * inside, inside, lower * inside)
-
     for g in range(chans // LANES):
         lanes = pl.ds(g * LANES, LANES)
+        kernel = tap_rows(taps, g)
 
         def one_row(h, sums):
-            here = band[h, :, lanes].astype(jnp.float32)
-            total = None
-            new = []
-            for j in range(3):
-                source = here * valid[j] if j != 1 else here
-                part = None
-                for t in range(3):
-                    value = spread[g, h + margin - (t - 1) * rate, pl.ds(wing - (j - 1) * rate, BAND)]
-                    new.append(sums[3 * j + t] + (source * value).reshape(BAND // 8, 8, LANES).sum(axis=0))
-                    scaled = value * kernel[3 * t + j:3 * t + j + 1, g * LANES:(g + 1) * LANES]
-                    part = scaled if part is None else part + scaled
-                part = part * valid[j]
-                total = part if total is None else total + part
-            term[h, :, lanes] = total.astype(jnp.bfloat16)
-            return tuple(new)
-
-        start = tuple(jnp.zeros((8, LANES), jnp.float32) for _ in range(9))
-        sums = lax.fori_loop(0, rows, one_row, start)
-        for t in range(3):
-            for j in range(3):
-                dw[3 * t + j:3 * t + j + 1, lanes] = jnp.sum(sums[3 * j + t], axis=0, keepdims=True)
-
-
-def backward_call(scal, grad, weight, taps, band, margin, wing):
+            sums = list(sums)
+            for u in range(0, BAND, 16):
+                here = band[h, u:u + 16, lanes].astype(jnp.float32).reshape(2, 8, LANES)
+                total = None
+                for j in range(3):
+                    mask = valid[j, u:u + 16].reshape(2, 8, LANES)
+                    source = here * mask if j != 1 else here
+                    part = None
+                    for t in range(3):
+                        value = spread[g, h + margin - (t - 1) * rate, pl.ds(wing - (j - 1) * rate + u, 16)]
+                        value = value.reshape(2, 8, LANES)
+                        both = source * value
+                        sums[3 * t + j] = sums[3 * t + j] + (both[0] + both[1])
+                        scaled = value * kernel[3 * t + j]
+                        part = scaled if part is None else part + scaled
+                    part = part * mask
+                    total = part if total is None else total + part
+                term[h, u:u + 16, lanes] = total.reshape(16, LANES).astype(jnp.bfloat16)
+            return tuple(sums)
+
+        sums = lax.fori_loop(0, rows, one_row, tuple(jnp.zeros((8, LANES), jnp.float32) for _ in range(9)))
+        for t in range(9):
+            dw[t:t + 1, lanes] = jnp.sum(sums[t], axis=0, keepdims=True)
+
+
+def backward_call(scal, grad, weight, taps, band, margin, wing, cut, cuts):
     rows, ext, outs = grad.shape
-    chans = weight.shape[0]
+    chans = weight.shape[0] // cuts
     block = min(256, chans)
+    first = cut * (chans // block)
     return pl.pallas_call(
         lambda *refs: backward_kernel(*refs, margin=margin, wing=wing),
         grid_spec=pltpu.PrefetchScalarGridSpec(
@@ -191,15 +214,18 @@
             grid=(chans // block,),
             in_specs=[
                 pl.BlockSpec((rows, ext, outs), lambda c, s: (0, 0, 0)),
-                pl.BlockSpec((block, outs), lambda c, s: (c, 0)),
-                pl.BlockSpec((9, block), lambda c, s: (0, c)),
-                pl.BlockSpec((rows, BAND, block), lambda c, s: (0, 0, c)),
+                pl.BlockSpec((block, outs), lambda c, s: (first + c, 0)),
+                pl.BlockSpec((9, block), lambda c, s: (0, first + c)),
+                pl.BlockSpec((rows, BAND, block), lambda c, s: (0, 0, first + c)),
             ],
             out_specs=[
                 pl.BlockSpec((rows, BAND, block), lambda c, s: (0, 0, c)),
                 pl.BlockSpec((9, block), lambda c, s: (0, c)),
             ],
-            scratch_shapes=[pltpu.VMEM((block // LANES, rows + 2 * margin, ext, LANES), jnp.float32)],
+            scratch_shapes=[
+                pltpu.VMEM((block // LANES, rows + 2 * margin, ext, LANES), jnp.float32),
+                pltpu.VMEM((3, BAND, LANES), jnp.float32),
+            ],
         ),
         out_shape=[
             jax.ShapeDtypeStruct((rows, BAND, chans), jnp.bfloat16),
@@ -270,6 +296,14 @@
         block = both.reshape((2 * block.shape[0],) + shape)
         bit //= 2
     return block
+
+
+def butterfly_sum(value, axis):
+    size, bit = lax.axis_size(axis), 1
+    while bit < size:
+        value = value + lax.ppermute(value, axis, [(i, i ^ bit) for i in range(size)])
+        bit *= 2
+    return value
 
 
 def rolled(array, start, axis):
@@ -293,9 +327,9 @@
     piece = pixels // sections
     taps, weight = dw_kernel[0], pw_weight[0]
 
-    proj_all = lax.all_gather(proj[0], "chan", axis=0, tiled=True)
-    biases = lax.all_gather(jnp.stack([pw_bias[0], proj_bias]), "chan", axis=1, tiled=True)
-    pw_bias_all, proj_bias_all = biases[0], biases[1]
+    proj_all = gather(proj[0], "chan").reshape(branch, branch)
+    biases = gather(jnp.stack([pw_bias[0], proj_bias]), "chan")
+    pw_bias_all, proj_bias_all = biases[:, 0].reshape(branch), biases[:, 1].reshape(branch)
 
     starts = [lax.rem(offsets[f] + (cols - wing), cols) for f in range(frames)]
     scals = [jnp.stack([offsets[f], widths[f], rate, jnp.int32(cols)]) for f in range(frames)]
@@ -310,8 +344,8 @@
 
     firsts = [forward_call(scals[f], feats, taps, weight, f, margin, wing) for f in range(frames)]
 
-    results, terms = [], []
-    dw_sum = pw_sum = proj_sum = pw_bias_sum = proj_bias_sum = 0.0
+    kept, grads, outs = [], [], []
+    proj_sum = pw_bias_sum = proj_bias_sum = 0.0
     for f in range(frames):
         depth, band, pre = firsts[f]
         own = owner_sum(pre.reshape(parts, rows_own * ext, branch), "chan") + pw_bias_all
@@ -320,26 +354,21 @@
         act = jax.nn.silu(preact).astype(jnp.bfloat16)
         zpart = jnp.dot(act, proj_all, preferred_element_type=jnp.float32)
         zvalue = halving_sum(zpart.reshape(sections, piece, branch), "section") + proj_bias_all
-        result = jax.nn.silu(zvalue).astype(jnp.bfloat16)
+        outs.append(jax.nn.silu(zvalue).astype(jnp.bfloat16))
         out_grad = ups[f].astype(jnp.float32) * swish_slope(zvalue) * labeled[f][:, None]
         out_grad = doubling_gather(out_grad.astype(jnp.bfloat16), "section").reshape(pixels, branch)
-
         act_grad = lax.dot_general(out_grad, proj_all, (((1,), (1,)), ((), ())), preferred_element_type=jnp.float32)
         pre_grad = (act_grad * swish_slope(preact)).astype(jnp.bfloat16)
         sent = pre_grad.reshape(rows_own, cols, branch)[:, :ext]
-        grad_rows = gather(sent, "chan").reshape(rows, ext, branch)
-        term, dw = backward_call(scals[f], grad_rows, weight, taps, band, margin, wing)
-        own_rows = halving_sum(term.reshape(sections, rows // sections, BAND, chans), "section")
-        own_rows = jnp.pad(own_rows.astype(jnp.bfloat16), ((0, 0), (0, cols - BAND), (0, 0)))
-        terms.append(rolled(own_rows, lax.rem(cols - offsets[f], cols), 1))
-
-        swapped = trade(result.reshape(piece, parts, share).transpose(1, 2, 0), "chan")
-        whole = doubling_gather(swapped, "section").transpose(2, 1, 0, 3).reshape(share, rows, cols)
-        results.append(rolled(whole, lax.rem(cols - starts[f], cols), 2))
-
-        dw_sum = dw_sum + dw
+        grads.append(gather(sent, "chan").reshape(rows, ext, branch))
+        kept.append((act, out_grad, pre_grad))
+
+    outs, kept, _ = lax.optimization_barrier((outs, kept, grads[-1]))
+    pw_sum = 0.0
+    for f in range(frames):
+        act, out_grad, pre_grad = kept[f]
         pw_sum = pw_sum + lax.dot_general(
-            depth.reshape(rows * ext, chans), grad_rows.reshape(rows * ext, branch),
+            firsts[f][0].reshape(rows * ext, chans), grads[f].reshape(rows * ext, branch),
             (((0,), (0,)), ((), ())), preferred_element_type=jnp.float32,
         )
         proj_sum = proj_sum + lax.dot_general(
@@ -347,19 +376,43 @@
         )
         pw_bias_sum = pw_bias_sum + jnp.sum(pre_grad.astype(jnp.float32), axis=0)
         proj_bias_sum = proj_bias_sum + jnp.sum(out_grad.astype(jnp.float32), axis=0)
-
-    shared = jnp.concatenate([proj_sum, pw_bias_sum[None], proj_bias_sum[None]], axis=0) * scaling
-    shared = lax.psum(shared, ("chan", "dp"))
-    kernel_grad, weight_grad = lax.psum((dw_sum * scaling, pw_sum * scaling), "dp")
-    mine = part * share
+    proj_rows = owner_sum(proj_sum.reshape(parts, share, branch), "chan")
+    bias_rows = jnp.stack([pw_bias_sum, proj_bias_sum]).reshape(2, parts, share).transpose(1, 0, 2)
+    bias_rows = owner_sum(bias_rows, "chan")
+    bias_rows = jnp.pad(bias_rows, ((0, 6), (0, branch - share)))
+    shared = jnp.concatenate([pw_sum, proj_rows, bias_rows], axis=0) * scaling
+    if frames > 1:
+        grads[-1], shared = lax.optimization_barrier((grads[-1], shared))
+    shared = lax.psum(shared, "dp")
+
+    cuts = 2 if chans % 512 == 0 else 1
+    terms, dw_sums = [], [0.0] * cuts
+    for f in range(frames):
+        band, halves = firsts[f][1], []
+        for cut in range(cuts):
+            term, dw = backward_call(scals[f], grads[f], weight, taps, band, margin, wing, cut, cuts)
+            own_rows = halving_sum(term.reshape(sections, rows // sections, BAND, chans // cuts), "section")
+            halves.append(own_rows.astype(jnp.bfloat16))
+            dw_sums[cut] = dw_sums[cut] + dw
+        own_rows = jnp.pad(jnp.concatenate(halves, axis=2), ((0, 0), (0, cols - BAND), (0, 0)))
+        terms.append(rolled(own_rows, lax.rem(cols - offsets[f], cols), 1))
+    kernel_grad = butterfly_sum(jnp.concatenate(dw_sums, axis=1) * scaling, "dp")
+
+    results = []
+    for f in range(frames):
+        swapped = trade(outs[f].reshape(piece, parts, share).transpose(1, 2, 0), "chan")
+        whole = doubling_gather(swapped, "section").transpose(2, 1, 0, 3).reshape(share, rows, cols)
+        results.append(rolled(whole, lax.rem(cols - starts[f], cols), 2))
+
+    proj_end = chans + share
     return (
         jnp.stack(results, 1),
         jnp.stack(terms, 0),
         kernel_grad[None],
-        weight_grad[None],
-        lax.dynamic_slice_in_dim(shared[branch], mine, share)[None],
-        lax.dynamic_slice_in_dim(shared, mine, share, 0)[None],
-        lax.dynamic_slice_in_dim(shared[branch + 1], mine, share),
+        shared[None, :chans],
+        shared[proj_end:proj_end + 1, :share],
+        shared[None, chans:proj_end],
+        shared[proj_end + 1, :share],
     )
 
 

time: 363 us -> 365 us (level)
  blocking collectives: 46.2 us -> 0 us
  waiting for transfers between devices: 60.8 us -> 93.8 us
  starting transfers between devices: 19.3 us -> 29.8 us
  Pallas kernels: 101 us -> 108 us
    ppermute x2 -> x4, waiting for transfers between devices: 13 us -> 38.6 us  [gather(): got = lax.ppermute(block, axis, [(0, 1), (1, 0)])]
    all_gather x2 -> x0, blocking collectives: 23.3 us -> none  [the longest x1 17.7 us: local(): lax.all_gather(jnp.stack([pw_bias[0], proj_bias]), 'chan', axis=1, tiled=...]
    psum x1 -> x0, blocking collectives: 22.9 us -> none  [local(): lax.psum((dw_sum * scaling, pw_sum * scaling), 'dp')]
    pallas_call x2 -> x4, Pallas kernels: 54.1 us -> 64.6 us  [backward_call(): pl.pallas_call(lambda *refs: backward_kernel(*refs, margin=margin, wing=w...]
    ppermute x0 -> x2, waiting for transfers between devices: none -> 5.74 us  [butterfly_sum(): lax.ppermute(value, axis, [(i, i ^ bit) for i in range(size)])]
    ppermute x8 -> x12, waiting for transfers between devices: 19.3 us -> 24.2 us  [halving_sum(): got = lax.ppermute(sent, axis, [(i, i ^ bit) for i in range(size)])]
    psum x2 -> x1, waiting for transfers between devices: 12.2 us -> 7.4 us  [local(): shared = lax.psum(shared, 'dp')]
    ppermute x0 -> x2, starting transfers between devices: none -> 4.16 us  [butterfly_sum(): lax.ppermute(value, axis, [(i, i ^ bit) for i in range(size)])]
  transfers between devices with their start and end apart: 26 -> 35, of which waited for: 11 -> 13; matrix products, arithmetic and copies ran while one was open for 23% -> 24% of each run, Pallas kernels for 22% -> 30%
where the time goes in v2:
time: 365 us; the launch traced here: 359 us
  Pallas kernels  108 us (30%)
  waiting for transfers between devices  93.8 us (26%)
  other arithmetic  51.1 us (14%)
  local copies, waits for them, and re-layouts  48.8 us (13%)
  starting transfers between devices  29.8 us (8%)
  between operations  18.1 us (5%)
  matrix products  10.1 us (3%)
    pallas_call x4, Pallas kernels, backward_call(): pl.pallas_call(lambda *refs: backward_kernel(*refs, margin=margin, wing=w...  64.6 us
    pallas_call x2, Pallas kernels, forward_call(): pl.pallas_call(lambda *refs: forward_kernel(*refs, margin=margin, wing=wi...  43 us
    ppermute x4, waiting for transfers between devices, gather(): got = lax.ppermute(block, axis, [(0, 1), (1, 0)])  38.6 us
    ppermute x12, waiting for transfers between devices, halving_sum(): got = lax.ppermute(sent, axis, [(i, i ^ bit) for i in range(size)])  24.2 us
    ppermute x8, waiting for transfers between devices, doubling_gather(): got = lax.ppermute(block, axis, [(i, i ^ bit) for i in range(size)])  17.8 us
    unnamed x80, local copies, waits for them, and re-layouts  8.7 us
    ppermute x12, starting transfers between devices, halving_sum(): got = lax.ppermute(sent, axis, [(i, i ^ bit) for i in range(size)])  8.1 us
    add x6, other arithmetic, halving_sum(): blocks = pick(blocks, mine, 1).astype(jnp.float32) + got.astype(jnp.float32)  7.63 us
  transfers between devices with their start and end apart: 35, of which 13 were waited for; matrix products, arithmetic and copies ran while one was open for 24% of the time, Pallas kernels for 30%

profile of v2, /device:TPU:0, one launch (start us, length us, event | category | flops | bytes accessed | tf_op | source)
XLA Modules:
  0.0 359.5 jit_solution(4295544909413020030)
XLA Ops:
  9.9 1.9 fusion.55
  15.6 3.0 collective-permute-start.11
  19.3 3.2 pad_add_fusion
  22.6 21.4 %depth_pointwise.3 = (bf16[32,112,1024]{2,1,0:T(8,128)(2,1)}, bf16[32,64,1024]{2,1,0:T(8,128)(2,1)}, f32[3584,256]{1,0:T(8,128)}) custom-call(s32[4]{0:T(128)} %get-tuple-element.119.refs_0_, bf16[2,32,128,1024]{3,2,1,0:T(8,128)(2,1)} %refs_1_.3, bf16[9,1024]{1,0:T(8,128)(2,1)} %bitcast.361, bf16[1024,256]{1,0:T(8,128)(2,1)} %bitcast.295), custom_call_target="tpu_custom_call" | custom-call | flops 1879048192 | bytes 19922944 | tf_op jit(solution)/shard_map/depth_pointwise/pallas_call | solution.py:112
  44.0 2.5 fusion.32
  46.5 2.0 collective-permute-start.5
  48.5 21.6 %depth_pointwise.2 = (bf16[32,112,1024]{2,1,0:T(8,128)(2,1)}, bf16[32,64,1024]{2,1,0:T(8,128)(2,1)}, f32[3584,256]{1,0:T(8,128)}) custom-call(s32[4]{0:T(128)} %get-tuple-element.120.refs_0_, bf16[2,32,128,1024]{3,2,1,0:T(8,128)(2,1)} %refs_1_.3, bf16[9,1024]{1,0:T(8,128)(2,1)} %bitcast.362, bf16[1024,256]{1,0:T(8,128)(2,1)} %bitcast.296), custom_call_target="tpu_custom_call" | custom-call | flops 1879048192 | bytes 19922944 | tf_op jit(solution)/shard_map/depth_pointwise/pallas_call | solution.py:112
  70.1 2.5 fusion.31
  72.7 2.0 collective-permute-start.2
  76.1 21.4 %collective-permute-done.2 = bf16[128,256]{1,0:T(8,128)(2,1)S(1)} collective-permute-done((bf16[128,256]{1,0:T(8,128)(2,1)S(1)}, bf16[128,256]{1,0:T(8,128)(2,1)S(1)}, u32[]{:S(2)}, u32[]{:S(2)}) %collective-permute-start.2) | collective-permute-done | bytes 65568 | tf_op jit(solution)/shard_map/ppermute | solution.py:268
  97.6 3.0 fusion.24
  100.6 2.5 pad_maximum_fusion.1
  106.4 2.3 collective-permute-start.7
  109.8 1.8 dynamic-slice_convert_fusion.8
  111.6 2.0 copy.103
  114.5 2.0 copy.102
  116.6 4.7 %collective-permute-done.4 = bf16[1,512,256]{2,1,0:T(8,128)(2,1)} collective-permute-done((bf16[1,512,256]{2,1,0:T(8,128)(2,1)}, bf16[1,512,256]{2,1,0:T(8,128)(2,1)}, u32[]{:S(2)}, u32[]{:S(2)}) %collective-permute-start.4) | collective-permute-done | bytes 262176 | tf_op jit(solution)/shard_map/ppermute | solution.py:281
  121.2 2.9 fusion.41
  124.1 1.7 collective-permute-start.9
  126.1 1.8 fusion.23
  127.9 5.4 %collective-permute-done.9 = bf16[1,512,256]{2,1,0:T(8,128)(2,1)S(1)} collective-permute-done((bf16[1,512,256]{2,1,0:T(8,128)(2,1)S(1)}, bf16[1,512,256]{2,1,0:T(8,128)(2,1)S(1)}, u32[]{:S(2)}, u32[]{:S(2)}) %collective-permute-start.9) | collective-permute-done | bytes 262176 | tf_op jit(solution)/shard_map/ppermute | solution.py:293
  133.5 4.0 %collective-permute-done.12 = bf16[1,512,256]{2,1,0:T(8,128)(2,1)S(1)} collective-permute-done((bf16[1,512,256]{2,1,0:T(8,128)(2,1)S(1)}, bf16[1,512,256]{2,1,0:T(8,128)(2,1)S(1)}, u32[]{:S(2)}, u32[]{:S(2)}) %collective-permute-start.12) | collective-permute-done | bytes 262176 | tf_op jit(solution)/shard_map/ppermute | solution.py:293
  137.6 1.8 fusion.17
  148.0 17.2 %collective-permute-done.21 = bf16[16,112,256]{2,1,0:T(8,128)(2,1)} collective-permute-done((bf16[16,112,256]{2,1,0:T(8,128)(2,1)}, bf16[16,112,256]{2,1,0:T(8,128)(2,1)}, u32[]{:S(2)}, u32[]{:S(2)}) %collective-permute-start.21) | collective-permute-done | bytes 917536 | tf_op jit(solution)/shard_map/ppermute | solution.py:268
  165.2 3.0 maximum_select_fusion.1
  168.3 15.8 %depth_gradients.5 = (bf16[32,64,512]{2,1,0:T(8,128)(2,1)}, f32[9,512]{1,0:T(8,128)}) custom-call(s32[4]{0:T(128)} %get-tuple-element.120.refs_0_, bf16[32,112,256]{2,1,0:T(8,128)(2,1)} %bitcast.292, bf16[1024,256]{1,0:T(8,128)(2,1)} %bitcast.297, bf16[9,1024]{1,0:T(8,128)(2,1)} %bitcast.363, bf16[32,64,1024]{2,1,0:T(8,128)(2,1)} %get-tuple-element.35.refs_4_), custom_call_target="tpu_custom_call" | custom-call | flops 939524096 | bytes 8388608 | tf_op jit(solution)/shard_map/depth_gradients/pallas_call | solution.py:210
  184.1 16.5 %depth_gradients.4 = (bf16[32,64,512]{2,1,0:T(8,128)(2,1)}, f32[9,512]{1,0:T(8,128)}) custom-call(s32[4]{0:T(128)} %get-tuple-element.120.refs_0_, bf16[32,112,256]{2,1,0:T(8,128)(2,1)} %bitcast.293, bf16[1024,256]{1,0:T(8,128)(2,1)} %bitcast.298, bf16[9,1024]{1,0:T(8,128)(2,1)} %bitcast.364, bf16[32,64,1024]{2,1,0:T(8,128)(2,1)} %get-tuple-element.35.refs_4_), custom_call_target="tpu_custom_call" | custom-call | flops 939524096 | bytes 8388608 | tf_op jit(solution)/shard_map/depth_gradients/pallas_call | solution.py:210
  201.6 1.7 maximum_select_fusion
  213.4 1.6 collective-permute-start.26
  216.1 5.3 %fusion.61 = f32[1024,256]{1,0:T(8,128)S(1)} fusion(bf16[3584,1024]{1,0:T(8,128)(2,1)} %bitcast.311, bf16[3584,256]{1,0:T(8,128)(2,1)S(1)} %bitcast.289), kind=kOutput, calls=%fused_computation.185 | convolution fusion | flops 1879048192 | bytes 10223616 | tf_op jit(solution)/shard_map/dot_general | solution.py:370
  221.5 2.1 convolution_add_fusion
  226.4 15.8 %depth_gradients.7 = (bf16[32,64,512]{2,1,0:T(8,128)(2,1)}, f32[9,512]{1,0:T(8,128)}) custom-call(s32[4]{0:T(128)} %get-tuple-element.119.refs_0_, bf16[32,112,256]{2,1,0:T(8,128)(2,1)} %bitcast.290, bf16[1024,256]{1,0:T(8,128)(2,1)} %bitcast.299, bf16[9,1024]{1,0:T(8,128)(2,1)} %bitcast.365, bf16[32,64,1024]{2,1,0:T(8,128)(2,1)} %get-tuple-element.47.refs_4_), custom_call_target="tpu_custom_call" | custom-call | flops 939524096 | bytes 8388608 | tf_op jit(solution)/shard_map/depth_gradients/pallas_call | solution.py:210
  242.2 16.4 %depth_gradients.6 = (bf16[32,64,512]{2,1,0:T(8,128)(2,1)}, f32[9,512]{1,0:T(8,128)}) custom-call(s32[4]{0:T(128)} %get-tuple-element.119.refs_0_, bf16[32,112,256]{2,1,0:T(8,128)(2,1)} %bitcast.291, bf16[1024,256]{1,0:T(8,128)(2,1)} %bitcast.300, bf16[9,1024]{1,0:T(8,128)(2,1)} %bitcast.366, bf16[32,64,1024]{2,1,0:T(8,128)(2,1)} %get-tuple-element.47.refs_4_), custom_call_target="tpu_custom_call" | custom-call | flops 939524096 | bytes 8388608 | tf_op jit(solution)/shard_map/depth_gradients/pallas_call | solution.py:210
  267.0 6.5 %collective-permute-done.19 = bf16[1,2,128,512]{3,2,1,0:T(8,128)(2,1)S(1)} collective-permute-done((bf16[1,2,128,512]{3,2,1,0:T(8,128)(2,1)S(1)}, bf16[1,2,128,512]{3,2,1,0:T(8,128)(2,1)S(1)}, u32[]{:S(2)}, u32[]{:S(2)}) %collective-permute-start.19) | collective-permute-done | bytes 262176 | tf_op jit(solution)/shard_map/ppermute | solution.py:293
  273.5 2.6 collective-permute-start.33
  276.2 1.9 collective-permute-done.16
  278.9 5.0 %collective-permute-done.33 = f32[9,1024]{1,0:T(8,128)S(1)} collective-permute-done((f32[9,1024]{1,0:T(8,128)S(1)}, f32[9,1024]{1,0:T(8,128)S(1)}, u32[]{:S(2)}, u32[]{:S(2)}) %collective-permute-start.33) | collective-permute-done | bytes 36896 | tf_op jit(solution)/shard_map/ppermute | solution.py:304
  287.8 1.8 maximum_select_fusion.4
  294.2 2.1 copy.99
  296.3 1.7 convert_add_fusion.2
  299.4 1.6 convert_add_fusion.3
  311.1 7.4 %all-reduce.5.cloned.1.call-done = f32[1160,256]{1,0:T(8,128)} async-done(((f32[1160,256]{1,0:T(8,128)}), f32[1160,256]{1,0:T(8,128)}) %all-reduce.5.cloned.1.call-update) | async-done | bytes 1187856 | tf_op jit(solution)/shard_map/psum | solution.py:386
  321.3 2.4 slice_bitcast_fusion
  326.7 1.6 fusion.9
  328.3 8.0 %collective-permute-done.31 = bf16[1,8,64,512]{3,2,1,0:T(8,128)(2,1)S(1)} collective-permute-done((bf16[1,8,64,512]{3,2,1,0:T(8,128)(2,1)}, bf16[1,8,64,512]{3,2,1,0:T(8,128)(2,1)S(1)}, u32[]{:S(2)}, u32[]{:S(2)}) %collective-permute-start.31) | collective-permute-done | bytes 524320 | tf_op jit(solution)/shard_map/ppermute | solution.py:281
  336.6 10.2 %collective-permute-done.29 = bf16[1,8,64,512]{3,2,1,0:T(8,128)(2,1)} collective-permute-done((bf16[1,8,64,512]{3,2,1,0:T(8,128)(2,1)}, bf16[1,8,64,512]{3,2,1,0:T(8,128)(2,1)}, u32[]{:S(2)}, u32[]{:S(2)}) %collective-permute-start.29) | collective-permute-done | bytes 524320 | tf_op jit(solution)/shard_map/ppermute | solution.py:281
  348.2 1.6 fusion.7
  349.8 2.4 pad_maximum_fusion
  (232 shorter events, 71.5 us)
Async XLA Ops:
  7.2 311.3 %all-reduce.5.cloned.1.call-start = ((), (), s32[]{:S(2)}) async-start(), calls=%async_computation | async-start | bytes 2375680 | tf_op jit(solution)/shard_map/psum | solution.py:386
  15.6 81.9 %collective-permute-start.11 = (bf16[128,512]{1,0:T(8,128)(2,1)S(1)}, bf16[128,512]{1,0:T(8,128)(2,1)S(1)}, u32[]{:S(2)}, u32[]{:S(2)}) collective-permute-start(bf16[128,512]{1,0:T(8,128)(2,1)S(1)} %bitcast.380), channel_id=1, source_target_pairs={{0,1},{1,0},{2,3},{3,2},{4,5},{5,4},{6,7},{7,6},{8,9},{9,8},{10,11... | collective-permute-start | bytes 393224 | tf_op jit(solution)/shard_map/ppermute | solution.py:260
  18.6 57.4 %collective-permute-start.1 = (f32[2,128]{1,0:T(2,128)S(1)}, f32[2,128]{1,0:T(2,128)S(1)}, u32[]{:S(2)}, u32[]{:S(2)}) collective-permute-start(f32[2,128]{1,0:T(2,128)S(1)} %get-tuple-element.114), channel_id=1, source_target_pairs={{0,1},{1,0},{2,3},{3,2},{4,5},{5,4},{6,7},{7,6},{8,9},{9,8},{10,11... | collective-permute-start | bytes 3080 | tf_op jit(solution)/shard_map/ppermute | solution.py:268
  46.5 51.1 %collective-permute-start.5 = (bf16[1792,256]{1,0:T(8,128)(2,1)}, bf16[1792,256]{1,0:T(8,128)(2,1)}, u32[]{:S(2)}, u32[]{:S(2)}) collective-permute-start(bf16[1792,256]{1,0:T(8,128)(2,1)} %fusion.32), channel_id=1, source_target_pairs={{0,1},{1,0},{2,3},{3,2},{4,5},{5,4},{6,7},{7,6},{8,9},{9,8},{10,11... | collective-permute-start | bytes 2752520 | tf_op jit(solution)/shard_map/ppermute | solution.py:251
  48.5 24.2 %copy-start.27 = (bf16[1,128,256]{2,1,0:T(8,128)(2,1)S(1)}, bf16[1,128,256]{2,1,0:T(8,128)(2,1)}, u32[]{:S(2)}) copy-start(bf16[1,128,256]{2,1,0:T(8,128)(2,1)} %param.17) | copy-start | bytes 196612
  48.5 26.2 %copy-start.32 = (s32[2,32,128]{2,1,0:T(8,128)S(1)}, s32[2,32,128]{2,1,0:T(8,128)}, u32[]{:S(2)}) copy-start(s32[2,32,128]{2,1,0:T(8,128)} %param.13) | copy-start | bytes 98308
  72.6 24.9 %collective-permute-start = (bf16[1792,256]{1,0:T(8,128)(2,1)}, bf16[1792,256]{1,0:T(8,128)(2,1)}, u32[]{:S(2)}, u32[]{:S(2)}) collective-permute-start(bf16[1792,256]{1,0:T(8,128)(2,1)} %fusion.31), channel_id=1, source_target_pairs={{0,1},{1,0},{2,3},{3,2},{4,5},{5,4},{6,7},{7,6},{8,9},{9,8},{10,11... | collective-permute-start | bytes 2752520 | tf_op jit(solution)/shard_map/ppermute | solution.py:251
  72.7 24.8 %collective-permute-start.2 = (bf16[128,256]{1,0:T(8,128)(2,1)S(1)}, bf16[128,256]{1,0:T(8,128)(2,1)S(1)}, u32[]{:S(2)}, u32[]{:S(2)}) collective-permute-start(bf16[128,256]{1,0:T(8,128)(2,1)S(1)} %bitcast.381), channel_id=1, source_target_pairs={{0,1},{1,0},{2,3},{3,2},{4,5},{5,4},{6,7},{7,6},{8,9},{9,8},{10,11... | collective-permute-start | bytes 196616 | tf_op jit(solution)/shard_map/ppermute | solution.py:268
  76.0 35.5 %collective-permute-start.8 = (bf16[128,512]{1,0:T(8,128)(2,1)}, bf16[128,512]{1,0:T(8,128)(2,1)S(1)}, u32[]{:S(2)}, u32[]{:S(2)}) collective-permute-start(bf16[128,512]{1,0:T(8,128)(2,1)} %bitcast.38), channel_id=1, source_target_pairs={{0,1},{1,0},{2,3},{3,2},{4,5},{5,4},{6,7},{7,6},{8,9},{9,8},{10,11... | collective-permute-start | bytes 393224 | tf_op jit(solution)/shard_map/ppermute | solution.py:260
  103.5 2.0 collective-permute-start.6
  104.1 4.6 %collective-permute-start.3 = (bf16[2,512,256]{2,1,0:T(8,128)(2,1)S(1)}, bf16[2,512,256]{2,1,0:T(8,128)(2,1)S(1)}, u32[]{:S(2)}, u32[]{:S(2)}) collective-permute-start(bf16[2,512,256]{2,1,0:T(8,128)(2,1)S(1)} %fusion.33), channel_id=1, source_target_pairs={{0,8},{8,0},{16,24},{24,16},{1,9},{9,1},{17,25},{25,17},{2,10},{10... | collective-permute-start | bytes 1572872 | tf_op jit(solution)/shard_map/ppermute | solution.py:281
  106.4 10.2 %collective-permute-start.7 = (bf16[1,512,256]{2,1,0:T(8,128)(2,1)}, bf16[1,512,256]{2,1,0:T(8,128)(2,1)}, u32[]{:S(2)}, u32[]{:S(2)}) collective-permute-start(bf16[1,512,256]{2,1,0:T(8,128)(2,1)} %dynamic-slice_convert_fusion.7), channel_id=1, source_target_pairs={{0,16},{8,24},{16,0},{24,8},{1,17},{9,25},{17,1},{25,9},{2,18},{10... | collective-permute-start | bytes 786440 | tf_op jit(solution)/shard_map/ppermute | solution.py:281
  111.6 9.7 %collective-permute-start.4 = (bf16[1,512,256]{2,1,0:T(8,128)(2,1)}, bf16[1,512,256]{2,1,0:T(8,128)(2,1)}, u32[]{:S(2)}, u32[]{:S(2)}) collective-permute-start(bf16[1,512,256]{2,1,0:T(8,128)(2,1)} %dynamic-slice_convert_fusion.8), channel_id=1, source_target_pairs={{0,16},{8,24},{16,0},{24,8},{1,17},{9,25},{17,1},{25,9},{2,18},{10... | collective-permute-start | bytes 786440 | tf_op jit(solution)/shard_map/ppermute | solution.py:281
  116.6 9.5 %copy-start.6 = (f32[16,128,256]{2,1,0:T(8,128)S(1)}, f32[16,128,256]{2,1,0:T(8,128)}, u32[]{:S(2)}) copy-start(f32[16,128,256]{2,1,0:T(8,128)} %get-tuple-element.104) | copy-start | bytes 6291460
  124.1 9.2 %collective-permute-start.9 = (bf16[1,512,256]{2,1,0:T(8,128)(2,1)S(1)}, bf16[1,512,256]{2,1,0:T(8,128)(2,1)S(1)}, u32[]{:S(2)}, u32[]{:S(2)}) collective-permute-start(bf16[1,512,256]{2,1,0:T(8,128)(2,1)S(1)} %bitcast.342), channel_id=1, source_target_pairs={{0,16},{8,24},{16,0},{24,8},{1,17},{9,25},{17,1},{25,9},{2,18},{10... | collective-permute-start | bytes 786440 | tf_op jit(solution)/shard_map/ppermute | solution.py:293
  125.8 11.7 %collective-permute-start.12 = (bf16[1,512,256]{2,1,0:T(8,128)(2,1)S(1)}, bf16[1,512,256]{2,1,0:T(8,128)(2,1)S(1)}, u32[]{:S(2)}, u32[]{:S(2)}) collective-permute-start(bf16[1,512,256]{2,1,0:T(8,128)(2,1)S(1)} %bitcast.339), channel_id=1, source_target_pairs={{0,16},{8,24},{16,0},{24,8},{1,17},{9,25},{17,1},{25,9},{2,18},{10... | collective-permute-start | bytes 786440 | tf_op jit(solution)/shard_map/ppermute | solution.py:293
  133.4 6.2 %collective-permute-start.10 = (bf16[2,512,256]{2,1,0:T(8,128)(2,1)S(1)}, bf16[2,512,256]{2,1,0:T(8,128)(2,1)S(1)}, u32[]{:S(2)}, u32[]{:S(2)}) collective-permute-start(bf16[2,512,256]{2,1,0:T(8,128)(2,1)S(1)} %maximum_select_fusion.7), channel_id=1, source_target_pairs={{0,8},{8,0},{16,24},{24,16},{1,9},{9,1},{17,25},{25,17},{2,10},{10... | collective-permute-start | bytes 1572872 | tf_op jit(solution)/shard_map/ppermute | solution.py:293
  137.6 2.3 collective-permute-start.13
  141.8 23.5 %collective-permute-start.21 = (bf16[16,112,256]{2,1,0:T(8,128)(2,1)}, bf16[16,112,256]{2,1,0:T(8,128)(2,1)}, u32[]{:S(2)}, u32[]{:S(2)}) collective-permute-start(bf16[16,112,256]{2,1,0:T(8,128)(2,1)} %get-tuple-element.100), channel_id=1, source_target_pairs={{0,1},{1,0},{2,3},{3,2},{4,5},{5,4},{6,7},{7,6},{8,9},{9,8},{10,11... | collective-permute-start | bytes 2752520 | tf_op jit(solution)/shard_map/ppermute | solution.py:268
  145.2 55.5 %collective-permute-start.14 = (bf16[16,112,256]{2,1,0:T(8,128)(2,1)}, bf16[16,112,256]{2,1,0:T(8,128)(2,1)S(1)}, u32[]{:S(2)}, u32[]{:S(2)}) collective-permute-start(bf16[16,112,256]{2,1,0:T(8,128)(2,1)} %get-tuple-element.102), channel_id=1, source_target_pairs={{0,1},{1,0},{2,3},{3,2},{4,5},{5,4},{6,7},{7,6},{8,9},{9,8},{10,11... | collective-permute-start | bytes 2752520 | tf_op jit(solution)/shard_map/ppermute | solution.py:268
  184.1 17.5 %copy-start.15 = (bf16[1,16,112,256]{3,2,1,0:T(8,128)(2,1)S(1)}, bf16[1,16,112,256]{3,2,1,0:T(8,128)(2,1)}, u32[]{:S(2)}) copy-start(bf16[1,16,112,256]{3,2,1,0:T(8,128)(2,1)} %get-tuple-element.101) | copy-start | bytes 2752516
  203.4 12.7 %copy-start = (bf16[2,16,112,256]{3,2,1,0:T(8,128)(2,1)}, bf16[2,16,112,256]{3,2,1,0:T(8,128)(2,1)S(1)}, u32[]{:S(2)}) copy-start(bf16[2,16,112,256]{3,2,1,0:T(8,128)(2,1)S(1)} %maximum_select_fusion) | copy-start | bytes 5505028
  204.4 57.4 %collective-permute-start.18 = (bf16[128,512]{1,0:T(8,128)(2,1)}, bf16[128,512]{1,0:T(8,128)(2,1)}, u32[]{:S(2)}, u32[]{:S(2)}) collective-permute-start(bf16[128,512]{1,0:T(8,128)(2,1)} %dynamic-slice_bitcast_fusion.4), channel_id=1, source_target_pairs={{0,1},{1,0},{2,3},{3,2},{4,5},{5,4},{6,7},{7,6},{8,9},{9,8},{10,11... | collective-permute-start | bytes 393224 | tf_op jit(solution)/shard_map/ppermute | solution.py:260
  206.0 5.5 %copy-start.3 = (bf16[2,2,512,256]{3,2,1,0:T(8,128)(2,1)S(1)}, bf16[2,2,512,256]{3,2,1,0:T(8,128)(2,1)}, u32[]{:S(2)}) copy-start(bf16[2,2,512,256]{3,2,1,0:T(8,128)(2,1)} %copy-done.2) | copy-start | bytes 3145732
  206.6 5.8 %copy-start.13 = (bf16[2048,256]{1,0:T(8,128)(2,1)S(1)}, bf16[2048,256]{1,0:T(8,128)(2,1)}, u32[]{:S(2)}) copy-start(bf16[2048,256]{1,0:T(8,128)(2,1)} %get-tuple-element.40) | copy-start | bytes 3145732
  206.6 57.6 %collective-permute-start.15 = (bf16[128,512]{1,0:T(8,128)(2,1)}, bf16[128,512]{1,0:T(8,128)(2,1)S(1)}, u32[]{:S(2)}, u32[]{:S(2)}) collective-permute-start(bf16[128,512]{1,0:T(8,128)(2,1)} %dynamic-slice_bitcast_fusion.5), channel_id=1, source_target_pairs={{0,1},{1,0},{2,3},{3,2},{4,5},{5,4},{6,7},{7,6},{8,9},{9,8},{10,11... | collective-permute-start | bytes 393224 | tf_op jit(solution)/shard_map/ppermute | solution.py:260
  211.8 12.8 %collective-permute-start.27 = (bf16[2,128]{1,0:T(2,128)(2,1)S(1)}, bf16[2,128]{1,0:T(2,128)(2,1)S(1)}, u32[]{:S(2)}, u32[]{:S(2)}) collective-permute-start(bf16[2,128]{1,0:T(2,128)(2,1)S(1)} %fusion.52), channel_id=1, source_target_pairs={{0,1},{1,0},{2,3},{3,2},{4,5},{5,4},{6,7},{7,6},{8,9},{9,8},{10,11... | collective-permute-start | bytes 1544 | tf_op jit(solution)/shard_map/ppermute | solution.py:251
  212.9 8.5 %slice-start = ((s8[7340032]{0:T(1024)(128)(4,1)}), s8[4194304]{0:T(1024)(128)(4,1)S(1)}, s32[]{:S(2)}) async-start(s8[7340032]{0:T(1024)(128)(4,1)} %bitcast.312), calls=%async_computation.1 | async-start | bytes 8388608
  213.4 11.7 %collective-permute-start.26 = (bf16[128,256]{1,0:T(8,128)(2,1)S(1)}, bf16[128,256]{1,0:T(8,128)(2,1)S(1)}, u32[]{:S(2)}, u32[]{:S(2)}) collective-permute-start(bf16[128,256]{1,0:T(8,128)(2,1)S(1)} %fusion.44), channel_id=1, source_target_pairs={{0,1},{1,0},{2,3},{3,2},{4,5},{5,4},{6,7},{7,6},{8,9},{9,8},{10,11... | collective-permute-start | bytes 196616 | tf_op jit(solution)/shard_map/ppermute | solution.py:251
  216.1 80.2 %collective-permute-start.24 = (bf16[2,8,64,512]{3,2,1,0:T(8,128)(2,1)}, bf16[2,8,64,512]{3,2,1,0:T(8,128)(2,1)}, u32[]{:S(2)}, u32[]{:S(2)}) collective-permute-start(bf16[2,8,64,512]{3,2,1,0:T(8,128)(2,1)} %dynamic-slice_bitcast_fusion.2), channel_id=1, source_target_pairs={{0,8},{8,0},{16,24},{24,16},{1,9},{9,1},{17,25},{25,17},{2,10},{10... | collective-permute-start | bytes 3145736 | tf_op jit(solution)/shard_map/ppermute | solution.py:281
  216.1 5.3 %copy-start.1 = (bf16[2,16,112,256]{3,2,1,0:T(8,128)(2,1)S(1)}, bf16[2,16,112,256]{3,2,1,0:T(8,128)(2,1)}, u32[]{:S(2)}) copy-start(bf16[2,16,112,256]{3,2,1,0:T(8,128)(2,1)} %maximum_select_fusion.1) | copy-start | bytes 5505028
  216.1 5.4 %slice-start.1 = ((s8[7340032]{0:T(1024)(128)(4,1)}), s8[3145728]{0:T(1024)(128)(4,1)S(1)}, s32[]{:S(2)}) async-start(s8[7340032]{0:T(1024)(128)(4,1)} %bitcast.312), calls=%async_computation.2 | async-start | bytes 6291456
  224.6 74.8 %collective-permute-start.22 = (bf16[2,8,64,512]{3,2,1,0:T(8,128)(2,1)}, bf16[2,8,64,512]{3,2,1,0:T(8,128)(2,1)}, u32[]{:S(2)}, u32[]{:S(2)}) collective-permute-start(bf16[2,8,64,512]{3,2,1,0:T(8,128)(2,1)} %dynamic-slice_bitcast_fusion.3), channel_id=1, source_target_pairs={{0,8},{8,0},{16,24},{24,16},{1,9},{9,1},{17,25},{25,17},{2,10},{10... | collective-permute-start | bytes 3145736 | tf_op jit(solution)/shard_map/ppermute | solution.py:281
  242.2 16.4 %copy-start.22 = (bf16[32,64,512]{2,1,0:T(8,128)(2,1)S(1)}, bf16[32,64,512]{2,1,0:T(8,128)(2,1)}, u32[]{:S(2)}) copy-start(bf16[32,64,512]{2,1,0:T(8,128)(2,1)} %get-tuple-element.49) | copy-start | bytes 6291460
  259.7 43.8 %collective-permute-start.30 = (bf16[2,8,64,512]{3,2,1,0:T(8,128)(2,1)}, bf16[2,8,64,512]{3,2,1,0:T(8,128)(2,1)}, u32[]{:S(2)}, u32[]{:S(2)}) collective-permute-start(bf16[2,8,64,512]{3,2,1,0:T(8,128)(2,1)} %dynamic-slice_bitcast_fusion), channel_id=1, source_target_pairs={{0,8},{8,0},{16,24},{24,16},{1,9},{9,1},{17,25},{25,17},{2,10},{10... | collective-permute-start | bytes 3145736 | tf_op jit(solution)/shard_map/ppermute | solution.py:281
  261.8 4.3 %collective-permute-start.32 = (f32[9,1024]{1,0:T(8,128)S(1)}, f32[9,1024]{1,0:T(8,128)S(1)}, u32[]{:S(2)}, u32[]{:S(2)}) collective-permute-start(f32[9,1024]{1,0:T(8,128)S(1)} %maximum_multiply_fusion), channel_id=1, source_target_pairs={{0,2},{2,0},{4,6},{6,4},{1,3},{3,1},{5,7},{7,5},{8,10},{10,8},{12,... | collective-permute-start | bytes 110600 | tf_op jit(solution)/shard_map/ppermute | solution.py:304
  264.3 9.3 %collective-permute-start.19 = (bf16[1,2,128,512]{3,2,1,0:T(8,128)(2,1)S(1)}, bf16[1,2,128,512]{3,2,1,0:T(8,128)(2,1)S(1)}, u32[]{:S(2)}, u32[]{:S(2)}) collective-permute-start(bf16[1,2,128,512]{3,2,1,0:T(8,128)(2,1)S(1)} %bitcast.336), channel_id=1, source_target_pairs={{0,16},{8,24},{16,0},{24,8},{1,17},{9,25},{17,1},{25,9},{2,18},{10... | collective-permute-start | bytes 786440 | tf_op jit(solution)/shard_map/ppermute | solution.py:293
  266.0 12.0 %collective-permute-start.16 = (bf16[1,2,128,512]{3,2,1,0:T(8,128)(2,1)S(1)}, bf16[1,2,128,512]{3,2,1,0:T(8,128)(2,1)S(1)}, u32[]{:S(2)}, u32[]{:S(2)}) collective-permute-start(bf16[1,2,128,512]{3,2,1,0:T(8,128)(2,1)S(1)} %bitcast.331), channel_id=1, source_target_pairs={{0,16},{8,24},{16,0},{24,8},{1,17},{9,25},{17,1},{25,9},{2,18},{10... | collective-permute-start | bytes 786440 | tf_op jit(solution)/shard_map/ppermute | solution.py:293
  273.5 10.4 %collective-permute-start.33 = (f32[9,1024]{1,0:T(8,128)S(1)}, f32[9,1024]{1,0:T(8,128)S(1)}, u32[]{:S(2)}, u32[]{:S(2)}) collective-permute-start(f32[9,1024]{1,0:T(8,128)S(1)} %fusion.54), channel_id=1, source_target_pairs={{0,4},{2,6},{4,0},{6,2},{1,5},{3,7},{5,1},{7,3},{8,12},{10,14},{12... | collective-permute-start | bytes 110600 | tf_op jit(solution)/shard_map/ppermute | solution.py:304
  278.1 7.5 %collective-permute-start.20 = (bf16[2,2,128,512]{3,2,1,0:T(8,128)(2,1)S(1)}, bf16[2,2,128,512]{3,2,1,0:T(8,128)(2,1)S(1)}, u32[]{:S(2)}, u32[]{:S(2)}) collective-permute-start(bf16[2,2,128,512]{3,2,1,0:T(8,128)(2,1)S(1)} %maximum_select_fusion.11), channel_id=1, source_target_pairs={{0,8},{8,0},{16,24},{24,16},{1,9},{9,1},{17,25},{25,17},{2,10},{10... | collective-permute-start | bytes 1572872 | tf_op jit(solution)/shard_map/ppermute | solution.py:293
  283.9 3.1 collective-permute-start.17
  285.5 21.1 %collective-permute-start.28 = (bf16[2,8,64,512]{3,2,1,0:T(8,128)(2,1)}, bf16[2,8,64,512]{3,2,1,0:T(8,128)(2,1)}, u32[]{:S(2)}, u32[]{:S(2)}) collective-permute-start(bf16[2,8,64,512]{3,2,1,0:T(8,128)(2,1)} %dynamic-slice_bitcast_fusion.1), channel_id=1, source_target_pairs={{0,8},{8,0},{16,24},{24,16},{1,9},{9,1},{17,25},{25,17},{2,10},{10... | collective-permute-start | bytes 3145736 | tf_op jit(solution)/shard_map/ppermute | solution.py:281
  298.9 24.8 %collective-permute-start.25 = (bf16[1,8,64,512]{3,2,1,0:T(8,128)(2,1)}, bf16[1,8,64,512]{3,2,1,0:T(8,128)(2,1)S(1)}, u32[]{:S(2)}, u32[]{:S(2)}) collective-permute-start(bf16[1,8,64,512]{3,2,1,0:T(8,128)(2,1)} %dynamic-slice_convert_fusion.4), channel_id=1, source_target_pairs={{0,16},{8,24},{16,0},{24,8},{1,17},{9,25},{17,1},{25,9},{2,18},{10... | collective-permute-start | bytes 1572872 | tf_op jit(solution)/shard_map/ppermute | solution.py:281
  302.1 23.2 %collective-permute-start.23 = (bf16[1,8,64,512]{3,2,1,0:T(8,128)(2,1)}, bf16[1,8,64,512]{3,2,1,0:T(8,128)(2,1)}, u32[]{:S(2)}, u32[]{:S(2)}) collective-permute-start(bf16[1,8,64,512]{3,2,1,0:T(8,128)(2,1)} %dynamic-slice_convert_fusion.5), channel_id=1, source_target_pairs={{0,16},{8,24},{16,0},{24,8},{1,17},{9,25},{17,1},{25,9},{2,18},{10... | collective-permute-start | bytes 1572872 | tf_op jit(solution)/shard_map/ppermute | solution.py:281
  306.0 30.4 %collective-permute-start.31 = (bf16[1,8,64,512]{3,2,1,0:T(8,128)(2,1)}, bf16[1,8,64,512]{3,2,1,0:T(8,128)(2,1)S(1)}, u32[]{:S(2)}, u32[]{:S(2)}) collective-permute-start(bf16[1,8,64,512]{3,2,1,0:T(8,128)(2,1)} %dynamic-slice_convert_fusion.2), channel_id=1, source_target_pairs={{0,16},{8,24},{16,0},{24,8},{1,17},{9,25},{17,1},{25,9},{2,18},{10... | collective-permute-start | bytes 1572872 | tf_op jit(solution)/shard_map/ppermute | solution.py:281
  309.7 37.0 %collective-permute-start.29 = (bf16[1,8,64,512]{3,2,1,0:T(8,128)(2,1)}, bf16[1,8,64,512]{3,2,1,0:T(8,128)(2,1)}, u32[]{:S(2)}, u32[]{:S(2)}) collective-permute-start(bf16[1,8,64,512]{3,2,1,0:T(8,128)(2,1)} %dynamic-slice_convert_fusion.3), channel_id=1, source_target_pairs={{0,16},{8,24},{16,0},{24,8},{1,17},{9,25},{17,1},{25,9},{2,18},{10... | collective-permute-start | bytes 1572872 | tf_op jit(solution)/shard_map/ppermute | solution.py:281
  326.7 9.7 %copy-start.8 = (f32[2,8,64,512]{3,2,1,0:T(8,128)S(1)}, f32[2,8,64,512]{3,2,1,0:T(8,128)}, u32[]{:S(2)}) copy-start(f32[2,8,64,512]{3,2,1,0:T(8,128)} %copy-done.7) | copy-start | bytes 6291460
  328.3 18.4 %copy-start.12 = (f32[2,8,64,512]{3,2,1,0:T(8,128)S(1)}, f32[2,8,64,512]{3,2,1,0:T(8,128)}, u32[]{:S(2)}) copy-start(f32[2,8,64,512]{3,2,1,0:T(8,128)} %copy-done.11) | copy-start | bytes 6291460
  (25 other events, 64.1 us)
Sparse Core Ops, SparseCore 0:
  260.1 58.3 all-reduce.4

commit v3 on v2

--- a/solution.py
+++ b/solution.py
@@ -12,6 +12,7 @@
 VOID = 19
 LANES = 128
 VMEM_LIMIT = 56 * 1024 * 1024
+VECTOR_COST = 3800
 
 
 def swish_slope(value):
@@ -140,7 +141,7 @@
         ],
         compiler_params=pltpu.CompilerParams(vmem_limit_bytes=VMEM_LIMIT),
         cost_estimate=pl.CostEstimate(
-            flops=2 * rows * ext * chans * outs, bytes_accessed=2 * rows * chans * (cols + ext + BAND), transcendentals=0
+            flops=VECTOR_COST * 3 * rows * BAND * chans, bytes_accessed=2 * rows * chans * (cols + ext + BAND), transcendentals=0
         ),
         name="depth_pointwise",
     )(scal, feats, taps, weight)
@@ -233,7 +234,7 @@
         ],
         compiler_params=pltpu.CompilerParams(vmem_limit_bytes=VMEM_LIMIT),
         cost_estimate=pl.CostEstimate(
-            flops=2 * rows * ext * chans * outs, bytes_accessed=8 * rows * chans * BAND, transcendentals=0
+            flops=VECTOR_COST * 4 * rows * BAND * chans, bytes_accessed=8 * rows * chans * BAND, transcendentals=0
         ),
         name="depth_gradients",
     )(scal, grad, weight, taps, band)
@@ -243,13 +244,24 @@
     return lax.dynamic_index_in_dim(array, index, axis, keepdims=False)
 
 
-def owner_sum(blocks, axis):
+def owner_terms(blocks, axis):
     size, me = lax.axis_size(axis), lax.axis_index(axis)
-    total = pick(blocks, me).astype(jnp.float32)
+    terms = []
     for k in range(1, size):
         sent = pick(blocks, lax.rem(me + k, size)).astype(jnp.bfloat16)
-        total = total + lax.ppermute(sent, axis, [(i, (i + k) % size) for i in range(size)]).astype(jnp.float32)
+        terms.append(lax.ppermute(sent, axis, [(i, (i + k) % size) for i in range(size)]))
+    return terms
+
+
+def owner_total(blocks, terms, axis):
+    total = pick(blocks, lax.axis_index(axis)).astype(jnp.float32)
+    for term in terms:
+        total = total + term.astype(jnp.float32)
     return total
+
+
+def owner_sum(blocks, axis):
+    return owner_total(blocks, owner_terms(blocks, axis), axis)
 
 
 def trade(blocks, axis):
@@ -270,26 +282,32 @@
     return lax.all_gather(block, axis)
 
 
-def halving_sum(blocks, axis):
+def halving_step(blocks, axis, bit):
     size, me = lax.axis_size(axis), lax.axis_index(axis)
-    shape = blocks.shape[1:]
-    bit = 1
-    while bit < size:
-        blocks = blocks.reshape((blocks.shape[0] // 2, 2) + shape)
-        mine = lax.rem(me // bit, 2)
-        sent = pick(blocks, 1 - mine, 1).astype(jnp.bfloat16)
-        got = lax.ppermute(sent, axis, [(i, i ^ bit) for i in range(size)])
-        blocks = pick(blocks, mine, 1).astype(jnp.float32) + got.astype(jnp.float32)
+    blocks = blocks.reshape((blocks.shape[0] // 2, 2) + blocks.shape[1:])
+    mine = lax.rem(me // bit, 2)
+    sent = pick(blocks, 1 - mine, 1).astype(jnp.bfloat16)
+    got = lax.ppermute(sent, axis, [(i, i ^ bit) for i in range(size)])
+    return pick(blocks, mine, 1).astype(jnp.float32) + got.astype(jnp.float32)
+
+
+def halving_rest(blocks, axis, bit):
+    while bit < lax.axis_size(axis):
+        blocks = halving_step(blocks, axis, bit)
         bit *= 2
     return blocks[0]
 
 
-def doubling_gather(block, axis):
+def halving_sum(blocks, axis):
+    return halving_rest(blocks, axis, 1)
+
+
+def doubling_gather(block, axis, bit=None, last=1):
     size, me = lax.axis_size(axis), lax.axis_index(axis)
-    shape = block.shape
-    block = block[None]
-    bit = size // 2
-    while bit:
+    if bit is None:
+        bit, block = size // 2, block[None]
+    shape = block.shape[1:]
+    while bit >= last:
         got = lax.ppermute(block, axis, [(i, i ^ bit) for i in range(size)])
         mine = lax.rem(me // bit, 2)
         both = jnp.where(mine == 0, jnp.stack([block, got], 1), jnp.stack([got, block], 1))
@@ -334,6 +352,14 @@
     starts = [lax.rem(offsets[f] + (cols - wing), cols) for f in range(frames)]
     scals = [jnp.stack([offsets[f], widths[f], rate, jnp.int32(cols)]) for f in range(frames)]
 
+    firsts = [forward_call(scals[0], feats, taps, weight, 0, margin, wing)]
+    for f in range(1, frames):
+        scal, proj_all, pw_bias_all, proj_bias_all = lax.optimization_barrier(
+            (scals[f], proj_all, pw_bias_all, proj_bias_all)
+        )
+        firsts.append(forward_call(scal, feats, taps, weight, f, margin, wing))
+
+    _, upstream, labels = lax.optimization_barrier((firsts[0][2], upstream, labels))
     ups, labeled = [], []
     for f in range(frames):
         up = rolled(upstream[:, f], starts[f], 2).reshape(share, parts, sections, piece)
@@ -342,18 +368,21 @@
         marks = rolled(labels[f], starts[f], 1).reshape(parts, sections, piece)
         labeled.append((pick(pick(marks, part), section) != VOID).astype(jnp.float32))
 
-    firsts = [forward_call(scals[f], feats, taps, weight, f, margin, wing) for f in range(frames)]
-
+    pre_grad = firsts[-1][2]
+    blocked = [first[2].reshape(parts, rows_own * ext, branch) for first in firsts]
+    terms = [owner_terms(blocks, "chan") for blocks in blocked]
     kept, grads, outs = [], [], []
     proj_sum = pw_bias_sum = proj_bias_sum = 0.0
     for f in range(frames):
-        depth, band, pre = firsts[f]
-        own = owner_sum(pre.reshape(parts, rows_own * ext, branch), "chan") + pw_bias_all
+        blocks, arrived, _ = lax.optimization_barrier((blocked[f], terms[f], pre_grad))
+        own = owner_total(blocks, arrived, "chan") + pw_bias_all
         rest = jnp.broadcast_to(pw_bias_all, (rows_own, cols - ext, branch))
         preact = jnp.concatenate([own.reshape(rows_own, ext, branch), rest], axis=1).reshape(pixels, branch)
         act = jax.nn.silu(preact).astype(jnp.bfloat16)
         zpart = jnp.dot(act, proj_all, preferred_element_type=jnp.float32)
         zvalue = halving_sum(zpart.reshape(sections, piece, branch), "section") + proj_bias_all
+        if f + 1 < frames:
+            zvalue, terms[f + 1] = lax.optimization_barrier((zvalue, terms[f + 1]))
         outs.append(jax.nn.silu(zvalue).astype(jnp.bfloat16))
         out_grad = ups[f].astype(jnp.float32) * swish_slope(zvalue) * labeled[f][:, None]
         out_grad = doubling_gather(out_grad.astype(jnp.bfloat16), "section").reshape(pixels, branch)
@@ -361,9 +390,9 @@
         pre_grad = (act_grad * swish_slope(preact)).astype(jnp.bfloat16)
         sent = pre_grad.reshape(rows_own, cols, branch)[:, :ext]
         grads.append(gather(sent, "chan").reshape(rows, ext, branch))
-        kept.append((act, out_grad, pre_grad))
-
-    outs, kept, _ = lax.optimization_barrier((outs, kept, grads[-1]))
+        kept.append(lax.optimization_barrier((act, out_grad, pre_grad)))
+
+    outs, grads[0], _ = lax.optimization_barrier((outs, grads[0], pre_grad))
     pw_sum = 0.0
     for f in range(frames):
         act, out_grad, pre_grad = kept[f]
@@ -381,27 +410,44 @@
     bias_rows = owner_sum(bias_rows, "chan")
     bias_rows = jnp.pad(bias_rows, ((0, 6), (0, branch - share)))
     shared = jnp.concatenate([pw_sum, proj_rows, bias_rows], axis=0) * scaling
-    if frames > 1:
-        grads[-1], shared = lax.optimization_barrier((grads[-1], shared))
-    shared = lax.psum(shared, "dp")
-
+    depth_count = lax.axis_size("dp")
+    shared = shared.reshape(depth_count, shared.shape[0] // depth_count, branch)
+    swapped = [trade(outs[f].reshape(piece, parts, share).transpose(1, 2, 0), "chan") for f in range(frames)]
+
+    def first_step(term):
+        term = term.reshape((sections, rows // sections) + term.shape[1:])
+        return halving_step(term, "section", 1)
+
+    stepped, dw_sum = [], 0.0
+    for f in range(frames - 1):
+        term, dw = backward_call(scals[f], grads[f], weight, taps, firsts[f][1], margin, wing, 0, 1)
+        stepped.append([first_step(term)])
+        dw_sum = dw_sum + dw
+    last = grads[-1]
+    last, stepped, shared, swapped = lax.optimization_barrier((last, stepped, shared, swapped))
+    shared = halving_step(shared, "dp", 1)
+    spreads = [doubling_gather(swapped[f][None], "section", sections // 2, 2) for f in range(frames)]
+    summed = [[halving_rest(part, "section", 2) for part in parts_of] for parts_of in stepped]
     cuts = 2 if chans % 512 == 0 else 1
-    terms, dw_sums = [], [0.0] * cuts
+    final, dw_last = [], []
+    for cut in range(cuts):
+        if cut:
+            last, shared, spreads, summed, term = lax.optimization_barrier((last, shared, spreads, summed, term))
+            final.append(first_step(term))
+        term, dw = backward_call(scals[-1], last, weight, taps, firsts[-1][1], margin, wing, cut, cuts)
+        dw_last.append(dw)
+    final.append(first_step(term))
+    summed.append([halving_rest(part, "section", 2) for part in final])
+    shared = halving_rest(shared, "dp", 2).astype(jnp.bfloat16)
+    shared = doubling_gather(shared, "dp").reshape(-1, branch).astype(jnp.float32)
+    kernel_grad = butterfly_sum((dw_sum + jnp.concatenate(dw_last, axis=1)) * scaling, "dp")
+
+    terms, results = [], []
     for f in range(frames):
-        band, halves = firsts[f][1], []
-        for cut in range(cuts):
-            term, dw = backward_call(scals[f], grads[f], weight, taps, band, margin, wing, cut, cuts)
-            own_rows = halving_sum(term.reshape(sections, rows // sections, BAND, chans // cuts), "section")
-            halves.append(own_rows.astype(jnp.bfloat16))
-            dw_sums[cut] = dw_sums[cut] + dw
-        own_rows = jnp.pad(jnp.concatenate(halves, axis=2), ((0, 0), (0, cols - BAND), (0, 0)))
+        own_rows = jnp.concatenate(summed[f], axis=2).astype(jnp.bfloat16)
+        own_rows = jnp.pad(own_rows, ((0, 0), (0, cols - BAND), (0, 0)))
         terms.append(rolled(own_rows, lax.rem(cols - offsets[f], cols), 1))
-    kernel_grad = butterfly_sum(jnp.concatenate(dw_sums, axis=1) * scaling, "dp")
-
-    results = []
-    for f in range(frames):
-        swapped = trade(outs[f].reshape(piece, parts, share).transpose(1, 2, 0), "chan")
-        whole = doubling_gather(swapped, "section").transpose(2, 1, 0, 3).reshape(share, rows, cols)
+        whole = doubling_gather(spreads[f], "section", 1).transpose(2, 1, 0, 3).reshape(share, rows, cols)
         results.append(rolled(whole, lax.rem(cols - starts[f], cols), 2))
 
     proj_end = chans + share

time: 365 us -> 371 us (1.016)
  between operations: 18.1 us -> 4.6 us
  local copies, waits for them, and re-layouts: 48.8 us -> 55.6 us
  matrix products: 10.1 us -> 16.7 us
  Pallas kernels: 108 us -> 103 us
  starting transfers between devices: 29.8 us -> 34.5 us
  waiting for transfers between devices: 93.8 us -> 97.6 us
    ppermute x16, waiting for transfers between devices: 24.2 us -> 50.7 us  [the longest x12 41 us: halving_step(): got = lax.ppermute(sent, axis, [(i, i ^ bit) for i in range(size)])]
    ppermute x4, waiting for transfers between devices: 38.6 us -> 23.5 us  [gather(): got = lax.ppermute(block, axis, [(0, 1), (1, 0)])]
    psum x1 -> x0, waiting for transfers between devices: 7.4 us -> none  [local(): shared = lax.psum(shared, 'dp')]
    dot_general x2, matrix products: 7.41 us -> 12.8 us  [local(): lax.dot_general(firsts[f][0].reshape(rows * ext, chans), grads[f].reshape...]
    pallas_call x4 -> x3, Pallas kernels: 64.6 us -> 60.2 us  [backward_call(): pl.pallas_call(lambda *refs: backward_kernel(*refs, margin=margin, wing=w...]
    ppermute x16, starting transfers between devices: 12.3 us -> 16.5 us  [the longest x12 12.3 us: halving_step(): got = lax.ppermute(sent, axis, [(i, i ^ bit) for i in range(size)])]
    concatenate x6, other arithmetic: 3.29 us -> 7.28 us  [rolled(): jnp.concatenate([array, array], axis)]
    convert_element_type x11 -> x13, local copies, waits for them, and re-layouts: 11.5 us -> 7.48 us  [the longest x3 5.08 us: owner_terms(): sent = pick(blocks, lax.rem(me + k, size)).astype(jnp.bfloat16)]
  transfers between devices with their start and end apart: 35 -> 36, of which waited for: 13 -> 15; matrix products, arithmetic and copies ran while one was open for 24% -> 29% of each run, Pallas kernels for 30% -> 24%
where the time goes in v3:
time: 371 us; the launch traced here: 366 us
  Pallas kernels  103 us (28%)
  waiting for transfers between devices  97.6 us (26%)
  local copies, waits for them, and re-layouts  55.6 us (15%)
  other arithmetic  53.1 us (14%)
  starting transfers between devices  34.5 us (9%)
  matrix products  16.7 us (5%)
  between operations  4.6 us (1%)
    pallas_call x3, Pallas kernels, backward_call(): pl.pallas_call(lambda *refs: backward_kernel(*refs, margin=margin, wing=w...  60.2 us
    pallas_call x2, Pallas kernels, forward_call(): pl.pallas_call(lambda *refs: forward_kernel(*refs, margin=margin, wing=wi...  43.3 us
    ppermute x12, waiting for transfers between devices, halving_step(): got = lax.ppermute(sent, axis, [(i, i ^ bit) for i in range(size)])  41 us
    ppermute x4, waiting for transfers between devices, gather(): got = lax.ppermute(block, axis, [(0, 1), (1, 0)])  23.5 us
    ppermute x10, waiting for transfers between devices, doubling_gather(): got = lax.ppermute(block, axis, [(i, i ^ bit) for i in range(size)])  17.3 us
    dot_general x2, matrix products, local(): lax.dot_general(firsts[f][0].reshape(rows * ext, chans), grads[f].reshape...  12.8 us
    ppermute x12, starting transfers between devices, halving_step(): got = lax.ppermute(sent, axis, [(i, i ^ bit) for i in range(size)])  12.3 us
    ppermute x4, waiting for transfers between devices, owner_terms(): lax.ppermute(sent, axis, [(i, (i + k) % size) for i in range(size)])  9.68 us
  transfers between devices with their start and end apart: 36, of which 15 were waited for; matrix products, arithmetic and copies ran while one was open for 29% of the time, Pallas kernels for 24%

profile of v3, /device:TPU:0, one launch (start us, length us, event | category | flops | bytes accessed | tf_op | source)
XLA Modules:
  0.0 365.6 jit_solution(11589673092961848160)
XLA Ops:
  1.3 3.0 collective-permute-start.2
  7.0 3.2 pad_add_fusion
  10.2 21.3 %depth_pointwise.2 = (bf16[32,112,1024]{2,1,0:T(8,128)(2,1)}, bf16[32,64,1024]{2,1,0:T(8,128)(2,1)}, f32[3584,256]{1,0:T(8,128)}) custom-call(s32[4]{0:T(128)} %get-tuple-element.150.refs_0_, bf16[2,32,128,1024]{3,2,1,0:T(8,128)(2,1)} %refs_1_.3, bf16[9,1024]{1,0:T(8,128)(2,1)} %bitcast.373, bf16[1024,256]{1,0:T(8,128)(2,1)} %bitcast.368), custom_call_target="tpu_custom_call" | custom-call | flops 23907532800 | bytes 19922944 | tf_op jit(solution)/shard_map/depth_pointwise/pallas_call | solution.py:113
  31.5 2.5 fusion.30
  34.0 2.0 collective-permute-start.3
  36.6 3.5 copy.69
  41.3 2.0 fusion.27
  46.5 2.0 collective-permute-start.7
  49.8 22.0 %depth_pointwise.3 = (bf16[32,112,1024]{2,1,0:T(8,128)(2,1)}, bf16[32,64,1024]{2,1,0:T(8,128)(2,1)}, f32[3584,256]{1,0:T(8,128)}) custom-call(s32[4]{0:T(128)} %get-tuple-element.53.refs_0_, bf16[2,32,128,1024]{3,2,1,0:T(8,128)(2,1)} %refs_1_.3, bf16[9,1024]{1,0:T(8,128)(2,1)} %bitcast.374, bf16[1024,256]{1,0:T(8,128)(2,1)} %bitcast.369), custom_call_target="tpu_custom_call" | custom-call | flops 23907532800 | bytes 19922944 | tf_op jit(solution)/shard_map/depth_pointwise/pallas_call | solution.py:113
  82.6 2.6 fusion.31
  87.5 3.0 collective-permute-start.5
  92.3 2.1 copy.98
  94.4 3.1 collective-permute-done.5
  98.5 9.7 %collective-permute-done.6 = bf16[1792,256]{1,0:T(8,128)(2,1)} collective-permute-done((bf16[1792,256]{1,0:T(8,128)(2,1)}, bf16[1792,256]{1,0:T(8,128)(2,1)}, u32[]{:S(2)}, u32[]{:S(2)}) %collective-permute-start.6) | collective-permute-done | bytes 917536 | tf_op jit(solution)/shard_map/ppermute | solution.py:252
  108.2 2.0 multiply_convert_fusion.5
  110.2 2.6 collective-permute-start.8
  114.8 4.2 %collective-permute-done.8 = bf16[1,512,256]{2,1,0:T(8,128)(2,1)S(1)} collective-permute-done((bf16[1,512,256]{2,1,0:T(8,128)(2,1)S(1)}, bf16[1,512,256]{2,1,0:T(8,128)(2,1)S(1)}, u32[]{:S(2)}, u32[]{:S(2)}) %collective-permute-start.8) | collective-permute-done | bytes 262176 | tf_op jit(solution)/shard_map/ppermute | solution.py:311
  127.8 1.8 collective-permute-start.11
  130.3 5.9 %collective-permute-done.11 = bf16[1,512,256]{2,1,0:T(8,128)(2,1)S(1)} collective-permute-done((bf16[1,512,256]{2,1,0:T(8,128)(2,1)S(1)}, bf16[1,512,256]{2,1,0:T(8,128)(2,1)S(1)}, u32[]{:S(2)}, u32[]{:S(2)}) %collective-permute-start.11) | collective-permute-done | bytes 262176 | tf_op jit(solution)/shard_map/ppermute | solution.py:290
  137.2 1.7 collective-permute-start.12
  140.1 4.6 %collective-permute-done.12 = bf16[1,512,256]{2,1,0:T(8,128)(2,1)S(1)} collective-permute-done((bf16[1,512,256]{2,1,0:T(8,128)(2,1)S(1)}, bf16[1,512,256]{2,1,0:T(8,128)(2,1)S(1)}, u32[]{:S(2)}, u32[]{:S(2)}) %collective-permute-start.12) | collective-permute-done | bytes 262176 | tf_op jit(solution)/shard_map/ppermute | solution.py:311
  145.5 6.5 %collective-permute-done.15 = bf16[16,112,256]{2,1,0:T(8,128)(2,1)S(1)} collective-permute-done((bf16[16,112,256]{2,1,0:T(8,128)(2,1)S(1)}, bf16[16,112,256]{2,1,0:T(8,128)(2,1)S(1)}, u32[]{:S(2)}, u32[]{:S(2)}) %collective-permute-start.15) | collective-permute-done | bytes 917536 | tf_op jit(solution)/shard_map/ppermute | solution.py:280
  156.6 6.9 %convolution_bitcast_fusion = f32[1024,256]{1,0:T(8,128)} fusion(bf16[32,112,1024]{2,1,0:T(8,128)(2,1)} %get-tuple-element.68, bf16[32,112,256]{2,1,0:T(8,128)(2,1)} %bitcast.294), kind=kOutput, calls=%fused_computation.66 | convolution fusion | flops 1879048192 | bytes 10223616 | tf_op jit(solution)/shard_map/dot_general | solution.py:399
  163.4 27.8 %depth_gradients.3 = (bf16[32,64,1024]{2,1,0:T(8,128)(2,1)}, f32[9,1024]{1,0:T(8,128)}) custom-call(s32[4]{0:T(128)} %get-tuple-element.150.refs_0_, bf16[32,112,256]{2,1,0:T(8,128)(2,1)} %bitcast.295, bf16[1024,256]{1,0:T(8,128)(2,1)} %bitcast.370, bf16[9,1024]{1,0:T(8,128)(2,1)} %bitcast.375, bf16[32,64,1024]{2,1,0:T(8,128)(2,1)} %get-tuple-element.66.refs_4_), custom_call_target="tpu_custom_call" | custom-call | flops 31876710400 | bytes 16777216 | tf_op jit(solution)/shard_map/depth_gradients/pallas_call | solution.py:211
  194.6 1.8 copy.100
  199.6 3.2 dynamic-slice_bitcast_fusion
  204.5 17.1 %collective-permute-done.14 = bf16[16,112,256]{2,1,0:T(8,128)(2,1)S(1)} collective-permute-done((bf16[16,112,256]{2,1,0:T(8,128)(2,1)S(1)}, bf16[16,112,256]{2,1,0:T(8,128)(2,1)S(1)}, u32[]{:S(2)}, u32[]{:S(2)}) %collective-permute-start.14) | collective-permute-done | bytes 917536 | tf_op jit(solution)/shard_map/ppermute | solution.py:280
  221.9 5.9 %convolution_add_fusion = f32[1024,256]{1,0:T(8,128)S(1)} fusion(f32[1024,256]{1,0:T(8,128)S(1)} %copy-done.3, bf16[3584,1024]{1,0:T(8,128)(2,1)} %bitcast.296, bf16[3584,256]{1,0:T(8,128)(2,1)S(1)} %bitcast.299), kind=kOutput, calls=%fused_computation.67 | convolution fusion | flops 1879310336 | bytes 11272192 | tf_op jit(solution)/shard_map/dot_general | solution.py:399
  228.0 3.2 convert_add_fusion
  231.3 2.0 collective-permute-start.23
  235.3 16.2 %depth_gradients.4 = (bf16[32,64,512]{2,1,0:T(8,128)(2,1)}, f32[9,512]{1,0:T(8,128)}) custom-call(s32[4]{0:T(128)} %get-tuple-element.53.refs_0_, bf16[32,112,256]{2,1,0:T(8,128)(2,1)} %bitcast.300, bf16[1024,256]{1,0:T(8,128)(2,1)} %bitcast.371, bf16[9,1024]{1,0:T(8,128)(2,1)} %bitcast.376, bf16[32,64,1024]{2,1,0:T(8,128)(2,1)} %get-tuple-element.83.refs_4_), custom_call_target="tpu_custom_call" | custom-call | flops 15938355200 | bytes 8388608 | tf_op jit(solution)/shard_map/depth_gradients/pallas_call | solution.py:211
  252.6 2.3 maximum_select_fusion.11
  255.0 10.9 %collective-permute-done.24 = bf16[1,8,64,1024]{3,2,1,0:T(8,128)(2,1)} collective-permute-done((bf16[1,8,64,1024]{3,2,1,0:T(8,128)(2,1)S(1)}, bf16[1,8,64,1024]{3,2,1,0:T(8,128)(2,1)}, u32[]{:S(2)}, u32[]{:S(2)}) %collective-permute-start.24) | collective-permute-done | bytes 1048608 | tf_op jit(solution)/shard_map/ppermute | solution.py:290
  267.4 16.2 %depth_gradients.5 = (bf16[32,64,512]{2,1,0:T(8,128)(2,1)}, f32[9,512]{1,0:T(8,128)}) custom-call(s32[4]{0:T(128)} %get-tuple-element.53.refs_0_, bf16[32,112,256]{2,1,0:T(8,128)(2,1)} %bitcast.301, bf16[1024,256]{1,0:T(8,128)(2,1)} %bitcast.372, bf16[9,1024]{1,0:T(8,128)(2,1)} %bitcast.377, bf16[32,64,1024]{2,1,0:T(8,128)(2,1)} %get-tuple-element.83.refs_4_), custom_call_target="tpu_custom_call" | custom-call | flops 15938355200 | bytes 8388608 | tf_op jit(solution)/shard_map/depth_gradients/pallas_call | solution.py:211
  286.2 2.7 collective-permute-start.33
  295.2 5.2 %collective-permute-done.32 = f32[9,1024]{1,0:T(8,128)S(1)} collective-permute-done((f32[9,1024]{1,0:T(8,128)S(1)}, f32[9,1024]{1,0:T(8,128)S(1)}, u32[]{:S(2)}, u32[]{:S(2)}) %collective-permute-start.32) | collective-permute-done | bytes 36896 | tf_op jit(solution)/shard_map/ppermute | solution.py:322
  301.0 7.5 %collective-permute-done.34 = bf16[1,290,256]{2,1,0:T(8,128)(2,1)S(1)} collective-permute-done((bf16[1,290,256]{2,1,0:T(8,128)(2,1)S(1)}, bf16[1,290,256]{2,1,0:T(8,128)(2,1)S(1)}, u32[]{:S(2)}, u32[]{:S(2)}) %collective-permute-start.34) | collective-permute-done | bytes 148512 | tf_op jit(solution)/shard_map/ppermute | solution.py:311
  311.5 2.0 fusion.25
  313.5 1.7 copy.89
  315.2 1.7 maximum_select_fusion.5
  319.6 1.8 fusion.24
  321.3 2.7 copy.92
  325.5 2.1 copy.94
  333.5 2.0 convert_add_fusion.1
  337.6 1.8 collective-permute-start.28
  340.5 10.0 %collective-permute-done.30 = bf16[1,8,64,512]{3,2,1,0:T(8,128)(2,1)S(1)} collective-permute-done((bf16[1,8,64,512]{3,2,1,0:T(8,128)(2,1)S(1)}, bf16[1,8,64,512]{3,2,1,0:T(8,128)(2,1)S(1)}, u32[]{:S(2)}, u32[]{:S(2)}) %collective-permute-start.30) | collective-permute-done | bytes 524320 | tf_op jit(solution)/shard_map/ppermute | solution.py:290
  350.7 10.1 %collective-permute-done.28 = bf16[1,8,64,512]{3,2,1,0:T(8,128)(2,1)S(1)} collective-permute-done((bf16[1,8,64,512]{3,2,1,0:T(8,128)(2,1)S(1)}, bf16[1,8,64,512]{3,2,1,0:T(8,128)(2,1)S(1)}, u32[]{:S(2)}, u32[]{:S(2)}) %collective-permute-start.28) | collective-permute-done | bytes 524320 | tf_op jit(solution)/shard_map/ppermute | solution.py:290
  362.8 2.4 pad_maximum_fusion
  (222 shorter events, 82.9 us)
Async XLA Ops:
  1.3 47.9 %collective-permute-start.2 = (f32[2,128]{1,0:T(2,128)S(1)}, f32[2,128]{1,0:T(2,128)S(1)}, u32[]{:S(2)}, u32[]{:S(2)}) collective-permute-start(f32[2,128]{1,0:T(2,128)S(1)} %get-tuple-element.144), channel_id=1, source_target_pairs={{0,1},{1,0},{2,3},{3,2},{4,5},{5,4},{6,7},{7,6},{8,9},{9,8},{10,11... | collective-permute-start | bytes 3080 | tf_op jit(solution)/shard_map/ppermute | solution.py:280
  4.3 45.5 %collective-permute-start.1 = (bf16[128,256]{1,0:T(8,128)(2,1)}, bf16[128,256]{1,0:T(8,128)(2,1)S(1)}, u32[]{:S(2)}, u32[]{:S(2)}) collective-permute-start(bf16[128,256]{1,0:T(8,128)(2,1)} %bitcast.353), channel_id=1, source_target_pairs={{0,1},{1,0},{2,3},{3,2},{4,5},{5,4},{6,7},{7,6},{8,9},{9,8},{10,11... | collective-permute-start | bytes 196616 | tf_op jit(solution)/shard_map/ppermute | solution.py:280
  34.0 37.8 %collective-permute-start.3 = (bf16[1792,256]{1,0:T(8,128)(2,1)}, bf16[1792,256]{1,0:T(8,128)(2,1)}, u32[]{:S(2)}, u32[]{:S(2)}) collective-permute-start(bf16[1792,256]{1,0:T(8,128)(2,1)} %fusion.30), channel_id=1, source_target_pairs={{0,1},{1,0},{2,3},{3,2},{4,5},{5,4},{6,7},{7,6},{8,9},{9,8},{10,11... | collective-permute-start | bytes 2752520 | tf_op jit(solution)/shard_map/ppermute | solution.py:252
  44.2 68.6 %collective-permute-start = (bf16[128,512]{1,0:T(8,128)(2,1)}, bf16[128,512]{1,0:T(8,128)(2,1)}, u32[]{:S(2)}, u32[]{:S(2)}) collective-permute-start(bf16[128,512]{1,0:T(8,128)(2,1)} %bitcast.8), channel_id=1, source_target_pairs={{0,1},{1,0},{2,3},{3,2},{4,5},{5,4},{6,7},{7,6},{8,9},{9,8},{10,11... | collective-permute-start | bytes 393224 | tf_op jit(solution)/shard_map/ppermute | solution.py:272
  46.5 44.1 %collective-permute-start.7 = (bf16[128,512]{1,0:T(8,128)(2,1)}, bf16[128,512]{1,0:T(8,128)(2,1)}, u32[]{:S(2)}, u32[]{:S(2)}) collective-permute-start(bf16[128,512]{1,0:T(8,128)(2,1)} %bitcast.37), channel_id=1, source_target_pairs={{0,1},{1,0},{2,3},{3,2},{4,5},{5,4},{6,7},{7,6},{8,9},{9,8},{10,11... | collective-permute-start | bytes 393224 | tf_op jit(solution)/shard_map/ppermute | solution.py:272
  49.8 23.4 %copy-start.25 = (f32[2,1,128]{2,1,0:T(1,128)}, f32[2,1,128]{2,1,0:T(1,128)S(1)}, u32[]{:S(2)}) copy-start(f32[2,1,128]{2,1,0:T(1,128)S(1)} %get-tuple-element.142) | copy-start | bytes 3076
  49.8 22.0 %copy-start.11 = (f32[3584,256]{1,0:T(8,128)S(1)}, f32[3584,256]{1,0:T(8,128)}, u32[]{:S(2)}) copy-start(f32[3584,256]{1,0:T(8,128)} %get-tuple-element.51) | copy-start | bytes 11010052
  75.5 9.7 %collective-permute-start.4 = (bf16[2,512,256]{2,1,0:T(8,128)(2,1)S(1)}, bf16[2,512,256]{2,1,0:T(8,128)(2,1)}, u32[]{:S(2)}, u32[]{:S(2)}) collective-permute-start(bf16[2,512,256]{2,1,0:T(8,128)(2,1)S(1)} %fusion.33), channel_id=1, source_target_pairs={{0,8},{8,0},{16,24},{24,16},{1,9},{9,1},{17,25},{25,17},{2,10},{10... | collective-permute-start | bytes 1572872 | tf_op jit(solution)/shard_map/ppermute | solution.py:290
  85.1 12.4 %copy-start.27 = (f32[2,1,128]{2,1,0:T(1,128)S(1)}, f32[2,1,128]{2,1,0:T(1,128)}, u32[]{:S(2)}) copy-start(f32[2,1,128]{2,1,0:T(1,128)} %get-tuple-element.141) | copy-start | bytes 3076
  85.1 23.1 %collective-permute-start.6 = (bf16[1792,256]{1,0:T(8,128)(2,1)}, bf16[1792,256]{1,0:T(8,128)(2,1)}, u32[]{:S(2)}, u32[]{:S(2)}) collective-permute-start(bf16[1792,256]{1,0:T(8,128)(2,1)} %fusion.31), channel_id=1, source_target_pairs={{0,1},{1,0},{2,3},{3,2},{4,5},{5,4},{6,7},{7,6},{8,9},{9,8},{10,11... | collective-permute-start | bytes 2752520 | tf_op jit(solution)/shard_map/ppermute | solution.py:252
  86.7 21.5 %copy-start.29 = (f32[1,1,512]{2,1,0:T(1,128)S(1)}, f32[1,1,512]{2,1,0:T(1,128)}, u32[]{:S(2)}) copy-start(f32[1,1,512]{2,1,0:T(1,128)} %compare_convert_fusion.1) | copy-start | bytes 6148
  87.5 10.0 %collective-permute-start.5 = (bf16[1,512,256]{2,1,0:T(8,128)(2,1)}, bf16[1,512,256]{2,1,0:T(8,128)(2,1)}, u32[]{:S(2)}, u32[]{:S(2)}) collective-permute-start(bf16[1,512,256]{2,1,0:T(8,128)(2,1)} %dynamic-slice_convert_fusion.7), channel_id=1, source_target_pairs={{0,16},{8,24},{16,0},{24,8},{1,17},{9,25},{17,1},{25,9},{2,18},{10... | collective-permute-start | bytes 786440 | tf_op jit(solution)/shard_map/ppermute | solution.py:290
  94.4 18.4 %copy-start.15 = (bf16[128,2,1,512]{3,0,2,1:T(8,128)(2,1)S(1)}, bf16[128,2,1,512]{3,0,2,1:T(8,128)(2,1)}, u32[]{:S(2)}) copy-start(bf16[128,2,1,512]{3,0,2,1:T(8,128)(2,1)} %copy.70) | copy-start | bytes 786436
  110.2 8.8 %collective-permute-start.8 = (bf16[1,512,256]{2,1,0:T(8,128)(2,1)S(1)}, bf16[1,512,256]{2,1,0:T(8,128)(2,1)S(1)}, u32[]{:S(2)}, u32[]{:S(2)}) collective-permute-start(bf16[1,512,256]{2,1,0:T(8,128)(2,1)S(1)} %bitcast.315), channel_id=1, source_target_pairs={{0,16},{8,24},{16,0},{24,8},{1,17},{9,25},{17,1},{25,9},{2,18},{10... | collective-permute-start | bytes 786440 | tf_op jit(solution)/shard_map/ppermute | solution.py:311
  119.0 2.0 collective-permute-start.9
  125.6 2.0 collective-permute-start.10
  127.8 8.4 %collective-permute-start.11 = (bf16[1,512,256]{2,1,0:T(8,128)(2,1)S(1)}, bf16[1,512,256]{2,1,0:T(8,128)(2,1)S(1)}, u32[]{:S(2)}, u32[]{:S(2)}) collective-permute-start(bf16[1,512,256]{2,1,0:T(8,128)(2,1)S(1)} %dynamic-slice_convert_fusion.6), channel_id=1, source_target_pairs={{0,16},{8,24},{16,0},{24,8},{1,17},{9,25},{17,1},{25,9},{2,18},{10... | collective-permute-start | bytes 786440 | tf_op jit(solution)/shard_map/ppermute | solution.py:290
  129.7 22.2 %collective-permute-start.15 = (bf16[16,112,256]{2,1,0:T(8,128)(2,1)S(1)}, bf16[16,112,256]{2,1,0:T(8,128)(2,1)S(1)}, u32[]{:S(2)}, u32[]{:S(2)}) collective-permute-start(bf16[16,112,256]{2,1,0:T(8,128)(2,1)S(1)} %get-tuple-element.134), channel_id=1, source_target_pairs={{0,1},{1,0},{2,3},{3,2},{4,5},{5,4},{6,7},{7,6},{8,9},{9,8},{10,11... | collective-permute-start | bytes 2752520 | tf_op jit(solution)/shard_map/ppermute | solution.py:280
  137.2 7.5 %collective-permute-start.12 = (bf16[1,512,256]{2,1,0:T(8,128)(2,1)S(1)}, bf16[1,512,256]{2,1,0:T(8,128)(2,1)S(1)}, u32[]{:S(2)}, u32[]{:S(2)}) collective-permute-start(bf16[1,512,256]{2,1,0:T(8,128)(2,1)S(1)} %bitcast.312), channel_id=1, source_target_pairs={{0,16},{8,24},{16,0},{24,8},{1,17},{9,25},{17,1},{25,9},{2,18},{10... | collective-permute-start | bytes 786440 | tf_op jit(solution)/shard_map/ppermute | solution.py:311
  144.8 8.7 %collective-permute-start.13 = (bf16[2,512,256]{2,1,0:T(8,128)(2,1)S(1)}, bf16[2,512,256]{2,1,0:T(8,128)(2,1)S(1)}, u32[]{:S(2)}, u32[]{:S(2)}) collective-permute-start(bf16[2,512,256]{2,1,0:T(8,128)(2,1)S(1)} %maximum_select_fusion.9), channel_id=1, source_target_pairs={{0,8},{8,0},{16,24},{24,16},{1,9},{9,1},{17,25},{25,17},{2,10},{10... | collective-permute-start | bytes 1572872 | tf_op jit(solution)/shard_map/ppermute | solution.py:311
  156.0 46.8 %collective-permute-start.18 = (bf16[2,128]{1,0:T(2,128)(2,1)S(1)}, bf16[2,128]{1,0:T(2,128)(2,1)S(1)}, u32[]{:S(2)}, u32[]{:S(2)}) collective-permute-start(bf16[2,128]{1,0:T(2,128)(2,1)S(1)} %fusion.54), channel_id=1, source_target_pairs={{0,1},{1,0},{2,3},{3,2},{4,5},{5,4},{6,7},{7,6},{8,9},{9,8},{10,11... | collective-permute-start | bytes 1544 | tf_op jit(solution)/shard_map/ppermute | solution.py:252
  163.4 27.8 %copy-start.14 = (f32[256,256]{1,0:T(8,128)S(1)}, f32[256,256]{1,0:T(8,128)}, u32[]{:S(2)}) copy-start(f32[256,256]{1,0:T(8,128)} %fusion.61) | copy-start | bytes 786436
  192.5 10.4 %collective-permute-start.17 = (bf16[128,256]{1,0:T(8,128)(2,1)S(1)}, bf16[128,256]{1,0:T(8,128)(2,1)S(1)}, u32[]{:S(2)}, u32[]{:S(2)}) collective-permute-start(bf16[128,256]{1,0:T(8,128)(2,1)S(1)} %fusion.45), channel_id=1, source_target_pairs={{0,1},{1,0},{2,3},{3,2},{4,5},{5,4},{6,7},{7,6},{8,9},{9,8},{10,11... | collective-permute-start | bytes 196616 | tf_op jit(solution)/shard_map/ppermute | solution.py:252
  194.0 8.8 %collective-permute-start.19 = (bf16[128,512]{1,0:T(8,128)(2,1)S(1)}, bf16[128,512]{1,0:T(8,128)(2,1)S(1)}, u32[]{:S(2)}, u32[]{:S(2)}) collective-permute-start(bf16[128,512]{1,0:T(8,128)(2,1)S(1)} %dynamic-slice_bitcast_fusion.4), channel_id=1, source_target_pairs={{0,1},{1,0},{2,3},{3,2},{4,5},{5,4},{6,7},{7,6},{8,9},{9,8},{10,11... | collective-permute-start | bytes 393224 | tf_op jit(solution)/shard_map/ppermute | solution.py:272
  197.3 6.5 %collective-permute-start.20 = (bf16[128,512]{1,0:T(8,128)(2,1)S(1)}, bf16[128,512]{1,0:T(8,128)(2,1)S(1)}, u32[]{:S(2)}, u32[]{:S(2)}) collective-permute-start(bf16[128,512]{1,0:T(8,128)(2,1)S(1)} %dynamic-slice_bitcast_fusion.3), channel_id=1, source_target_pairs={{0,1},{1,0},{2,3},{3,2},{4,5},{5,4},{6,7},{7,6},{8,9},{9,8},{10,11... | collective-permute-start | bytes 393224 | tf_op jit(solution)/shard_map/ppermute | solution.py:272
  199.0 22.5 %collective-permute-start.14 = (bf16[16,112,256]{2,1,0:T(8,128)(2,1)S(1)}, bf16[16,112,256]{2,1,0:T(8,128)(2,1)S(1)}, u32[]{:S(2)}, u32[]{:S(2)}) collective-permute-start(bf16[16,112,256]{2,1,0:T(8,128)(2,1)S(1)} %get-tuple-element.136), channel_id=1, source_target_pairs={{0,1},{1,0},{2,3},{3,2},{4,5},{5,4},{6,7},{7,6},{8,9},{9,8},{10,11... | collective-permute-start | bytes 2752520 | tf_op jit(solution)/shard_map/ppermute | solution.py:280
  202.8 25.2 %collective-permute-start.16 = (bf16[2,8,64,1024]{3,2,1,0:T(8,128)(2,1)}, bf16[2,8,64,1024]{3,2,1,0:T(8,128)(2,1)}, u32[]{:S(2)}, u32[]{:S(2)}) collective-permute-start(bf16[2,8,64,1024]{3,2,1,0:T(8,128)(2,1)} %dynamic-slice_bitcast_fusion), channel_id=1, source_target_pairs={{0,8},{8,0},{16,24},{24,16},{1,9},{9,1},{17,25},{25,17},{2,10},{10... | collective-permute-start | bytes 6291464 | tf_op jit(solution)/shard_map/ppermute | solution.py:290
  202.9 19.0 %copy-start.3 = (f32[1024,256]{1,0:T(8,128)S(1)}, f32[1024,256]{1,0:T(8,128)}, u32[]{:S(2)}) copy-start(f32[1024,256]{1,0:T(8,128)} %convolution_bitcast_fusion) | copy-start | bytes 3145732
  231.2 20.3 %collective-permute-start.22 = (bf16[1,2,128,512]{3,2,1,0:T(8,128)(2,1)S(1)}, bf16[1,2,128,512]{3,2,1,0:T(8,128)(2,1)}, u32[]{:S(2)}, u32[]{:S(2)}) collective-permute-start(bf16[1,2,128,512]{3,2,1,0:T(8,128)(2,1)S(1)} %bitcast.333), channel_id=1, source_target_pairs={{0,16},{8,24},{16,0},{24,8},{1,17},{9,25},{17,1},{25,9},{2,18},{10... | collective-permute-start | bytes 786440 | tf_op jit(solution)/shard_map/ppermute | solution.py:311
  231.3 21.3 %collective-permute-start.23 = (bf16[1,2,128,512]{3,2,1,0:T(8,128)(2,1)}, bf16[1,2,128,512]{3,2,1,0:T(8,128)(2,1)}, u32[]{:S(2)}, u32[]{:S(2)}) collective-permute-start(bf16[1,2,128,512]{3,2,1,0:T(8,128)(2,1)} %bitcast.98), channel_id=1, source_target_pairs={{0,16},{8,24},{16,0},{24,8},{1,17},{9,25},{17,1},{25,9},{2,18},{10... | collective-permute-start | bytes 786440 | tf_op jit(solution)/shard_map/ppermute | solution.py:311
  233.3 21.5 %collective-permute-start.21 = (bf16[2,290,256]{2,1,0:T(8,128)(2,1)S(1)}, bf16[2,290,256]{2,1,0:T(8,128)(2,1)S(1)}, u32[]{:S(2)}, u32[]{:S(2)}) collective-permute-start(bf16[2,290,256]{2,1,0:T(8,128)(2,1)S(1)} %fusion.42), channel_id=1, source_target_pairs={{0,2},{2,0},{4,6},{6,4},{1,3},{3,1},{5,7},{7,5},{8,10},{10,8},{12,... | collective-permute-start | bytes 890888 | tf_op jit(solution)/shard_map/ppermute | solution.py:290
  235.1 30.7 %collective-permute-start.24 = (bf16[1,8,64,1024]{3,2,1,0:T(8,128)(2,1)S(1)}, bf16[1,8,64,1024]{3,2,1,0:T(8,128)(2,1)}, u32[]{:S(2)}, u32[]{:S(2)}) collective-permute-start(bf16[1,8,64,1024]{3,2,1,0:T(8,128)(2,1)S(1)} %dynamic-slice_convert_fusion), channel_id=1, source_target_pairs={{0,16},{8,24},{16,0},{24,8},{1,17},{9,25},{17,1},{25,9},{2,18},{10... | collective-permute-start | bytes 3145736 | tf_op jit(solution)/shard_map/ppermute | solution.py:290
  252.6 36.4 %copy-start.8 = (bf16[2,2,128,512]{3,2,1,0:T(8,128)(2,1)}, bf16[2,2,128,512]{3,2,1,0:T(8,128)(2,1)S(1)}, u32[]{:S(2)}) copy-start(bf16[2,2,128,512]{3,2,1,0:T(8,128)(2,1)S(1)} %maximum_select_fusion.10) | copy-start | bytes 1572868
  267.4 16.2 %copy-start.20 = (f32[9,1024]{1,0:T(8,128)S(1)}, f32[9,1024]{1,0:T(8,128)}, u32[]{:S(2)}) copy-start(f32[9,1024]{1,0:T(8,128)} %get-tuple-element.91) | copy-start | bytes 110596
  267.4 16.2 %copy-start.24 = (f32[9,512]{1,0:T(8,128)S(1)}, f32[9,512]{1,0:T(8,128)}, u32[]{:S(2)}) copy-start(f32[9,512]{1,0:T(8,128)} %get-tuple-element.92) | copy-start | bytes 55300
  267.4 22.0 %copy-start.4 = (bf16[32,64,512]{2,1,0:T(8,128)(2,1)S(1)}, bf16[32,64,512]{2,1,0:T(8,128)(2,1)}, u32[]{:S(2)}) copy-start(bf16[32,64,512]{2,1,0:T(8,128)(2,1)} %get-tuple-element.88) | copy-start | bytes 6291460
  284.6 9.0 %collective-permute-start.31 = (f32[9,1024]{1,0:T(8,128)S(1)}, f32[9,1024]{1,0:T(8,128)S(1)}, u32[]{:S(2)}, u32[]{:S(2)}) collective-permute-start(f32[9,1024]{1,0:T(8,128)S(1)} %fusion.46), channel_id=1, source_target_pairs={{0,2},{2,0},{4,6},{6,4},{1,3},{3,1},{5,7},{7,5},{8,10},{10,8},{12,... | collective-permute-start | bytes 110600 | tf_op jit(solution)/shard_map/ppermute | solution.py:322
  286.2 8.0 %collective-permute-start.33 = (bf16[1,290,256]{2,1,0:T(8,128)(2,1)S(1)}, bf16[1,290,256]{2,1,0:T(8,128)(2,1)S(1)}, u32[]{:S(2)}, u32[]{:S(2)}) collective-permute-start(bf16[1,290,256]{2,1,0:T(8,128)(2,1)S(1)} %dynamic-slice_convert_fusion.8), channel_id=1, source_target_pairs={{0,4},{2,6},{4,0},{6,2},{1,5},{3,7},{5,1},{7,3},{8,12},{10,14},{12... | collective-permute-start | bytes 445448 | tf_op jit(solution)/shard_map/ppermute | solution.py:290
  288.9 21.1 %collective-permute-start.25 = (bf16[2,2,128,512]{3,2,1,0:T(8,128)(2,1)S(1)}, bf16[2,2,128,512]{3,2,1,0:T(8,128)(2,1)S(1)}, u32[]{:S(2)}, u32[]{:S(2)}) collective-permute-start(bf16[2,2,128,512]{3,2,1,0:T(8,128)(2,1)S(1)} %maximum_select_fusion.10), channel_id=1, source_target_pairs={{0,8},{8,0},{16,24},{24,16},{1,9},{9,1},{17,25},{25,17},{2,10},{10... | collective-permute-start | bytes 1572872 | tf_op jit(solution)/shard_map/ppermute | solution.py:311
  289.0 26.2 %collective-permute-start.26 = (bf16[2,2,128,512]{3,2,1,0:T(8,128)(2,1)}, bf16[2,2,128,512]{3,2,1,0:T(8,128)(2,1)}, u32[]{:S(2)}, u32[]{:S(2)}) collective-permute-start(bf16[2,2,128,512]{3,2,1,0:T(8,128)(2,1)} %maximum_select_fusion.11), channel_id=1, source_target_pairs={{0,8},{8,0},{16,24},{24,16},{1,9},{9,1},{17,25},{25,17},{2,10},{10... | collective-permute-start | bytes 1572872 | tf_op jit(solution)/shard_map/ppermute | solution.py:311
  291.7 41.8 %collective-permute-start.29 = (bf16[2,8,64,512]{3,2,1,0:T(8,128)(2,1)}, bf16[2,8,64,512]{3,2,1,0:T(8,128)(2,1)}, u32[]{:S(2)}, u32[]{:S(2)}) collective-permute-start(bf16[2,8,64,512]{3,2,1,0:T(8,128)(2,1)} %dynamic-slice_bitcast_fusion.1), channel_id=1, source_target_pairs={{0,8},{8,0},{16,24},{24,16},{1,9},{9,1},{17,25},{25,17},{2,10},{10... | collective-permute-start | bytes 3145736 | tf_op jit(solution)/shard_map/ppermute | solution.py:290
  293.6 16.5 %copy-start.9 = (bf16[2,2,128,512]{3,2,1,0:T(8,128)(2,1)S(1)}, bf16[2,2,128,512]{3,2,1,0:T(8,128)(2,1)}, u32[]{:S(2)}) copy-start(bf16[2,2,128,512]{3,2,1,0:T(8,128)(2,1)} %copy-done.8) | copy-start | bytes 1572868
  293.6 42.3 %collective-permute-start.27 = (bf16[2,8,64,512]{3,2,1,0:T(8,128)(2,1)}, bf16[2,8,64,512]{3,2,1,0:T(8,128)(2,1)}, u32[]{:S(2)}, u32[]{:S(2)}) collective-permute-start(bf16[2,8,64,512]{3,2,1,0:T(8,128)(2,1)} %dynamic-slice_bitcast_fusion.2), channel_id=1, source_target_pairs={{0,8},{8,0},{16,24},{24,16},{1,9},{9,1},{17,25},{25,17},{2,10},{10... | collective-permute-start | bytes 3145736 | tf_op jit(solution)/shard_map/ppermute | solution.py:290
  294.2 6.2 %collective-permute-start.32 = (f32[9,1024]{1,0:T(8,128)S(1)}, f32[9,1024]{1,0:T(8,128)S(1)}, u32[]{:S(2)}, u32[]{:S(2)}) collective-permute-start(f32[9,1024]{1,0:T(8,128)S(1)} %add.374), channel_id=1, source_target_pairs={{0,4},{2,6},{4,0},{6,2},{1,5},{3,7},{5,1},{7,3},{8,12},{10,14},{12... | collective-permute-start | bytes 110600 | tf_op jit(solution)/shard_map/ppermute | solution.py:322
  300.4 8.2 %collective-permute-start.34 = (bf16[1,290,256]{2,1,0:T(8,128)(2,1)S(1)}, bf16[1,290,256]{2,1,0:T(8,128)(2,1)S(1)}, u32[]{:S(2)}, u32[]{:S(2)}) collective-permute-start(bf16[1,290,256]{2,1,0:T(8,128)(2,1)S(1)} %add_convert_fusion.2), channel_id=1, source_target_pairs={{0,4},{2,6},{4,0},{6,2},{1,5},{3,7},{5,1},{7,3},{8,12},{10,14},{12... | collective-permute-start | bytes 445448 | tf_op jit(solution)/shard_map/ppermute | solution.py:311
  309.3 18.3 %collective-permute-start.35 = (bf16[2,290,256]{2,1,0:T(8,128)(2,1)}, bf16[2,290,256]{2,1,0:T(8,128)(2,1)S(1)}, u32[]{:S(2)}, u32[]{:S(2)}) collective-permute-start(bf16[2,290,256]{2,1,0:T(8,128)(2,1)} %maximum_select_fusion.13), channel_id=1, source_target_pairs={{0,2},{2,0},{4,6},{6,4},{1,3},{3,1},{5,7},{7,5},{8,10},{10,8},{12,... | collective-permute-start | bytes 890888 | tf_op jit(solution)/shard_map/ppermute | solution.py:311
  335.6 14.8 %collective-permute-start.30 = (bf16[1,8,64,512]{3,2,1,0:T(8,128)(2,1)S(1)}, bf16[1,8,64,512]{3,2,1,0:T(8,128)(2,1)S(1)}, u32[]{:S(2)}, u32[]{:S(2)}) collective-permute-start(bf16[1,8,64,512]{3,2,1,0:T(8,128)(2,1)S(1)} %dynamic-slice_convert_fusion.3), channel_id=1, source_target_pairs={{0,16},{8,24},{16,0},{24,8},{1,17},{9,25},{17,1},{25,9},{2,18},{10... | collective-permute-start | bytes 1572872 | tf_op jit(solution)/shard_map/ppermute | solution.py:290
  337.6 23.2 %collective-permute-start.28 = (bf16[1,8,64,512]{3,2,1,0:T(8,128)(2,1)S(1)}, bf16[1,8,64,512]{3,2,1,0:T(8,128)(2,1)S(1)}, u32[]{:S(2)}, u32[]{:S(2)}) collective-permute-start(bf16[1,8,64,512]{3,2,1,0:T(8,128)(2,1)S(1)} %dynamic-slice_convert_fusion.4), channel_id=1, source_target_pairs={{0,16},{8,24},{16,0},{24,8},{1,17},{9,25},{17,1},{25,9},{2,18},{10... | collective-permute-start | bytes 1572872 | tf_op jit(solution)/shard_map/ppermute | solution.py:290
  (18 other events, 73.3 us)

commit v4 on v3

--- a/solution.py
+++ b/solution.py
@@ -437,6 +437,7 @@
         term, dw = backward_call(scals[-1], last, weight, taps, firsts[-1][1], margin, wing, cut, cuts)
         dw_last.append(dw)
     final.append(first_step(term))
+    spreads, shared, final = lax.optimization_barrier((spreads, shared, final))
     summed.append([halving_rest(part, "section", 2) for part in final])
     shared = halving_rest(shared, "dp", 2).astype(jnp.bfloat16)
     shared = doubling_gather(shared, "dp").reshape(-1, branch).astype(jnp.float32)

time: 371 us -> 352 us (0.949)
  waiting for transfers between devices: 97.6 us -> 77.5 us
    ppermute x12, waiting for transfers between devices: 41 us -> 29.7 us  [halving_step(): got = lax.ppermute(sent, axis, [(i, i ^ bit) for i in range(size)])]
    ppermute x10, waiting for transfers between devices: 17.3 us -> 12.9 us  [doubling_gather(): got = lax.ppermute(block, axis, [(i, i ^ bit) for i in range(size)])]
    ppermute x2, waiting for transfers between devices: 5.19 us -> 0.81 us  [butterfly_sum(): lax.ppermute(value, axis, [(i, i ^ bit) for i in range(size)])]
  transfers between devices with their start and end apart: 36 -> 36, of which waited for: 15 -> 15; matrix products, arithmetic and copies ran while one was open for 29% -> 31% of each run, Pallas kernels for 24% -> 25%
where the time goes in v4:
time: 352 us; the launch traced here: 347 us
  Pallas kernels  103 us (29%)
  waiting for transfers between devices  77.5 us (22%)
  local copies, waits for them, and re-layouts  55.9 us (16%)
  other arithmetic  54.9 us (16%)
  starting transfers between devices  33.5 us (10%)
  matrix products  16.7 us (5%)
  between operations  4.67 us (1%)
    pallas_call x3, Pallas kernels, backward_call(): pl.pallas_call(lambda *refs: backward_kernel(*refs, margin=margin, wing=w...  60.1 us
    pallas_call x2, Pallas kernels, forward_call(): pl.pallas_call(lambda *refs: forward_kernel(*refs, margin=margin, wing=wi...  43.3 us
    ppermute x12, waiting for transfers between devices, halving_step(): got = lax.ppermute(sent, axis, [(i, i ^ bit) for i in range(size)])  29.7 us
    ppermute x4, waiting for transfers between devices, gather(): got = lax.ppermute(block, axis, [(0, 1), (1, 0)])  23.5 us
    ppermute x10, waiting for transfers between devices, doubling_gather(): got = lax.ppermute(block, axis, [(i, i ^ bit) for i in range(size)])  12.9 us
    dot_general x2, matrix products, local(): lax.dot_general(firsts[f][0].reshape(rows * ext, chans), grads[f].reshape...  12.7 us
    ppermute x12, starting transfers between devices, halving_step(): got = lax.ppermute(sent, axis, [(i, i ^ bit) for i in range(size)])  9.96 us
    ppermute x4, waiting for transfers between devices, owner_terms(): lax.ppermute(sent, axis, [(i, (i + k) % size) for i in range(size)])  9.67 us
  transfers between devices with their start and end apart: 36, of which 15 were waited for; matrix products, arithmetic and copies ran while one was open for 31% of the time, Pallas kernels for 25%

profile of v4, /device:TPU:0, one launch (start us, length us, event | category | flops | bytes accessed | tf_op | source)
XLA Modules:
  0.0 346.6 jit_solution(2580755072760090820)
XLA Ops:
  1.3 3.0 collective-permute-start.2
  7.0 3.2 pad_add_fusion
  10.2 21.3 %depth_pointwise.2 = (bf16[32,112,1024]{2,1,0:T(8,128)(2,1)}, bf16[32,64,1024]{2,1,0:T(8,128)(2,1)}, f32[3584,256]{1,0:T(8,128)}) custom-call(s32[4]{0:T(128)} %get-tuple-element.160.refs_0_, bf16[2,32,128,1024]{3,2,1,0:T(8,128)(2,1)} %refs_1_.3, bf16[9,1024]{1,0:T(8,128)(2,1)} %bitcast.372, bf16[1024,256]{1,0:T(8,128)(2,1)} %bitcast.367), custom_call_target="tpu_custom_call" | custom-call | flops 23907532800 | bytes 19922944 | tf_op jit(solution)/shard_map/depth_pointwise/pallas_call | solution.py:113
  31.5 2.5 fusion.30
  34.1 2.0 collective-permute-start.3
  36.7 3.5 %copy.69 = bf16[128,2,32,128]{0,3,2,1:T(8,128)(2,1)S(1)} copy(bf16[128,2,32,128]{3,2,1,0:T(8,128)(2,1)} %param.19) | data formatting | bytes 4194304 | tf_op jit(solution)/shard_map/optimization_barrier | solution.py:362
  41.4 2.0 fusion.27
  46.5 2.0 collective-permute-start.7
  49.8 22.0 %depth_pointwise.3 = (bf16[32,112,1024]{2,1,0:T(8,128)(2,1)}, bf16[32,64,1024]{2,1,0:T(8,128)(2,1)}, f32[3584,256]{1,0:T(8,128)}) custom-call(s32[4]{0:T(128)} %get-tuple-element.58.refs_0_, bf16[2,32,128,1024]{3,2,1,0:T(8,128)(2,1)} %refs_1_.3, bf16[9,1024]{1,0:T(8,128)(2,1)} %bitcast.373, bf16[1024,256]{1,0:T(8,128)(2,1)} %bitcast.368), custom_call_target="tpu_custom_call" | custom-call | flops 23907532800 | bytes 19922944 | tf_op jit(solution)/shard_map/depth_pointwise/pallas_call | solution.py:113
  81.2 2.6 fusion.31
  86.1 3.0 collective-permute-start.5
  91.0 2.1 copy.98
  93.0 3.1 collective-permute-done.5
  97.2 9.7 %collective-permute-done.6 = bf16[1792,256]{1,0:T(8,128)(2,1)} collective-permute-done((bf16[1792,256]{1,0:T(8,128)(2,1)}, bf16[1792,256]{1,0:T(8,128)(2,1)}, u32[]{:S(2)}, u32[]{:S(2)}) %collective-permute-start.6) | collective-permute-done | bytes 917536 | tf_op jit(solution)/shard_map/ppermute | solution.py:252
  106.8 2.0 multiply_convert_fusion.5
  108.8 2.6 collective-permute-start.8
  114.5 3.1 collective-permute-done.8
  126.5 1.8 collective-permute-start.11
  129.0 5.9 %collective-permute-done.11 = bf16[1,512,256]{2,1,0:T(8,128)(2,1)S(1)} collective-permute-done((bf16[1,512,256]{2,1,0:T(8,128)(2,1)S(1)}, bf16[1,512,256]{2,1,0:T(8,128)(2,1)S(1)}, u32[]{:S(2)}, u32[]{:S(2)}) %collective-permute-start.11) | collective-permute-done | bytes 262176 | tf_op jit(solution)/shard_map/ppermute | solution.py:290
  135.9 1.7 collective-permute-start.12
  138.8 4.6 %collective-permute-done.12 = bf16[1,512,256]{2,1,0:T(8,128)(2,1)S(1)} collective-permute-done((bf16[1,512,256]{2,1,0:T(8,128)(2,1)S(1)}, bf16[1,512,256]{2,1,0:T(8,128)(2,1)S(1)}, u32[]{:S(2)}, u32[]{:S(2)}) %collective-permute-start.12) | collective-permute-done | bytes 262176 | tf_op jit(solution)/shard_map/ppermute | solution.py:311
  144.1 6.5 %collective-permute-done.15 = bf16[16,112,256]{2,1,0:T(8,128)(2,1)S(1)} collective-permute-done((bf16[16,112,256]{2,1,0:T(8,128)(2,1)S(1)}, bf16[16,112,256]{2,1,0:T(8,128)(2,1)S(1)}, u32[]{:S(2)}, u32[]{:S(2)}) %collective-permute-start.15) | collective-permute-done | bytes 917536 | tf_op jit(solution)/shard_map/ppermute | solution.py:280
  155.2 6.9 %convolution_bitcast_fusion = f32[1024,256]{1,0:T(8,128)} fusion(bf16[32,112,1024]{2,1,0:T(8,128)(2,1)} %get-tuple-element.73, bf16[32,112,256]{2,1,0:T(8,128)(2,1)} %bitcast.294), kind=kOutput, calls=%fused_computation.66 | convolution fusion | flops 1879048192 | bytes 10223616 | tf_op jit(solution)/shard_map/dot_general | solution.py:399
  162.1 27.8 %depth_gradients.3 = (bf16[32,64,1024]{2,1,0:T(8,128)(2,1)}, f32[9,1024]{1,0:T(8,128)}) custom-call(s32[4]{0:T(128)} %get-tuple-element.160.refs_0_, bf16[32,112,256]{2,1,0:T(8,128)(2,1)} %bitcast.295, bf16[1024,256]{1,0:T(8,128)(2,1)} %bitcast.369, bf16[9,1024]{1,0:T(8,128)(2,1)} %bitcast.374, bf16[32,64,1024]{2,1,0:T(8,128)(2,1)} %get-tuple-element.71.refs_4_), custom_call_target="tpu_custom_call" | custom-call | flops 31876710400 | bytes 16777216 | tf_op jit(solution)/shard_map/depth_gradients/pallas_call | solution.py:211
  193.3 1.8 copy.100
  198.3 3.2 dynamic-slice_bitcast_fusion
  203.2 17.1 %collective-permute-done.14 = bf16[16,112,256]{2,1,0:T(8,128)(2,1)S(1)} collective-permute-done((bf16[16,112,256]{2,1,0:T(8,128)(2,1)S(1)}, bf16[16,112,256]{2,1,0:T(8,128)(2,1)S(1)}, u32[]{:S(2)}, u32[]{:S(2)}) %collective-permute-start.14) | collective-permute-done | bytes 917536 | tf_op jit(solution)/shard_map/ppermute | solution.py:280
  220.6 5.9 %convolution_add_fusion = f32[1024,256]{1,0:T(8,128)S(1)} fusion(f32[1024,256]{1,0:T(8,128)S(1)} %copy-done.6, bf16[3584,1024]{1,0:T(8,128)(2,1)} %bitcast.296, bf16[3584,256]{1,0:T(8,128)(2,1)S(1)} %bitcast.299), kind=kOutput, calls=%fused_computation.67 | convolution fusion | flops 1879310336 | bytes 11272192 | tf_op jit(solution)/shard_map/dot_general | solution.py:399
  226.7 3.2 convert_add_fusion
  230.0 2.0 collective-permute-start.23
  234.0 16.2 %depth_gradients.4 = (bf16[32,64,512]{2,1,0:T(8,128)(2,1)}, f32[9,512]{1,0:T(8,128)}) custom-call(s32[4]{0:T(128)} %get-tuple-element.58.refs_0_, bf16[32,112,256]{2,1,0:T(8,128)(2,1)} %bitcast.300, bf16[1024,256]{1,0:T(8,128)(2,1)} %bitcast.370, bf16[9,1024]{1,0:T(8,128)(2,1)} %bitcast.375, bf16[32,64,1024]{2,1,0:T(8,128)(2,1)} %get-tuple-element.88.refs_4_), custom_call_target="tpu_custom_call" | custom-call | flops 15938355200 | bytes 8388608 | tf_op jit(solution)/shard_map/depth_gradients/pallas_call | solution.py:211
  251.3 2.3 maximum_select_fusion.11
  253.7 10.8 %collective-permute-done.24 = bf16[1,8,64,1024]{3,2,1,0:T(8,128)(2,1)} collective-permute-done((bf16[1,8,64,1024]{3,2,1,0:T(8,128)(2,1)S(1)}, bf16[1,8,64,1024]{3,2,1,0:T(8,128)(2,1)}, u32[]{:S(2)}, u32[]{:S(2)}) %collective-permute-start.24) | collective-permute-done | bytes 1048608 | tf_op jit(solution)/shard_map/ppermute | solution.py:290
  266.1 16.0 %depth_gradients.5 = (bf16[32,64,512]{2,1,0:T(8,128)(2,1)}, f32[9,512]{1,0:T(8,128)}) custom-call(s32[4]{0:T(128)} %get-tuple-element.58.refs_0_, bf16[32,112,256]{2,1,0:T(8,128)(2,1)} %bitcast.301, bf16[1024,256]{1,0:T(8,128)(2,1)} %bitcast.371, bf16[9,1024]{1,0:T(8,128)(2,1)} %bitcast.376, bf16[32,64,1024]{2,1,0:T(8,128)(2,1)} %get-tuple-element.88.refs_4_), custom_call_target="tpu_custom_call" | custom-call | flops 15938355200 | bytes 8388608 | tf_op jit(solution)/shard_map/depth_gradients/pallas_call | solution.py:211
  282.2 2.4 dynamic-slice_bitcast_fusion.1
  287.6 1.6 collective-permute-start.31
  292.0 2.7 collective-permute-start.32
  296.3 2.3 convert_add_fusion.2
  299.9 7.5 %collective-permute-done.33 = bf16[1,290,256]{2,1,0:T(8,128)(2,1)S(1)} collective-permute-done((bf16[1,290,256]{2,1,0:T(8,128)(2,1)S(1)}, bf16[1,290,256]{2,1,0:T(8,128)(2,1)S(1)}, u32[]{:S(2)}, u32[]{:S(2)}) %collective-permute-start.33) | collective-permute-done | bytes 148512 | tf_op jit(solution)/shard_map/ppermute | solution.py:290
  309.4 1.8 collective-permute-start.29
  311.2 4.2 %collective-permute-done.34 = bf16[1,290,256]{2,1,0:T(8,128)(2,1)S(1)} collective-permute-done((bf16[1,290,256]{2,1,0:T(8,128)(2,1)S(1)}, bf16[1,290,256]{2,1,0:T(8,128)(2,1)S(1)}, u32[]{:S(2)}, u32[]{:S(2)}) %collective-permute-start.34) | collective-permute-done | bytes 148512 | tf_op jit(solution)/shard_map/ppermute | solution.py:311
  317.7 2.0 fusion.25
  319.7 1.7 copy.90
  321.4 1.7 maximum_select_fusion.5
  325.8 1.7 fusion.24
  327.6 2.8 copy.93
  338.2 2.1 copy.94
  340.2 2.4 pad_maximum_fusion
  (224 shorter events, 81.7 us)
Async XLA Ops:
  1.3 47.9 %collective-permute-start.2 = (f32[2,128]{1,0:T(2,128)S(1)}, f32[2,128]{1,0:T(2,128)S(1)}, u32[]{:S(2)}, u32[]{:S(2)}) collective-permute-start(f32[2,128]{1,0:T(2,128)S(1)} %get-tuple-element.154), channel_id=1, source_target_pairs={{0,1},{1,0},{2,3},{3,2},{4,5},{5,4},{6,7},{7,6},{8,9},{9,8},{10,11... | collective-permute-start | bytes 3080 | tf_op jit(solution)/shard_map/ppermute | solution.py:280
  4.3 45.5 %collective-permute-start.1 = (bf16[128,256]{1,0:T(8,128)(2,1)}, bf16[128,256]{1,0:T(8,128)(2,1)S(1)}, u32[]{:S(2)}, u32[]{:S(2)}) collective-permute-start(bf16[128,256]{1,0:T(8,128)(2,1)} %bitcast.352), channel_id=1, source_target_pairs={{0,1},{1,0},{2,3},{3,2},{4,5},{5,4},{6,7},{7,6},{8,9},{9,8},{10,11... | collective-permute-start | bytes 196616 | tf_op jit(solution)/shard_map/ppermute | solution.py:280
  34.1 37.7 %collective-permute-start.3 = (bf16[1792,256]{1,0:T(8,128)(2,1)}, bf16[1792,256]{1,0:T(8,128)(2,1)}, u32[]{:S(2)}, u32[]{:S(2)}) collective-permute-start(bf16[1792,256]{1,0:T(8,128)(2,1)} %fusion.30), channel_id=1, source_target_pairs={{0,1},{1,0},{2,3},{3,2},{4,5},{5,4},{6,7},{7,6},{8,9},{9,8},{10,11... | collective-permute-start | bytes 2752520 | tf_op jit(solution)/shard_map/ppermute | solution.py:252
  44.2 67.3 %collective-permute-start = (bf16[128,512]{1,0:T(8,128)(2,1)}, bf16[128,512]{1,0:T(8,128)(2,1)}, u32[]{:S(2)}, u32[]{:S(2)}) collective-permute-start(bf16[128,512]{1,0:T(8,128)(2,1)} %bitcast.8), channel_id=1, source_target_pairs={{0,1},{1,0},{2,3},{3,2},{4,5},{5,4},{6,7},{7,6},{8,9},{9,8},{10,11... | collective-permute-start | bytes 393224 | tf_op jit(solution)/shard_map/ppermute | solution.py:272
  46.5 42.7 %collective-permute-start.7 = (bf16[128,512]{1,0:T(8,128)(2,1)}, bf16[128,512]{1,0:T(8,128)(2,1)}, u32[]{:S(2)}, u32[]{:S(2)}) collective-permute-start(bf16[128,512]{1,0:T(8,128)(2,1)} %bitcast.37), channel_id=1, source_target_pairs={{0,1},{1,0},{2,3},{3,2},{4,5},{5,4},{6,7},{7,6},{8,9},{9,8},{10,11... | collective-permute-start | bytes 393224 | tf_op jit(solution)/shard_map/ppermute | solution.py:272
  49.8 23.4 %copy-start.26 = (f32[2,1,128]{2,1,0:T(1,128)}, f32[2,1,128]{2,1,0:T(1,128)S(1)}, u32[]{:S(2)}) copy-start(f32[2,1,128]{2,1,0:T(1,128)S(1)} %get-tuple-element.152) | copy-start | bytes 3076
  49.8 22.0 %copy-start.13 = (f32[3584,256]{1,0:T(8,128)S(1)}, f32[3584,256]{1,0:T(8,128)}, u32[]{:S(2)}) copy-start(f32[3584,256]{1,0:T(8,128)} %get-tuple-element.56) | copy-start | bytes 11010052
  75.5 8.4 %collective-permute-start.4 = (bf16[2,512,256]{2,1,0:T(8,128)(2,1)S(1)}, bf16[2,512,256]{2,1,0:T(8,128)(2,1)}, u32[]{:S(2)}, u32[]{:S(2)}) collective-permute-start(bf16[2,512,256]{2,1,0:T(8,128)(2,1)S(1)} %fusion.33), channel_id=1, source_target_pairs={{0,8},{8,0},{16,24},{24,16},{1,9},{9,1},{17,25},{25,17},{2,10},{10... | collective-permute-start | bytes 1572872 | tf_op jit(solution)/shard_map/ppermute | solution.py:290
  83.8 12.4 %copy-start.28 = (f32[2,1,128]{2,1,0:T(1,128)S(1)}, f32[2,1,128]{2,1,0:T(1,128)}, u32[]{:S(2)}) copy-start(f32[2,1,128]{2,1,0:T(1,128)} %get-tuple-element.151) | copy-start | bytes 3076
  83.8 23.1 %collective-permute-start.6 = (bf16[1792,256]{1,0:T(8,128)(2,1)}, bf16[1792,256]{1,0:T(8,128)(2,1)}, u32[]{:S(2)}, u32[]{:S(2)}) collective-permute-start(bf16[1792,256]{1,0:T(8,128)(2,1)} %fusion.31), channel_id=1, source_target_pairs={{0,1},{1,0},{2,3},{3,2},{4,5},{5,4},{6,7},{7,6},{8,9},{9,8},{10,11... | collective-permute-start | bytes 2752520 | tf_op jit(solution)/shard_map/ppermute | solution.py:252
  85.4 21.5 %copy-start.30 = (f32[1,1,512]{2,1,0:T(1,128)S(1)}, f32[1,1,512]{2,1,0:T(1,128)}, u32[]{:S(2)}) copy-start(f32[1,1,512]{2,1,0:T(1,128)} %compare_convert_fusion.1) | copy-start | bytes 6148
  86.1 10.0 %collective-permute-start.5 = (bf16[1,512,256]{2,1,0:T(8,128)(2,1)}, bf16[1,512,256]{2,1,0:T(8,128)(2,1)}, u32[]{:S(2)}, u32[]{:S(2)}) collective-permute-start(bf16[1,512,256]{2,1,0:T(8,128)(2,1)} %dynamic-slice_convert_fusion.7), channel_id=1, source_target_pairs={{0,16},{8,24},{16,0},{24,8},{1,17},{9,25},{17,1},{25,9},{2,18},{10... | collective-permute-start | bytes 786440 | tf_op jit(solution)/shard_map/ppermute | solution.py:290
  93.0 18.4 %copy-start.16 = (bf16[128,2,1,512]{3,0,2,1:T(8,128)(2,1)S(1)}, bf16[128,2,1,512]{3,0,2,1:T(8,128)(2,1)}, u32[]{:S(2)}) copy-start(bf16[128,2,1,512]{3,0,2,1:T(8,128)(2,1)} %copy.70) | copy-start | bytes 786436
  108.8 8.8 %collective-permute-start.8 = (bf16[1,512,256]{2,1,0:T(8,128)(2,1)S(1)}, bf16[1,512,256]{2,1,0:T(8,128)(2,1)S(1)}, u32[]{:S(2)}, u32[]{:S(2)}) collective-permute-start(bf16[1,512,256]{2,1,0:T(8,128)(2,1)S(1)} %bitcast.315), channel_id=1, source_target_pairs={{0,16},{8,24},{16,0},{24,8},{1,17},{9,25},{17,1},{25,9},{2,18},{10... | collective-permute-start | bytes 786440 | tf_op jit(solution)/shard_map/ppermute | solution.py:311
  117.7 2.0 collective-permute-start.9
  124.3 2.0 collective-permute-start.10
  126.4 8.5 %copy-start.29 = (f32[1,1,512]{2,1,0:T(1,128)S(1)}, f32[1,1,512]{2,1,0:T(1,128)}, u32[]{:S(2)}) copy-start(f32[1,1,512]{2,1,0:T(1,128)} %compare_convert_fusion) | copy-start | bytes 6148
  126.5 8.4 %collective-permute-start.11 = (bf16[1,512,256]{2,1,0:T(8,128)(2,1)S(1)}, bf16[1,512,256]{2,1,0:T(8,128)(2,1)S(1)}, u32[]{:S(2)}, u32[]{:S(2)}) collective-permute-start(bf16[1,512,256]{2,1,0:T(8,128)(2,1)S(1)} %dynamic-slice_convert_fusion.6), channel_id=1, source_target_pairs={{0,16},{8,24},{16,0},{24,8},{1,17},{9,25},{17,1},{25,9},{2,18},{10... | collective-permute-start | bytes 786440 | tf_op jit(solution)/shard_map/ppermute | solution.py:290
  128.4 22.2 %collective-permute-start.15 = (bf16[16,112,256]{2,1,0:T(8,128)(2,1)S(1)}, bf16[16,112,256]{2,1,0:T(8,128)(2,1)S(1)}, u32[]{:S(2)}, u32[]{:S(2)}) collective-permute-start(bf16[16,112,256]{2,1,0:T(8,128)(2,1)S(1)} %get-tuple-element.144), channel_id=1, source_target_pairs={{0,1},{1,0},{2,3},{3,2},{4,5},{5,4},{6,7},{7,6},{8,9},{9,8},{10,11... | collective-permute-start | bytes 2752520 | tf_op jit(solution)/shard_map/ppermute | solution.py:280
  135.9 7.5 %collective-permute-start.12 = (bf16[1,512,256]{2,1,0:T(8,128)(2,1)S(1)}, bf16[1,512,256]{2,1,0:T(8,128)(2,1)S(1)}, u32[]{:S(2)}, u32[]{:S(2)}) collective-permute-start(bf16[1,512,256]{2,1,0:T(8,128)(2,1)S(1)} %bitcast.312), channel_id=1, source_target_pairs={{0,16},{8,24},{16,0},{24,8},{1,17},{9,25},{17,1},{25,9},{2,18},{10... | collective-permute-start | bytes 786440 | tf_op jit(solution)/shard_map/ppermute | solution.py:311
  143.5 8.7 %collective-permute-start.13 = (bf16[2,512,256]{2,1,0:T(8,128)(2,1)S(1)}, bf16[2,512,256]{2,1,0:T(8,128)(2,1)S(1)}, u32[]{:S(2)}, u32[]{:S(2)}) collective-permute-start(bf16[2,512,256]{2,1,0:T(8,128)(2,1)S(1)} %maximum_select_fusion.9), channel_id=1, source_target_pairs={{0,8},{8,0},{16,24},{24,16},{1,9},{9,1},{17,25},{25,17},{2,10},{10... | collective-permute-start | bytes 1572872 | tf_op jit(solution)/shard_map/ppermute | solution.py:311
  154.7 46.8 %collective-permute-start.18 = (bf16[2,128]{1,0:T(2,128)(2,1)S(1)}, bf16[2,128]{1,0:T(2,128)(2,1)S(1)}, u32[]{:S(2)}, u32[]{:S(2)}) collective-permute-start(bf16[2,128]{1,0:T(2,128)(2,1)S(1)} %fusion.54), channel_id=1, source_target_pairs={{0,1},{1,0},{2,3},{3,2},{4,5},{5,4},{6,7},{7,6},{8,9},{9,8},{10,11... | collective-permute-start | bytes 1544 | tf_op jit(solution)/shard_map/ppermute | solution.py:252
  162.1 27.8 %copy-start.15 = (f32[256,256]{1,0:T(8,128)S(1)}, f32[256,256]{1,0:T(8,128)}, u32[]{:S(2)}) copy-start(f32[256,256]{1,0:T(8,128)} %fusion.61) | copy-start | bytes 786436
  191.1 10.4 %collective-permute-start.17 = (bf16[128,256]{1,0:T(8,128)(2,1)S(1)}, bf16[128,256]{1,0:T(8,128)(2,1)S(1)}, u32[]{:S(2)}, u32[]{:S(2)}) collective-permute-start(bf16[128,256]{1,0:T(8,128)(2,1)S(1)} %fusion.45), channel_id=1, source_target_pairs={{0,1},{1,0},{2,3},{3,2},{4,5},{5,4},{6,7},{7,6},{8,9},{9,8},{10,11... | collective-permute-start | bytes 196616 | tf_op jit(solution)/shard_map/ppermute | solution.py:252
  192.7 8.8 %collective-permute-start.19 = (bf16[128,512]{1,0:T(8,128)(2,1)S(1)}, bf16[128,512]{1,0:T(8,128)(2,1)S(1)}, u32[]{:S(2)}, u32[]{:S(2)}) collective-permute-start(bf16[128,512]{1,0:T(8,128)(2,1)S(1)} %dynamic-slice_bitcast_fusion.4), channel_id=1, source_target_pairs={{0,1},{1,0},{2,3},{3,2},{4,5},{5,4},{6,7},{7,6},{8,9},{9,8},{10,11... | collective-permute-start | bytes 393224 | tf_op jit(solution)/shard_map/ppermute | solution.py:272
  196.0 6.5 %collective-permute-start.20 = (bf16[128,512]{1,0:T(8,128)(2,1)S(1)}, bf16[128,512]{1,0:T(8,128)(2,1)S(1)}, u32[]{:S(2)}, u32[]{:S(2)}) collective-permute-start(bf16[128,512]{1,0:T(8,128)(2,1)S(1)} %dynamic-slice_bitcast_fusion.3), channel_id=1, source_target_pairs={{0,1},{1,0},{2,3},{3,2},{4,5},{5,4},{6,7},{7,6},{8,9},{9,8},{10,11... | collective-permute-start | bytes 393224 | tf_op jit(solution)/shard_map/ppermute | solution.py:272
  197.7 22.5 %collective-permute-start.14 = (bf16[16,112,256]{2,1,0:T(8,128)(2,1)S(1)}, bf16[16,112,256]{2,1,0:T(8,128)(2,1)S(1)}, u32[]{:S(2)}, u32[]{:S(2)}) collective-permute-start(bf16[16,112,256]{2,1,0:T(8,128)(2,1)S(1)} %get-tuple-element.146), channel_id=1, source_target_pairs={{0,1},{1,0},{2,3},{3,2},{4,5},{5,4},{6,7},{7,6},{8,9},{9,8},{10,11... | collective-permute-start | bytes 2752520 | tf_op jit(solution)/shard_map/ppermute | solution.py:280
  201.5 25.2 %collective-permute-start.16 = (bf16[2,8,64,1024]{3,2,1,0:T(8,128)(2,1)}, bf16[2,8,64,1024]{3,2,1,0:T(8,128)(2,1)}, u32[]{:S(2)}, u32[]{:S(2)}) collective-permute-start(bf16[2,8,64,1024]{3,2,1,0:T(8,128)(2,1)} %dynamic-slice_bitcast_fusion), channel_id=1, source_target_pairs={{0,8},{8,0},{16,24},{24,16},{1,9},{9,1},{17,25},{25,17},{2,10},{10... | collective-permute-start | bytes 6291464 | tf_op jit(solution)/shard_map/ppermute | solution.py:290
  201.6 19.0 %copy-start.6 = (f32[1024,256]{1,0:T(8,128)S(1)}, f32[1024,256]{1,0:T(8,128)}, u32[]{:S(2)}) copy-start(f32[1024,256]{1,0:T(8,128)} %convolution_bitcast_fusion) | copy-start | bytes 3145732
  229.9 20.3 %collective-permute-start.22 = (bf16[1,2,128,512]{3,2,1,0:T(8,128)(2,1)S(1)}, bf16[1,2,128,512]{3,2,1,0:T(8,128)(2,1)}, u32[]{:S(2)}, u32[]{:S(2)}) collective-permute-start(bf16[1,2,128,512]{3,2,1,0:T(8,128)(2,1)S(1)} %bitcast.333), channel_id=1, source_target_pairs={{0,16},{8,24},{16,0},{24,8},{1,17},{9,25},{17,1},{25,9},{2,18},{10... | collective-permute-start | bytes 786440 | tf_op jit(solution)/shard_map/ppermute | solution.py:311
  230.0 21.4 %collective-permute-start.23 = (bf16[1,2,128,512]{3,2,1,0:T(8,128)(2,1)}, bf16[1,2,128,512]{3,2,1,0:T(8,128)(2,1)}, u32[]{:S(2)}, u32[]{:S(2)}) collective-permute-start(bf16[1,2,128,512]{3,2,1,0:T(8,128)(2,1)} %bitcast.98), channel_id=1, source_target_pairs={{0,16},{8,24},{16,0},{24,8},{1,17},{9,25},{17,1},{25,9},{2,18},{10... | collective-permute-start | bytes 786440 | tf_op jit(solution)/shard_map/ppermute | solution.py:311
  232.0 21.6 %collective-permute-start.21 = (bf16[2,290,256]{2,1,0:T(8,128)(2,1)S(1)}, bf16[2,290,256]{2,1,0:T(8,128)(2,1)S(1)}, u32[]{:S(2)}, u32[]{:S(2)}) collective-permute-start(bf16[2,290,256]{2,1,0:T(8,128)(2,1)S(1)} %fusion.42), channel_id=1, source_target_pairs={{0,2},{2,0},{4,6},{6,4},{1,3},{3,1},{5,7},{7,5},{8,10},{10,8},{12,... | collective-permute-start | bytes 890888 | tf_op jit(solution)/shard_map/ppermute | solution.py:290
  233.8 30.7 %collective-permute-start.24 = (bf16[1,8,64,1024]{3,2,1,0:T(8,128)(2,1)S(1)}, bf16[1,8,64,1024]{3,2,1,0:T(8,128)(2,1)}, u32[]{:S(2)}, u32[]{:S(2)}) collective-permute-start(bf16[1,8,64,1024]{3,2,1,0:T(8,128)(2,1)S(1)} %dynamic-slice_convert_fusion), channel_id=1, source_target_pairs={{0,16},{8,24},{16,0},{24,8},{1,17},{9,25},{17,1},{25,9},{2,18},{10... | collective-permute-start | bytes 3145736 | tf_op jit(solution)/shard_map/ppermute | solution.py:290
  251.3 48.6 %copy-start.10 = (bf16[2,2,128,512]{3,2,1,0:T(8,128)(2,1)}, bf16[2,2,128,512]{3,2,1,0:T(8,128)(2,1)S(1)}, u32[]{:S(2)}) copy-start(bf16[2,2,128,512]{3,2,1,0:T(8,128)(2,1)S(1)} %maximum_select_fusion.10) | copy-start | bytes 1572868
  284.6 10.1 %collective-permute-start.26 = (bf16[2,8,64,512]{3,2,1,0:T(8,128)(2,1)}, bf16[2,8,64,512]{3,2,1,0:T(8,128)(2,1)}, u32[]{:S(2)}, u32[]{:S(2)}) collective-permute-start(bf16[2,8,64,512]{3,2,1,0:T(8,128)(2,1)} %dynamic-slice_bitcast_fusion.1), channel_id=1, source_target_pairs={{0,8},{8,0},{16,24},{24,16},{1,9},{9,1},{17,25},{25,17},{2,10},{10... | collective-permute-start | bytes 3145736 | tf_op jit(solution)/shard_map/ppermute | solution.py:290
  285.7 10.5 %collective-permute-start.25 = (bf16[2,8,64,512]{3,2,1,0:T(8,128)(2,1)}, bf16[2,8,64,512]{3,2,1,0:T(8,128)(2,1)}, u32[]{:S(2)}, u32[]{:S(2)}) collective-permute-start(bf16[2,8,64,512]{3,2,1,0:T(8,128)(2,1)} %dynamic-slice_bitcast_fusion.2), channel_id=1, source_target_pairs={{0,8},{8,0},{16,24},{24,16},{1,9},{9,1},{17,25},{25,17},{2,10},{10... | collective-permute-start | bytes 3145736 | tf_op jit(solution)/shard_map/ppermute | solution.py:290
  287.6 4.3 %collective-permute-start.31 = (f32[9,1024]{1,0:T(8,128)S(1)}, f32[9,1024]{1,0:T(8,128)S(1)}, u32[]{:S(2)}, u32[]{:S(2)}) collective-permute-start(f32[9,1024]{1,0:T(8,128)S(1)} %fusion.46), channel_id=1, source_target_pairs={{0,2},{2,0},{4,6},{6,4},{1,3},{3,1},{5,7},{7,5},{8,10},{10,8},{12,... | collective-permute-start | bytes 110600 | tf_op jit(solution)/shard_map/ppermute | solution.py:322
  292.0 7.2 %collective-permute-start.32 = (f32[9,1024]{1,0:T(8,128)S(1)}, f32[9,1024]{1,0:T(8,128)S(1)}, u32[]{:S(2)}, u32[]{:S(2)}) collective-permute-start(f32[9,1024]{1,0:T(8,128)S(1)} %add.374), channel_id=1, source_target_pairs={{0,4},{2,6},{4,0},{6,2},{1,5},{3,7},{5,1},{7,3},{8,12},{10,14},{12... | collective-permute-start | bytes 110600 | tf_op jit(solution)/shard_map/ppermute | solution.py:322
  296.2 12.1 %copy-start.3 = (f32[2,8,64,512]{3,2,1,0:T(8,128)}, f32[2,8,64,512]{3,2,1,0:T(8,128)S(1)}, u32[]{:S(2)}) copy-start(f32[2,8,64,512]{3,2,1,0:T(8,128)S(1)} %convert_add_fusion.1) | copy-start | bytes 6291460
  298.6 17.6 %copy-start.1 = (f32[2,8,64,512]{3,2,1,0:T(8,128)}, f32[2,8,64,512]{3,2,1,0:T(8,128)S(1)}, u32[]{:S(2)}) copy-start(f32[2,8,64,512]{3,2,1,0:T(8,128)S(1)} %convert_add_fusion.2) | copy-start | bytes 6291460
  298.6 8.7 %collective-permute-start.33 = (bf16[1,290,256]{2,1,0:T(8,128)(2,1)S(1)}, bf16[1,290,256]{2,1,0:T(8,128)(2,1)S(1)}, u32[]{:S(2)}, u32[]{:S(2)}) collective-permute-start(bf16[1,290,256]{2,1,0:T(8,128)(2,1)S(1)} %dynamic-slice_convert_fusion.8), channel_id=1, source_target_pairs={{0,4},{2,6},{4,0},{6,2},{1,5},{3,7},{5,1},{7,3},{8,12},{10,14},{12... | collective-permute-start | bytes 445448 | tf_op jit(solution)/shard_map/ppermute | solution.py:290
  299.9 16.3 %collective-permute-start.27 = (bf16[2,2,128,512]{3,2,1,0:T(8,128)(2,1)S(1)}, bf16[2,2,128,512]{3,2,1,0:T(8,128)(2,1)S(1)}, u32[]{:S(2)}, u32[]{:S(2)}) collective-permute-start(bf16[2,2,128,512]{3,2,1,0:T(8,128)(2,1)S(1)} %maximum_select_fusion.10), channel_id=1, source_target_pairs={{0,8},{8,0},{16,24},{24,16},{1,9},{9,1},{17,25},{25,17},{2,10},{10... | collective-permute-start | bytes 1572872 | tf_op jit(solution)/shard_map/ppermute | solution.py:311
  299.9 16.3 %copy-start.11 = (bf16[2,2,128,512]{3,2,1,0:T(8,128)(2,1)S(1)}, bf16[2,2,128,512]{3,2,1,0:T(8,128)(2,1)}, u32[]{:S(2)}) copy-start(bf16[2,2,128,512]{3,2,1,0:T(8,128)(2,1)} %copy-done.10) | copy-start | bytes 1572868
  307.4 8.0 %collective-permute-start.34 = (bf16[1,290,256]{2,1,0:T(8,128)(2,1)S(1)}, bf16[1,290,256]{2,1,0:T(8,128)(2,1)S(1)}, u32[]{:S(2)}, u32[]{:S(2)}) collective-permute-start(bf16[1,290,256]{2,1,0:T(8,128)(2,1)S(1)} %add_convert_fusion.2), channel_id=1, source_target_pairs={{0,4},{2,6},{4,0},{6,2},{1,5},{3,7},{5,1},{7,3},{8,12},{10,14},{12... | collective-permute-start | bytes 445448 | tf_op jit(solution)/shard_map/ppermute | solution.py:311
  308.3 13.1 %collective-permute-start.28 = (bf16[2,2,128,512]{3,2,1,0:T(8,128)(2,1)}, bf16[2,2,128,512]{3,2,1,0:T(8,128)(2,1)}, u32[]{:S(2)}, u32[]{:S(2)}) collective-permute-start(bf16[2,2,128,512]{3,2,1,0:T(8,128)(2,1)} %maximum_select_fusion.11), channel_id=1, source_target_pairs={{0,8},{8,0},{16,24},{24,16},{1,9},{9,1},{17,25},{25,17},{2,10},{10... | collective-permute-start | bytes 1572872 | tf_op jit(solution)/shard_map/ppermute | solution.py:311
  309.2 22.7 %collective-permute-start.30 = (bf16[1,8,64,512]{3,2,1,0:T(8,128)(2,1)}, bf16[1,8,64,512]{3,2,1,0:T(8,128)(2,1)}, u32[]{:S(2)}, u32[]{:S(2)}) collective-permute-start(bf16[1,8,64,512]{3,2,1,0:T(8,128)(2,1)} %dynamic-slice_convert_fusion.3), channel_id=1, source_target_pairs={{0,16},{8,24},{16,0},{24,8},{1,17},{9,25},{17,1},{25,9},{2,18},{10... | collective-permute-start | bytes 1572872 | tf_op jit(solution)/shard_map/ppermute | solution.py:290
  309.4 25.7 %collective-permute-start.29 = (bf16[1,8,64,512]{3,2,1,0:T(8,128)(2,1)}, bf16[1,8,64,512]{3,2,1,0:T(8,128)(2,1)}, u32[]{:S(2)}, u32[]{:S(2)}) collective-permute-start(bf16[1,8,64,512]{3,2,1,0:T(8,128)(2,1)} %dynamic-slice_convert_fusion.4), channel_id=1, source_target_pairs={{0,16},{8,24},{16,0},{24,8},{1,17},{9,25},{17,1},{25,9},{2,18},{10... | collective-permute-start | bytes 1572872 | tf_op jit(solution)/shard_map/ppermute | solution.py:290
  316.2 26.4 %collective-permute-start.35 = (bf16[2,290,256]{2,1,0:T(8,128)(2,1)}, bf16[2,290,256]{2,1,0:T(8,128)(2,1)}, u32[]{:S(2)}, u32[]{:S(2)}) collective-permute-start(bf16[2,290,256]{2,1,0:T(8,128)(2,1)} %maximum_select_fusion.13), channel_id=1, source_target_pairs={{0,2},{2,0},{4,6},{6,4},{1,3},{3,1},{5,7},{7,5},{8,10},{10,8},{12,... | collective-permute-start | bytes 890888 | tf_op jit(solution)/shard_map/ppermute | solution.py:311
  (19 other events, 73.0 us)
